TPU v7x, 128 devices: a whole 4x4x4 slice. The times are simulated.
128 devices in a mesh: uly: 4 (over x_lo, core), blk: 32 (over x_hi, z, y).
Axes of the slice: x: 4 (x_hi: 2, x_lo: 2; x = x_hi * 2 + x_lo), y: 4, z: 4, core: 2. Of those that a mesh axis runs over, the one named last changes fastest.
Arguments:
- queries: bfloat16 [12288, 2560], P(('blk', 'uly')), may hold values from -5 to 5
- key_rows: bfloat16 [12288, 2560], P(('blk', 'uly')), may hold values from -5 to 5
- value_rows: bfloat16 [12288, 2560], P(('blk', 'uly')), may hold values from -6 to 6
- block_list: int32 [20, 96, 16], replicated, may hold values from 0 to 95, as said below
- block_count: int32 [20, 96], replicated, may hold values from 1 to 16, as said below
- w_out: bfloat16 [2560, 5120], P('uly'), may hold values from -0.125 to 0.125
Outputs:
- projected: bfloat16 [12288, 5120], P(('blk', 'uly'))
Inputs may be any that keep to these rules, and one draw needn't show every extreme that they name: `block_list`: each row of 16 entries holds distinct key block indices; its first entry is the row's own query block. `block_count`: some head and query block uses all 16 entries.
All inputs are finite; a program needn't handle non-finite values.
Results may differ from a plain program's by a relative error of at most 0.015.
Values may be sent and summed in bfloat16 or wider, within the bound.
No kernel may reach another device: no remote copies, remote signals or barrier semaphores. Data moves between devices by JAX's collectives and lax.ppermute only.
A program may use at most 384 MiB of HBM per device.

v0:
```python
import jax
import jax.numpy as jnp
from jax import lax
from jax.sharding import PartitionSpec as P

HEAD = 128
BLOCK = 128


masked_floor = -1e30


def head_update(running, query_heads, key_heads, value_heads, allowed):
    run_max, run_sum, run_acc = running
    scaling = HEAD ** (-0.5)
    scores = (
        jnp.einsum("qhd,khd->hqk", query_heads, key_heads, preferred_element_type=jnp.float32)
        * scaling
    )
    masked = jnp.where(allowed, scores, masked_floor)
    new_max = jnp.maximum(run_max, jnp.max(masked, axis=2))
    weights = jnp.where(allowed, jnp.exp(masked - new_max[:, :, None]), 0.0)
    new_sum = jnp.sum(weights, axis=2)
    product = jnp.einsum(
        "hqk,khd->hqd",
        weights.astype(jnp.bfloat16),
        value_heads,
        preferred_element_type=jnp.float32,
    )
    return (new_max, new_sum, product)


def per_device(queries, key_rows, value_rows, block_list, block_count, w_out):
    groups = lax.axis_size("uly")
    head_total = block_count.shape[0]
    heads_dev = head_total // groups
    head_order = jnp.arange(head_total, dtype=jnp.int32)
    q_local, k_local, v_local = (
        lax.all_to_all(queries, "uly", split_axis=1, concat_axis=0, tiled=True),
        lax.all_to_all(key_rows, "uly", split_axis=1, concat_axis=0, tiled=True),
        lax.all_to_all(value_rows, "uly", split_axis=1, concat_axis=0, tiled=True),
    )
    seg_rows = q_local.shape[0]
    query_blocks = seg_rows // BLOCK
    block_total = block_list.shape[1]
    my_heads = lax.dynamic_slice_in_dim(head_order, lax.axis_index("uly") * heads_dev, heads_dev)
    first_block = lax.axis_index("blk") * query_blocks
    my_lists = lax.dynamic_slice_in_dim(
        jnp.take(block_list, my_heads, axis=0), first_block, query_blocks, 1
    )
    my_counts = lax.dynamic_slice_in_dim(
        jnp.take(block_count, my_heads, axis=0), first_block, query_blocks, 1
    )
    slot_live = (
        jnp.arange(my_lists.shape[2], dtype=jnp.int32)[None, None, :] < my_counts[:, :, None]
    )
    block_ids = jnp.arange(block_total, dtype=jnp.int32)
    mask_small = jnp.any((my_lists[..., None] == block_ids) & slot_live[..., None], axis=2).astype(
        jnp.float32
    )
    query_heads = q_local.reshape(seg_rows, heads_dev, HEAD)
    initial = (
        jnp.full((heads_dev, seg_rows), masked_floor, jnp.float32),
        jnp.zeros((heads_dev, seg_rows), jnp.float32),
        jnp.zeros((heads_dev, seg_rows, HEAD), jnp.float32),
    )
    key_part = lax.all_gather(k_local, "blk", axis=0, tiled=True)
    value_part = lax.all_gather(v_local, "blk", axis=0, tiled=True)
    piece_rows = key_part.shape[0]
    key_heads = key_part.reshape(piece_rows, heads_dev, HEAD)
    value_heads = value_part.reshape(piece_rows, heads_dev, HEAD)
    key_block = jnp.arange(piece_rows, dtype=jnp.int32) // BLOCK
    onehot = (block_ids[:, None] == key_block[None, :]).astype(jnp.float32)
    tile_live = jnp.einsum("hqn,nk->hqk", mask_small, onehot) > 0.5
    allowed = jnp.repeat(tile_live, BLOCK, axis=1)
    run_max, run_sum, run_acc = head_update(initial, query_heads, key_heads, value_heads, allowed)
    normed = run_acc / run_sum[:, :, None]
    attended = normed.transpose(1, 0, 2).reshape(seg_rows, heads_dev * HEAD).astype(jnp.bfloat16)
    return lax.psum_scatter(
        jnp.dot(attended, w_out, preferred_element_type=jnp.float32).astype(jnp.bfloat16),
        "uly",
        scatter_dimension=0,
        tiled=True,
    )


def solution(mesh):
    placed = (
        P(("blk", "uly"), None),
        P(("blk", "uly"), None),
        P(("blk", "uly"), None),
        P(),
        P(),
        P("uly", None),
    )
    return jax.shard_map(
        per_device, mesh=mesh, in_specs=placed, out_specs=P(("blk", "uly"), None), check_vma=False
    )
```

profile of v0, /device:TPU:1, one launch (start us, length us, event | category | flops | bytes accessed | tf_op | source)
XLA Modules:
  0.0 423.8 jit_solution(4883823823809964805)
XLA Ops:
  6.5 0.0 copy-start
  6.5 0.0 all-gather.3.cloned.1.call-start
  6.5 1.1 copy.74
  7.7 12.1 %all_to_all.54 = bf16[96,4,640]{2,0,1:T(8,128)(2,1)} all-to-all(bf16[96,4,640]{2,0,1:T(8,128)(2,1)S(1)} %bitcast.54), channel_id=1, replica_groups=mesh['uly'=4,'blk'=32] {'uly'}, dimensions={1} | all-to-all | bytes 983040 | tf_op jit(solution)/shard_map/all_to_all | solution.py:40
  19.7 0.0 all-gather.3.cloned.1.call-update
  19.7 0.0 all-gather.5.cloned.1.call-start
  19.8 1.1 copy.73
  20.9 11.6 %all_to_all.55 = bf16[96,4,640]{2,0,1:T(8,128)(2,1)} all-to-all(bf16[96,4,640]{2,0,1:T(8,128)(2,1)S(1)} %bitcast.55), channel_id=1, replica_groups=mesh['uly'=4,'blk'=32] {'uly'}, dimensions={1} | all-to-all | bytes 983040 | tf_op jit(solution)/shard_map/all_to_all | solution.py:41
  32.5 0.0 all-gather.5.cloned.1.call-update
  32.5 1.9 copy.75
  34.4 4.4 %all-to-all-start = ((bf16[96,4,640]{2,0,1:T(8,128)(2,1)}), bf16[96,4,640]{2,0,1:T(8,128)(2,1)S(1)}, u32[]{:S(2)}, u32[]{:S(2)}) async-start(bf16[96,4,640]{2,0,1:T(8,128)(2,1)} %bitcast.47), calls=%async_computation | async-start | bytes 983040 | tf_op jit(solution)/shard_map/all_to_all | solution.py:39
  38.8 0.0 reduce-scatter.2.cloned.1.call-start
  38.8 0.1 compare_and_fusion
  38.9 0.0 copy-done
  38.9 0.6 gather_fusion
  39.4 1.3 gather_fusion.1
  40.7 0.1 broadcast_select_fusion
  40.8 0.1 constant_dynamic-slice_fusion
  40.8 0.1 dynamic-slice_select_fusion
  40.9 0.1 iota_compare_fusion.2
  41.0 0.1 copy.45
  41.1 0.2 fusion.11
  41.3 0.9 convolution_compare_fusion
  42.2 0.3 copy.47
  42.5 3.9 all-to-all-done
  46.5 0.6 reshape.74
  47.0 125.4 %all-gather.3.cloned.1.call-done = bf16[12288,640]{1,0:T(8,128)(2,1)} async-done(((bf16[384,640]{1,0:T(8,128)(2,1)}), bf16[12288,640]{1,0:T(8,128)(2,1)}) %all-gather.3.cloned.1.call-update) | async-done | bytes 15728656 | tf_op jit(solution)/shard_map/all_gather | solution.py:67
  172.5 20.7 %copy.51 = bf16[12288,640]{0,1:T(8,128)(2,1)} copy(bf16[12288,640]{1,0:T(8,128)(2,1)} %all-gather.3.cloned.1.call-done) | data formatting | bytes 31457280 | tf_op jit(solution)/shard_map/all_gather | solution.py:67
  193.2 39.2 %fusion = (f32[5,384]{1,0:T(8,128)S(1)}, f32[5,384,12288]{2,1,0:T(8,128)}) fusion(pred[5,3,12288]{2,1,0:T(4,128)(4,1)S(1)} %copy.47, bf16[12288,5,128]{0,2,1:T(8,128)(2,1)} %bitcast.48, bf16[384,5,128]{2,1,0:T(8,128)(2,1)S(1)} %reshape.74), kind=kOutput, calls=%fused_computation.4 | convolution fusion | flops 6110574592 | bytes 110784000 | tf_op jit(solution)/shard_map/qhd,khd->hqk/dot_general | solution.py:17
  232.4 47.4 %fusion.1 = (f32[5,384]{1,0:T(8,128)S(1)}, bf16[5,384,12288]{2,1,0:T(8,128)(2,1)}) fusion(f32[5,384,12288]{2,1,0:T(8,128)} %get-tuple-element.10, f32[5,384]{1,0:T(8,128)S(1)} %broadcast_maximum_fusion, pred[5,3,12288]{2,1,0:T(4,128)(4,1)S(1)} %copy.47), kind=kLoop, calls=%fused_computation.5 | loop fusion | flops 141555840 | bytes 141757440 | tf_op jit(solution)/shard_map/reduce_sum | solution.py:23
  279.8 44.0 %all-gather.5.cloned.1.call-done = bf16[12288,640]{1,0:T(8,128)(2,1)} async-done(((bf16[384,640]{1,0:T(8,128)(2,1)}), bf16[12288,640]{1,0:T(8,128)(2,1)}) %all-gather.5.cloned.1.call-update) | async-done | bytes 15728656 | tf_op jit(solution)/shard_map/all_gather | solution.py:68
  323.8 20.7 %copy.55 = bf16[12288,640]{0,1:T(8,128)(2,1)} copy(bf16[12288,640]{1,0:T(8,128)(2,1)} %all-gather.5.cloned.1.call-done) | data formatting | bytes 31457280 | tf_op jit(solution)/shard_map/all_gather | solution.py:68
  344.5 0.0 copy-start.1
  344.5 22.9 %fusion.7 = bf16[384,5,128]{0,2,1:T(8,128)(2,1)S(1)} fusion(bf16[5,384,12288]{2,1,0:T(8,128)(2,1)} %get-tuple-element.8, bf16[12288,5,128]{0,2,1:T(8,128)(2,1)} %bitcast.49, f32[384,5]{0,1:T(8,128)S(1)} %bitcast.56), kind=kOutput, calls=%fused_computation.14 | convolution fusion | flops 6040289280 | bytes 63413760 | tf_op jit(solution)/shard_map/hqk,khd->hqd/dot_general | solution.py:24
  367.4 8.0 %convolution_convert_fusion = bf16[384,5120]{1,0:T(8,128)(2,1)} fusion(bf16[384,640]{0,1:T(8,128)(2,1)S(1)} %bitcast.50, bf16[640,5120]{1,0:T(8,128)(2,1)} %param.11), kind=kOutput, calls=%fused_computation.8 | convolution fusion | flops 2518548480 | bytes 10977280 | tf_op jit(solution)/shard_map/dot_general | solution.py:80
  375.4 0.0 reduce-scatter.2.cloned.1.call-update
  375.4 41.9 %reduce-scatter.2.cloned.1.call-done = bf16[96,5120]{1,0:T(8,128)(2,1)} async-done(((bf16[384,5120]{1,0:T(8,128)(2,1)}), bf16[96,5120]{1,0:T(8,128)(2,1)}) %reduce-scatter.2.cloned.1.call-update) | async-done | bytes 983056 | tf_op jit(solution)/shard_map/reduce_scatter | solution.py:79
  417.3 0.0 copy-done.1
  (4 shorter events, 0.0 us)
Async XLA Ops:
  6.5 32.3 %copy-start = (s32[20,96,16]{1,2,0:T(8,128)S(1)}, s32[20,96,16]{1,2,0:T(8,128)}, u32[]{:S(2)}) copy-start(s32[20,96,16]{1,2,0:T(8,128)} %param.9) | copy-start | bytes 368644
  6.5 165.9 %all-gather.3.cloned.1.call-start = ((), (), s32[]{:S(2)}) async-start(), calls=%async_computation.4 | async-start | bytes 16220160 | tf_op jit(solution)/shard_map/all_gather | solution.py:67
  19.7 304.0 %all-gather.5.cloned.1.call-start = ((), (), s32[]{:S(2)}) async-start(), calls=%async_computation.5 | async-start | bytes 16220160 | tf_op jit(solution)/shard_map/all_gather | solution.py:68
  34.4 12.1 %all-to-all-start = ((bf16[96,4,640]{2,0,1:T(8,128)(2,1)}), bf16[96,4,640]{2,0,1:T(8,128)(2,1)S(1)}, u32[]{:S(2)}, u32[]{:S(2)}) async-start(bf16[96,4,640]{2,0,1:T(8,128)(2,1)} %bitcast.47), calls=%async_computation | async-start | bytes 983040 | tf_op jit(solution)/shard_map/all_to_all | solution.py:39
  38.8 378.5 %reduce-scatter.2.cloned.1.call-start = ((), (), s32[]{:S(2)}) async-start(), calls=%async_computation.6 | async-start | bytes 4915200 | tf_op jit(solution)/shard_map/reduce_scatter | solution.py:79
  344.5 72.8 %copy-start.1 = (s32[20,96,16]{1,2,0:T(8,128)S(1)}, s32[20,96,16]{1,2,0:T(8,128)}, u32[]{:S(2)}) copy-start(s32[20,96,16]{1,2,0:T(8,128)} %param.9) | copy-start | bytes 368644
Sparse Core Ops, SparseCore 0:
  19.9 152.5 all-gather.2
  175.5 148.2 all-gather.4
  375.5 41.7 reduce-scatter.1
where the time goes:
time: 425 us; the launch traced here: 424 us
  waiting for transfers between devices  215 us (51%)
  matrix products  71 us (17%)
  local copies, waits for them, and re-layouts  48.4 us (11%)
  other arithmetic  47.9 us (11%)
  blocking collectives  23.6 us (6%)
  between operations  13.2 us (3%)
  starting transfers between devices  4.44 us (1%)
    all_gather x1, waiting for transfers between devices, per_device(): key_part = lax.all_gather(k_local, 'blk', axis=0, tiled=True)  125 us
    reduce_sum x1, other arithmetic, head_update(): new_sum = jnp.sum(weights, axis=2)  47.4 us
    all_gather x1, waiting for transfers between devices, per_device(): value_part = lax.all_gather(v_local, 'blk', axis=0, tiled=True)  44 us
    reduce_scatter x1, waiting for transfers between devices, per_device(): lax.psum_scatter(jnp.dot(attended, w_out, preferred_element_type=jnp.floa...  41.9 us
    dot_general x1, matrix products, head_update(): jnp.einsum('qhd,khd->hqk', query_heads, key_heads, preferred_element_type...  39.2 us
    dot_general x1, matrix products, head_update(): jnp.einsum('hqk,khd->hqd', weights.astype(jnp.bfloat16), value_heads, pre...  22.9 us
    all_gather x1, local copies, waits for them, and re-layouts, per_device(): key_part = lax.all_gather(k_local, 'blk', axis=0, tiled=True)  20.7 us
    all_gather x1, local copies, waits for them, and re-layouts, per_device(): value_part = lax.all_gather(v_local, 'blk', axis=0, tiled=True)  20.7 us
  transfers between devices with their start and end apart: 4, of which 4 were waited for; matrix products, arithmetic and copies ran while one was open for 27% of the time, Pallas kernels for 0%

commit v1 on v0

v1 whole, which is shorter than its diff:
```python
import functools

import jax
import jax.numpy as jnp
from jax import lax
from jax.experimental import pallas as pl
from jax.experimental.pallas import tpu as pltpu
from jax.sharding import Mesh, PartitionSpec as P

HEAD = 128
BLOCK = 128
ROWS = 96
CHUNKS = 4
SUPER = ROWS * CHUNKS
EXT = 32
HALF = 16
LOG2E = 1.4426950408889634
SCALE = HEAD ** -0.5 * LOG2E
FLOOR = -1e30
NAMES = ("xh", "zh", "zl", "y", "xl", "c")
GRID = ("xl", "c", "xh", "zh", "zl", "y")
SIZES = (2, 2, 2, 2, 2, 4)
SPREAD = ("xh", "zh", "xl", "c")
STATS = 16


def ring_up(x):
    return lax.ppermute(x, "y", [(i, (i + 1) % 4) for i in range(4)])


def ring_down(x):
    return lax.ppermute(x, "y", [(i, (i - 1) % 4) for i in range(4)])


def swap(x):
    return lax.ppermute(x, "zl", [(0, 1), (1, 0)])


def attention_kernel(
    where_ref, list_ref, count_ref, shared_list_ref, shared_count_ref, q_ref,
    a00, a01, am0, ap0, a11, am1, a20, last_k, last_v, last_e,
    out_ref, k_main, v_main, k_ext, v_ext, sem,
):
    y = where_ref[0]
    zl = where_ref[1]
    group = where_ref[2]
    copies = []

    def put(source, lo, rows, target, dy, dz):
        yy = lax.rem(y + (dy + 4), 4)
        zz = lax.rem(zl + dz, 2)
        copy = pltpu.make_async_copy(
            source.at[:, :, pl.ds(lo, rows)], target.at[:, zz, yy], sem.at[len(copies)]
        )
        copy.start()
        copies.append(copy)

    for source, dy, dz in (
        (a00, 0, 0), (a01, 0, 1), (am0, -1, 0), (ap0, 1, 0), (a11, 1, 1), (am1, -1, 1), (a20, 2, 0),
    ):
        put(source, 0, ROWS, k_main, dy, dz)
        put(source, ROWS, ROWS, v_main, dy, dz)
        put(source, 2 * ROWS, EXT, k_ext, dy, dz)
        put(source, 2 * ROWS + EXT, EXT, v_ext, dy, dz)
    put(last_k, 0, ROWS, k_main, 2, 1)
    put(last_v, 0, ROWS, v_main, 2, 1)
    put(last_e, 0, EXT, k_ext, 2, 1)
    put(last_e, EXT, EXT, v_ext, 2, 1)
    for copy in copies:
        copy.wait()

    k_flat = k_main.reshape(32 * SUPER, HEAD)
    v_flat = v_main.reshape(32 * SUPER, HEAD)
    ke_flat = k_ext.reshape(32 * CHUNKS * EXT, HEAD)
    ve_flat = v_ext.reshape(32 * CHUNKS * EXT, HEAD)
    col = lax.broadcasted_iota(jnp.int32, (BLOCK, 512), 1)
    eye = lax.broadcasted_iota(jnp.int32, (BLOCK, BLOCK), 0) == lax.broadcasted_iota(
        jnp.int32, (BLOCK, BLOCK), 1
    )

    def dot_t(a, b):
        return lax.dot_general(a, b, (((1,), (1,)), ((), ())), preferred_element_type=jnp.float32)

    def place(unit):
        sb = lax.div(unit, 3)
        return sb, pl.multiple_of((unit - 3 * sb) * BLOCK, BLOCK)

    def main_unit(unit, carry):
        count = count_ref[unit]
        q = q_ref[unit]

        def step(t, state):
            top, total, acc = state
            rows = [pl.multiple_of(list_ref[unit, 4 * t + i] * BLOCK, BLOCK) for i in range(4)]
            keys = jnp.concatenate([k_flat[pl.ds(r, BLOCK), :] for r in rows], axis=0)
            values = jnp.concatenate([v_flat[pl.ds(r, BLOCK), :] for r in rows], axis=0)
            s = dot_t(q, keys)
            s = jnp.where(col < (count - 4 * t) * BLOCK, s, FLOOR)
            new_top = jnp.maximum(top, jnp.max(s, axis=1, keepdims=True))
            p = jnp.exp2((s - new_top) * SCALE)
            alpha = jnp.exp2((top - new_top) * SCALE)
            total = total * alpha + jnp.sum(p, axis=1, keepdims=True)
            acc = acc * alpha + jnp.dot(
                p.astype(jnp.bfloat16), values, preferred_element_type=jnp.float32
            )
            return new_top, total, acc

        top, total, acc = lax.fori_loop(
            0,
            lax.div(count + 3, 4),
            step,
            (
                jnp.full((BLOCK, 1), FLOOR, jnp.float32),
                jnp.zeros((BLOCK, 1), jnp.float32),
                jnp.zeros((BLOCK, HEAD), jnp.float32),
            ),
        )
        sb, row = place(unit)
        out_ref[sb, pl.ds(row, BLOCK), :] = (acc / total).astype(jnp.bfloat16)
        return carry

    def shared_unit(unit, carry):
        count = shared_count_ref[unit]
        q = q_ref[12 + unit]
        rows = []
        for i in range(16):
            block = shared_list_ref[unit, i]
            sb = lax.div(block, 3)
            for e in range(2):
                h = (block - 3 * sb) * 8 + group + 4 * e
                chunk = lax.div(h, 6)
                slot = lax.div(h - 6 * chunk, 4)
                rows.append(pl.multiple_of((sb * CHUNKS + chunk) * EXT + slot * HALF, HALF))
        keys = jnp.concatenate([ke_flat[pl.ds(r, HALF), :] for r in rows], axis=0)
        values = jnp.concatenate([ve_flat[pl.ds(r, HALF), :] for r in rows], axis=0)
        s = dot_t(q, keys)
        s = jnp.where(col < count * (2 * HALF), s, FLOOR)
        top = jnp.max(s, axis=1, keepdims=True)
        p = jnp.exp2((s - top) * SCALE)
        total = jnp.sum(p, axis=1, keepdims=True)
        acc = jnp.dot(p.astype(jnp.bfloat16), values, preferred_element_type=jnp.float32)
        sb, row = place(unit)
        out_ref[sb, pl.ds(SUPER + row, BLOCK), :] = (acc / total).astype(jnp.bfloat16)
        level = top * SCALE + jnp.log2(total)
        level = jnp.sum(jnp.where(eye, level, 0.0), axis=0, keepdims=True)
        high = level.astype(jnp.bfloat16).astype(jnp.float32)
        rest = level - high
        mid = rest.astype(jnp.bfloat16).astype(jnp.float32)
        low = rest - mid
        index = lax.broadcasted_iota(jnp.int32, (STATS, HEAD), 0)
        tile = jnp.where(index == 0, high, jnp.where(index == 1, mid, jnp.where(index == 2, low, 0.0)))
        at = pl.multiple_of(2 * SUPER + (unit - 3 * sb) * STATS, STATS)
        out_ref[sb, pl.ds(at, STATS), :] = tile.astype(jnp.bfloat16)
        return carry

    lax.fori_loop(0, 12, main_unit, 0)
    lax.fori_loop(0, 12, shared_unit, 0)


def attention(where, lists, counts, shared_lists, shared_counts, q, pieces):
    smem = pl.BlockSpec(memory_space=pltpu.SMEM)
    vmem = pl.BlockSpec(memory_space=pltpu.VMEM)
    hbm = pl.BlockSpec(memory_space=pl.ANY)
    return pl.pallas_call(
        attention_kernel,
        out_shape=jax.ShapeDtypeStruct((4, 2 * SUPER + 3 * STATS, HEAD), jnp.bfloat16),
        in_specs=[smem] * 5 + [vmem] + [hbm] * 10,
        out_specs=vmem,
        scratch_shapes=[
            pltpu.VMEM((4, 2, 4, CHUNKS, ROWS, HEAD), jnp.bfloat16),
            pltpu.VMEM((4, 2, 4, CHUNKS, ROWS, HEAD), jnp.bfloat16),
            pltpu.VMEM((4, 2, 4, CHUNKS, EXT, HEAD), jnp.bfloat16),
            pltpu.VMEM((4, 2, 4, CHUNKS, EXT, HEAD), jnp.bfloat16),
            pltpu.SemaphoreType.DMA((32,)),
        ],
        compiler_params=pltpu.CompilerParams(vmem_limit_bytes=40 * 1024 * 1024),
        cost_estimate=pl.CostEstimate(
            flops=4 * 240 * BLOCK * BLOCK * HEAD, bytes_accessed=10_000_000, transcendentals=4_000_000
        ),
    )(where, lists, counts, shared_lists, shared_counts, q, *pieces)


def to_groups(main):
    rows = main.shape[0]
    return main.transpose(2, 1, 0, 3).reshape(16, rows, HEAD)


def shared_keys(rows, core):
    runs = jnp.pad(rows, ((0, 32), (0, 0), (0, 0))).reshape(2, 4, HALF, 4, HEAD)
    runs = jnp.where(core == 0, runs, jnp.roll(runs, 2, axis=1))
    return runs.transpose(1, 3, 0, 2, 4).reshape(16, EXT, HEAD)


def per_device(queries, key_rows, value_rows, block_list, block_count, w_out):
    xh, zh, zl, y, xl, c = [lax.axis_index(name) for name in NAMES]
    u = 2 * xl + c
    group = 2 * xh + zh
    k5 = key_rows.reshape(ROWS, 4, 5, HEAD)
    v5 = value_rows.reshape(ROWS, 4, 5, HEAD)
    q5 = queries.reshape(ROWS, 4, 5, HEAD)
    kv = jnp.concatenate(
        [
            to_groups(k5[:, :, :4]),
            to_groups(v5[:, :, :4]),
            shared_keys(k5[:, :, 4], c),
            shared_keys(v5[:, :, 4], c),
        ],
        axis=1,
    )
    kv = lax.all_to_all(kv, SPREAD, 0, 0, tiled=True).reshape(4, CHUNKS, 2 * ROWS + 2 * EXT, HEAD)

    q_shared = jnp.broadcast_to(q5[:, :, 4:], (ROWS, 4, 4, HEAD))
    q = jnp.stack([to_groups(q5[:, :, :4]), to_groups(q_shared)], axis=1)
    q = lax.all_to_all(q, SPREAD, 0, 0, tiled=True)
    q = q.reshape(4, CHUNKS, 2, ROWS, HEAD).transpose(2, 0, 1, 3, 4).reshape(24, BLOCK, HEAD)

    a01, am0, ap0 = swap(kv), ring_up(kv), ring_down(kv)
    a11, am1, a20 = swap(ap0), ring_up(a01), ring_down(ap0)
    last_k = swap(a20[:, :, :ROWS])
    last_v = ring_up(am1[:, :, ROWS : 2 * ROWS])
    last_e = ring_down(a11[:, :, 2 * ROWS :])
    pieces = (kv, a01, am0, ap0, a11, am1, a20, last_k, last_v, last_e)

    def pick(table, head):
        mine = lax.dynamic_index_in_dim(table, head, 0, keepdims=False)
        mine = mine.reshape((4, 8, 3) + mine.shape[1:])
        return lax.dynamic_index_in_dim(mine, 4 * zl + y, 1, keepdims=False)

    lists = pick(block_list, 5 * u + group).reshape(12, 16)
    counts = pick(block_count, 5 * u + group).reshape(12)
    shared_lists = pick(block_list, 5 * u + 4).reshape(12, 16)
    shared_counts = pick(block_count, 5 * u + 4).reshape(12)
    where = jnp.stack([y, zl, group]).astype(jnp.int32)

    out = attention(where, lists, counts, shared_lists, shared_counts, q, pieces)
    out = lax.all_to_all(out, ("xh", "zh"), 0, 0, tiled=True)

    heads = out[:, :SUPER]
    shares = out[:, SUPER : 2 * SUPER].astype(jnp.float32)
    level = out[:, 2 * SUPER :].reshape(4, 3, STATS, BLOCK)[:, :, :3].astype(jnp.float32)
    level = jnp.sum(level, axis=2).reshape(4, SUPER, 1)
    weight = jnp.exp2(level - jnp.max(level, axis=0, keepdims=True))
    shared = jnp.sum(shares * weight, axis=0) / jnp.sum(weight, axis=0)
    attended = jnp.concatenate(
        [heads.transpose(1, 0, 2).reshape(SUPER, 4 * HEAD), shared.astype(jnp.bfloat16)], axis=1
    )
    return lax.psum_scatter(
        jnp.dot(attended, w_out, preferred_element_type=jnp.float32).astype(jnp.bfloat16),
        ("xl", "c"),
        scatter_dimension=0,
        tiled=True,
    )


def solution(mesh):
    fine = Mesh(mesh.devices.reshape(SIZES), GRID)
    rows = P(NAMES, None)
    return jax.shard_map(
        per_device,
        mesh=fine,
        in_specs=(rows, rows, rows, P(), P(), P(("xl", "c"), None)),
        out_specs=rows,
        check_vma=False,
    )
```

time: 425 us -> 224 us (0.53)
  waiting for transfers between devices: 215 us -> 79.6 us
  matrix products: 71 us -> 8.01 us
  other arithmetic: 47.9 us -> 1.38 us
  Pallas kernels: 0 us -> 22.6 us
  blocking collectives: 23.6 us -> 43.8 us
  starting transfers between devices: 4.44 us -> 17.4 us
  local copies, waits for them, and re-layouts: 48.4 us -> 35.7 us
    all_gather x2 -> x0, waiting for transfers between devices: 169 us -> none  [the longest x1 125 us: per_device(): key_part = lax.all_gather(k_local, 'blk', axis=0, tiled=True)]
    dot_general x3 -> x0, matrix products: 63 us -> none  [the longest x1 39.2 us: head_update(): jnp.einsum('qhd,khd->hqk', query_heads, key_heads, preferred_element_type...]
    reduce_sum x1 -> x3, other arithmetic: 47.4 us -> 0.32 us  [the longest x2 0.29 us: per_device(): shared = jnp.sum(shares * weight, axis=0) / jnp.sum(weight, axis=0)]
    all_gather x2 -> x0, local copies, waits for them, and re-layouts: 41.5 us -> none  [the longest x1 20.7 us: per_device(): key_part = lax.all_gather(k_local, 'blk', axis=0, tiled=True)]
    ppermute x0 -> x9, waiting for transfers between devices: none -> 35.3 us  [the longest x3 24.7 us: ring_down(): return lax.ppermute(x, 'y', [(i, (i - 1) % 4) for i in range(4)])]
    pallas_call x0 -> x1, Pallas kernels: none -> 22.6 us  [attention(): pl.pallas_call(attention_kernel, out_shape=jax.ShapeDtypeStruct((4, 2 * S...]
    all_to_all x2, blocking collectives: 23.6 us -> 43.8 us  [the longest x1 26.3 us: per_device(): lax.all_to_all(kv, SPREAD, 0, 0, tiled=True)]
    ppermute x0 -> x9, starting transfers between devices: none -> 11.1 us  [the longest x3 8.92 us: ring_down(): return lax.ppermute(x, 'y', [(i, (i - 1) % 4) for i in range(4)])]
  transfers between devices with their start and end apart: 4 -> 11, of which waited for: 4 -> 6; matrix products, arithmetic and copies ran while one was open for 27% -> 14% of each run, Pallas kernels for 0% -> 0%
where the time goes in v1:
time: 224 us; the launch traced here: 222 us
  waiting for transfers between devices  79.6 us (36%)
  blocking collectives  43.8 us (20%)
  local copies, waits for them, and re-layouts  35.7 us (16%)
  Pallas kernels  22.6 us (10%)
  starting transfers between devices  17.4 us (8%)
  between operations  13.6 us (6%)
  matrix products  8.01 us (4%)
    reduce_scatter x1, waiting for transfers between devices, per_device(): lax.psum_scatter(jnp.dot(attended, w_out, preferred_element_type=jnp.floa...  44.3 us
    all_to_all x1, blocking collectives, per_device(): lax.all_to_all(kv, SPREAD, 0, 0, tiled=True)  26.3 us
    ppermute x3, waiting for transfers between devices, ring_down(): return lax.ppermute(x, 'y', [(i, (i - 1) % 4) for i in range(4)])  24.7 us
    pallas_call x1, Pallas kernels, attention(): pl.pallas_call(attention_kernel, out_shape=jax.ShapeDtypeStruct((4, 2 * S...  22.6 us
    all_to_all x1, blocking collectives, per_device(): out = lax.all_to_all(out, ('xh', 'zh'), 0, 0, tiled=True)  17.5 us
    ppermute x3, waiting for transfers between devices, ring_up(): return lax.ppermute(x, 'y', [(i, (i + 1) % 4) for i in range(4)])  10.5 us
    ppermute x3, starting transfers between devices, ring_down(): return lax.ppermute(x, 'y', [(i, (i - 1) % 4) for i in range(4)])  8.92 us
    dot_general x1, matrix products, per_device(): jnp.dot(attended, w_out, preferred_element_type=jnp.float32)  8.01 us
  transfers between devices with their start and end apart: 11, of which 6 were waited for; matrix products, arithmetic and copies ran while one was open for 14% of the time, Pallas kernels for 0%

profile of v1, /device:TPU:1, one launch (start us, length us, event | category | flops | bytes accessed | tf_op | source)
XLA Modules:
  0.0 222.0 jit_solution(3413868286879055241)
XLA Ops:
  6.5 1.4 copy.53
  8.0 1.4 copy.55
  9.4 0.2 copy.54
  9.6 0.1 copy.57
  9.8 0.2 copy.56
  10.0 0.1 copy.61
  10.2 0.1 maximum_select_fusion
  10.3 0.1 pad_maximum_fusion
  10.4 26.3 %all_to_all.15 = bf16[16,256,128]{2,1,0:T(8,128)(2,1)S(1)} all-to-all(bf16[16,256,128]{2,1,0:T(8,128)(2,1)S(1)} %pad_maximum_fusion), channel_id=1, replica_groups=mesh['xl'=2,'c'=2,'xh'=2,'zh'=2,'zl'=2,'y'=4] {'xh','zh','xl','c'}, dimensions={0} | all-to-all | bytes 2097152 | tf_op jit(solution)/shard_map/all_to_all | solution.py:210
  36.7 2.7 %collective-permute-start.2 = (bf16[4,4,256,128]{3,2,1,0:T(8,128)(2,1)S(1)}, bf16[4,4,256,128]{3,2,1,0:T(8,128)(2,1)}, u32[]{:S(2)}, u32[]{:S(2)}) collective-permute-start(bf16[4,4,256,128]{3,2,1,0:T(8,128)(2,1)S(1)} %bitcast.48), channel_id=1, source_target_pairs={{0,3},{1,0},{2,1},{3,2},{4,7},{5,4},{6,5},{7,6},{8,11},{9,8},{10,9... | collective-permute-start | bytes 3145736 | tf_op jit(solution)/shard_map/ppermute | solution.py:32
  39.4 0.7 collective-permute-start
  40.2 21.0 %collective-permute-done.2.ap0 = bf16[4,4,256,128]{3,2,1,0:T(8,128)(2,1)} collective-permute-done((bf16[4,4,256,128]{3,2,1,0:T(8,128)(2,1)S(1)}, bf16[4,4,256,128]{3,2,1,0:T(8,128)(2,1)}, u32[]{:S(2)}, u32[]{:S(2)}) %collective-permute-start.2) | collective-permute-done | bytes 1048608 | tf_op jit(solution)/shard_map/ppermute | solution.py:32
  61.2 3.5 %collective-permute-start.5 = (bf16[4,4,256,128]{3,2,1,0:T(8,128)(2,1)}, bf16[4,4,256,128]{3,2,1,0:T(8,128)(2,1)S(1)}, u32[]{:S(2)}, u32[]{:S(2)}) collective-permute-start(bf16[4,4,256,128]{3,2,1,0:T(8,128)(2,1)} %collective-permute-done.2.ap0), channel_id=1, source_target_pairs={{0,3},{1,0},{2,1},{3,2},{4,7},{5,4},{6,5},{7,6},{8,11},{9,8},{10,9... | collective-permute-start | bytes 3145736 | tf_op jit(solution)/shard_map/ppermute | solution.py:32
  64.7 0.7 collective-permute-start.3
  65.5 2.1 copy.48
  67.6 1.6 slice.71
  69.1 0.0 collective-permute-start.1
  69.1 1.9 slice_bitcast_fusion.2
  71.0 1.3 copy.49
  72.3 1.6 copy.50
  73.9 0.9 broadcast_in_dim.9
  74.9 0.1 pad_maximum_fusion.1
  75.0 1.0 copy.51
  75.9 6.2 %all-to-all-start = ((bf16[16,2,96,128]{3,2,1,0:T(8,128)(2,1)}), bf16[16,2,96,128]{3,2,1,0:T(8,128)(2,1)}, u32[]{:S(2)}, u32[]{:S(2)}) async-start(bf16[16,2,96,128]{3,2,1,0:T(8,128)(2,1)} %copy.51), calls=%async_computation | async-start | bytes 1572864 | tf_op jit(solution)/shard_map/all_to_all | solution.py:214
  82.1 0.0 reduce-scatter.2.cloned.1.call-start
  82.2 3.7 %collective-permute-done.5.a20 = bf16[4,4,256,128]{3,2,1,0:T(8,128)(2,1)S(1)} collective-permute-done((bf16[4,4,256,128]{3,2,1,0:T(8,128)(2,1)}, bf16[4,4,256,128]{3,2,1,0:T(8,128)(2,1)S(1)}, u32[]{:S(2)}, u32[]{:S(2)}) %collective-permute-start.5) | collective-permute-done | bytes 1048608 | tf_op jit(solution)/shard_map/ppermute | solution.py:32
  85.9 0.8 slice.80
  86.7 0.7 collective-permute-start.6
  87.4 1.6 collective-permute-done.4.am1
  89.0 0.8 slice.81
  89.8 1.7 slice.82
  91.5 2.7 %collective-permute-start.8 = (bf16[4,4,64,128]{3,2,1,0:T(8,128)(2,1)}, bf16[4,4,64,128]{3,2,1,0:T(8,128)(2,1)}, u32[]{:S(2)}, u32[]{:S(2)}) collective-permute-start(bf16[4,4,64,128]{3,2,1,0:T(8,128)(2,1)} %slice.82), channel_id=1, source_target_pairs={{0,3},{1,0},{2,1},{3,2},{4,7},{5,4},{6,5},{7,6},{8,11},{9,8},{10,9... | collective-permute-start | bytes 786440 | tf_op jit(solution)/shard_map/ppermute | solution.py:32
  94.1 0.7 constant_dynamic-slice_fusion.2
  94.8 1.3 fusion.6
  96.1 1.3 reshape.119
  97.5 1.4 reshape.115
  98.8 1.3 dynamic-slice_reduce_fusion
  100.2 1.3 reshape.120.shared_count_ref
  101.5 1.3 reshape.116.count_ref
  102.8 0.7 copy.47
  103.5 1.4 reshape.117
  104.9 0.7 copy.46
  105.6 1.4 reshape.113
  107.1 1.3 constant_dynamic-slice_fusion.1
  108.4 0.7 reshape.114.list_ref
  109.1 0.7 pad_add_fusion.where_ref
  109.8 0.0 all-to-all-done
  109.8 1.2 copy.52
  111.0 0.5 collective-permute-done.1.am0
  111.5 0.0 collective-permute-done.8.last_e
  111.5 0.0 collective-permute-done.6.last_k
  111.5 8.4 %collective-permute-done.7.last_v = bf16[4,4,96,128]{3,2,1,0:T(8,128)(2,1)} collective-permute-done((bf16[4,4,96,128]{3,2,1,0:T(8,128)(2,1)}, bf16[4,4,96,128]{3,2,1,0:T(8,128)(2,1)}, u32[]{:S(2)}, u32[]{:S(2)}) %collective-permute-start.7) | collective-permute-done | bytes 393248 | tf_op jit(solution)/shard_map/ppermute | solution.py:28
  119.9 0.7 copy-done
  120.6 0.6 copy-done.1
  121.2 0.7 copy-done.2
  121.9 22.6 %shard_map.64 = bf16[4,816,128]{2,1,0:T(8,128)(2,1)S(1)} custom-call(s32[3]{0:T(128)S(1)} %copy-done.2, s32[12,16]{1,0:T(8,128)S(1)} %reshape.114.list_ref, s32[12]{0:T(128)S(1)} %copy-done.1, s32[12,16]{1,0:T(8,128)S(1)} %reshape.118.shared_list_ref, s32[12]{0:T(128)S(1)} %copy-done, bf16[24,128,128]{2,1,0:T(8,128)(2,1)S(1)} %bitcast.52, ...), custom_call_target="tpu_custom_call" | custom-call | flops 2013265920 | bytes 10000000 | tf_op jit(solution)/shard_map/pallas_call | solution.py:164
  144.5 17.5 %all_to_all.16 = bf16[4,816,128]{2,1,0:T(8,128)(2,1)S(1)} all-to-all(bf16[4,816,128]{2,1,0:T(8,128)(2,1)S(1)} %shard_map.64), channel_id=1, replica_groups=mesh['xl'=2,'c'=2,'xh'=2,'zh'=2,'zl'=2,'y'=4] {'xh','zh'}, dimensions={0} | all-to-all | bytes 1671168 | tf_op jit(solution)/shard_map/all_to_all | solution.py:236
  162.1 0.3 multiply_reduce_fusion
  162.3 0.1 divide_convert_fusion
  162.5 0.1 copy.66
  162.6 0.2 copy.65
  162.9 8.0 %convolution_convert_fusion = bf16[384,5120]{1,0:T(8,128)(2,1)} fusion(bf16[640,5120]{1,0:T(8,128)(2,1)} %param.11, bf16[384,128]{0,1:T(8,128)(2,1)S(1)} %copy.66, bf16[384,512]{0,1:T(8,128)(2,1)S(1)} %bitcast.59), kind=kOutput, calls=%fused_computation | convolution fusion | flops 2519531520 | bytes 10977280 | tf_op jit(solution)/shard_map/dot_general | solution.py:248
  170.9 0.0 reduce-scatter.2.cloned.1.call-update
  170.9 44.3 %reduce-scatter.2.cloned.1.call-done = bf16[96,5120]{1,0:T(8,128)(2,1)} async-done(((bf16[384,5120]{1,0:T(8,128)(2,1)}), bf16[96,5120]{1,0:T(8,128)(2,1)}) %reduce-scatter.2.cloned.1.call-update) | async-done | bytes 983056 | tf_op jit(solution)/shard_map/reduce_scatter | solution.py:247
  (22 shorter events, 0.3 us)
Async XLA Ops:
  36.7 24.5 %collective-permute-start.2 = (bf16[4,4,256,128]{3,2,1,0:T(8,128)(2,1)S(1)}, bf16[4,4,256,128]{3,2,1,0:T(8,128)(2,1)}, u32[]{:S(2)}, u32[]{:S(2)}) collective-permute-start(bf16[4,4,256,128]{3,2,1,0:T(8,128)(2,1)S(1)} %bitcast.48), channel_id=1, source_target_pairs={{0,3},{1,0},{2,1},{3,2},{4,7},{5,4},{6,5},{7,6},{8,11},{9,8},{10,9... | collective-permute-start | bytes 3145736 | tf_op jit(solution)/shard_map/ppermute | solution.py:32
  39.4 25.3 %collective-permute-start = (bf16[4,4,256,128]{3,2,1,0:T(8,128)(2,1)S(1)}, bf16[4,4,256,128]{3,2,1,0:T(8,128)(2,1)}, u32[]{:S(2)}, u32[]{:S(2)}) collective-permute-start(bf16[4,4,256,128]{3,2,1,0:T(8,128)(2,1)S(1)} %bitcast.49), channel_id=1, source_target_pairs={{0,4},{4,0},{1,5},{5,1},{2,6},{6,2},{3,7},{7,3},{8,12},{12,8},{9,1... | collective-permute-start | bytes 3145736 | tf_op jit(solution)/shard_map/ppermute | solution.py:36
  61.2 24.7 %collective-permute-start.5 = (bf16[4,4,256,128]{3,2,1,0:T(8,128)(2,1)}, bf16[4,4,256,128]{3,2,1,0:T(8,128)(2,1)S(1)}, u32[]{:S(2)}, u32[]{:S(2)}) collective-permute-start(bf16[4,4,256,128]{3,2,1,0:T(8,128)(2,1)} %collective-permute-done.2.ap0), channel_id=1, source_target_pairs={{0,3},{1,0},{2,1},{3,2},{4,7},{5,4},{6,5},{7,6},{8,11},{9,8},{10,9... | collective-permute-start | bytes 3145736 | tf_op jit(solution)/shard_map/ppermute | solution.py:32
  64.7 24.3 %collective-permute-start.4 = (bf16[4,4,256,128]{3,2,1,0:T(8,128)(2,1)}, bf16[4,4,256,128]{3,2,1,0:T(8,128)(2,1)S(1)}, u32[]{:S(2)}, u32[]{:S(2)}) collective-permute-start(bf16[4,4,256,128]{3,2,1,0:T(8,128)(2,1)} %collective-permute-done.a01), channel_id=1, source_target_pairs={{0,1},{1,2},{2,3},{3,0},{4,5},{5,6},{6,7},{7,4},{8,9},{9,10},{10,1... | collective-permute-start | bytes 3145736 | tf_op jit(solution)/shard_map/ppermute | solution.py:28
  64.7 25.1 %collective-permute-start.3 = (bf16[4,4,256,128]{3,2,1,0:T(8,128)(2,1)}, bf16[4,4,256,128]{3,2,1,0:T(8,128)(2,1)}, u32[]{:S(2)}, u32[]{:S(2)}) collective-permute-start(bf16[4,4,256,128]{3,2,1,0:T(8,128)(2,1)} %collective-permute-done.2.ap0), channel_id=1, source_target_pairs={{0,4},{4,0},{1,5},{5,1},{2,6},{6,2},{3,7},{7,3},{8,12},{12,8},{9,1... | collective-permute-start | bytes 3145736 | tf_op jit(solution)/shard_map/ppermute | solution.py:36
  69.1 42.4 %collective-permute-start.1 = (bf16[4,4,256,128]{3,2,1,0:T(8,128)(2,1)S(1)}, bf16[4,4,256,128]{3,2,1,0:T(8,128)(2,1)}, u32[]{:S(2)}, u32[]{:S(2)}) collective-permute-start(bf16[4,4,256,128]{3,2,1,0:T(8,128)(2,1)S(1)} %bitcast.50), channel_id=1, source_target_pairs={{0,1},{1,2},{2,3},{3,0},{4,5},{5,6},{6,7},{7,4},{8,9},{9,10},{10,1... | collective-permute-start | bytes 3145736 | tf_op jit(solution)/shard_map/ppermute | solution.py:28
  75.9 33.8 %all-to-all-start = ((bf16[16,2,96,128]{3,2,1,0:T(8,128)(2,1)}), bf16[16,2,96,128]{3,2,1,0:T(8,128)(2,1)}, u32[]{:S(2)}, u32[]{:S(2)}) async-start(bf16[16,2,96,128]{3,2,1,0:T(8,128)(2,1)} %copy.51), calls=%async_computation | async-start | bytes 1572864 | tf_op jit(solution)/shard_map/all_to_all | solution.py:214
  82.1 133.0 %reduce-scatter.2.cloned.1.call-start = ((), (), s32[]{:S(2)}) async-start(), calls=%async_computation.4 | async-start | bytes 4915200 | tf_op jit(solution)/shard_map/reduce_scatter | solution.py:247
  86.7 24.8 %collective-permute-start.6 = (bf16[4,4,96,128]{3,2,1,0:T(8,128)(2,1)}, bf16[4,4,96,128]{3,2,1,0:T(8,128)(2,1)S(1)}, u32[]{:S(2)}, u32[]{:S(2)}) collective-permute-start(bf16[4,4,96,128]{3,2,1,0:T(8,128)(2,1)} %slice.80), channel_id=1, source_target_pairs={{0,4},{4,0},{1,5},{5,1},{2,6},{6,2},{3,7},{7,3},{8,12},{12,8},{9,1... | collective-permute-start | bytes 1179656 | tf_op jit(solution)/shard_map/ppermute | solution.py:36
  89.8 30.1 %collective-permute-start.7 = (bf16[4,4,96,128]{3,2,1,0:T(8,128)(2,1)}, bf16[4,4,96,128]{3,2,1,0:T(8,128)(2,1)}, u32[]{:S(2)}, u32[]{:S(2)}) collective-permute-start(bf16[4,4,96,128]{3,2,1,0:T(8,128)(2,1)} %slice.81), channel_id=1, source_target_pairs={{0,1},{1,2},{2,3},{3,0},{4,5},{5,6},{6,7},{7,4},{8,9},{9,10},{10,1... | collective-permute-start | bytes 1179656 | tf_op jit(solution)/shard_map/ppermute | solution.py:28
  91.5 20.0 %collective-permute-start.8 = (bf16[4,4,64,128]{3,2,1,0:T(8,128)(2,1)}, bf16[4,4,64,128]{3,2,1,0:T(8,128)(2,1)}, u32[]{:S(2)}, u32[]{:S(2)}) collective-permute-start(bf16[4,4,64,128]{3,2,1,0:T(8,128)(2,1)} %slice.82), channel_id=1, source_target_pairs={{0,3},{1,0},{2,1},{3,2},{4,7},{5,4},{6,5},{7,6},{8,11},{9,8},{10,9... | collective-permute-start | bytes 786440 | tf_op jit(solution)/shard_map/ppermute | solution.py:32
  119.9 0.7 copy-start
  120.6 0.6 copy-start.1
  121.2 0.7 copy-start.2
Sparse Core Ops, SparseCore 0:
  171.0 44.0 reduce-scatter.1

commit v2 on v1

v2 whole, which is shorter than its diff:
```python
import functools

import jax
import jax.numpy as jnp
from jax import lax
from jax.experimental import pallas as pl
from jax.experimental.pallas import tpu as pltpu
from jax.sharding import Mesh, PartitionSpec as P

HEAD = 128
BLOCK = 128
ROWS = 96
CHUNKS = 4
SUPER = ROWS * CHUNKS
EXT = 32
HALF = 16
KV = 2 * ROWS + 2 * EXT
LOG2E = 1.4426950408889634
SCALE = HEAD ** -0.5 * LOG2E
FLOOR = -1e30
NAMES = ("xh", "zh", "zl", "y", "xl", "c")
GRID = ("xl", "c", "xh", "zh", "zl", "y")
SIZES = (2, 2, 2, 2, 2, 4)
SPREAD = ("xh", "zh", "xl", "c")
STATS = 16
UNITS = 12
SLOTS = 16
SMEM = pl.BlockSpec(memory_space=pltpu.SMEM)
VMEM = pl.BlockSpec(memory_space=pltpu.VMEM)
HBM = pl.BlockSpec(memory_space=pl.ANY)


def ring_up(x):
    return lax.ppermute(x, "y", [(i, (i + 1) % 4) for i in range(4)])


def ring_down(x):
    return lax.ppermute(x, "y", [(i, (i - 1) % 4) for i in range(4)])


def swap(x):
    return lax.ppermute(x, "zl", [(0, 1), (1, 0)])


def plan_kernel(where_ref, count_ref, table_ref, main_ref, ext0_ref, ext1_ref, n_ref, lists, sem):
    y, zl, head, shared, group = [where_ref[i] for i in range(5)]
    copies = [
        pltpu.make_async_copy(table_ref.at[h], lists.at[i], sem.at[i])
        for i, h in enumerate((head, shared))
    ]
    for copy in copies:
        copy.start()
    for copy in copies:
        copy.wait()

    def unit_step(unit, carry):
        which = lax.div(unit, UNITS)
        local = unit - which * UNITS
        sb = lax.div(local, 3)
        row = (sb * 8 + zl * 4 + y) * 3 + (local - 3 * sb)
        count = count_ref[jnp.where(which == 0, head, shared), row]
        for stage in range(3):
            n_ref[stage, unit] = 0

        def slot_step(slot, carry):
            block = lists[which, row, slot]
            sb = lax.div(block, 3)
            r = block - 3 * sb
            column = lax.div(sb, 8)
            zy = sb - 8 * column
            dz = lax.rem(lax.div(zy, 4) + zl, 2)
            dy = lax.rem(lax.rem(zy, 4) + 4 - y, 4)
            stage = jnp.where(
                dz == 0, jnp.where(dy == 2, 1, 0), jnp.where(dy == 0, 0, jnp.where(dy == 2, 2, 1))
            )
            piece = jnp.where(
                dz == 0,
                jnp.where(dy == 0, 0, jnp.where(dy == 3, 2, jnp.where(dy == 1, 3, 2))),
                jnp.where(dy == 0, 1, jnp.where(dy == 3, 1, 0)),
            )
            n = n_ref[stage, unit]
            n_ref[stage, unit] = n + 1
            place = piece * 4 + column
            main_ref[stage * 24 + unit, n] = (place * 3 + r) * BLOCK
            for e, ref in enumerate((ext0_ref, ext1_ref)):
                h = r * 8 + group + 4 * e
                chunk = lax.div(h, 6)
                run = lax.div(h - 6 * chunk, 4)
                ref[stage * 24 + unit, n] = (place * CHUNKS + chunk) * EXT + run * HALF
            return carry

        lax.fori_loop(0, count, slot_step, 0)
        return carry

    lax.fori_loop(0, 2 * UNITS, unit_step, 0)


def plan(where, counts, table):
    lists = jax.ShapeDtypeStruct((72, SLOTS), jnp.int32)
    return pl.pallas_call(
        plan_kernel,
        out_shape=(lists, lists, lists, jax.ShapeDtypeStruct((3, 2 * UNITS), jnp.int32)),
        in_specs=[SMEM, SMEM, HBM],
        out_specs=(SMEM, SMEM, SMEM, SMEM),
        scratch_shapes=[pltpu.SMEM((2, 96, SLOTS), jnp.int32), pltpu.SemaphoreType.DMA((2,))],
        cost_estimate=pl.CostEstimate(flops=8_000_000_000, bytes_accessed=100_000, transcendentals=0),
    )(where, counts, table)


def stage_kernel(stage, shapes, *refs):
    first, last = stage == 0, stage == 2
    main_ref, ext0_ref, ext1_ref, n_ref, q_ref = refs[:5]
    refs = refs[5:]
    if not first:
        acc_in, ml_in = refs[:2]
        refs = refs[2:]
    sources, refs = refs[: len(shapes)], refs[len(shapes) :]
    if last:
        out_ref = refs[0]
        refs = refs[1:]
    else:
        acc_out, ml_out = refs[:2]
        refs = refs[2:]
    k_main, v_main, k_ext, v_ext, sem = refs
    copies = []
    for source, parts in zip(sources, shapes):
        lo = 0
        for piece, name in parts:
            target = {"k": k_main, "v": v_main, "a": k_ext, "b": v_ext}[name]
            rows = ROWS if name in "kv" else EXT
            copy = pltpu.make_async_copy(
                source.at[:, :, pl.ds(lo, rows)], target.at[piece], sem.at[len(copies)]
            )
            copy.start()
            copies.append(copy)
            lo += rows
    for copy in copies:
        copy.wait()

    pieces = k_main.shape[0]
    k_flat = k_main.reshape(pieces * 4 * SUPER, HEAD)
    v_flat = v_main.reshape(pieces * 4 * SUPER, HEAD)
    ke_flat = k_ext.reshape(pieces * 4 * CHUNKS * EXT, HEAD)
    ve_flat = v_ext.reshape(pieces * 4 * CHUNKS * EXT, HEAD)
    lane = lax.broadcasted_iota(jnp.int32, (BLOCK, HEAD), 1)
    eye = lax.broadcasted_iota(jnp.int32, (BLOCK, BLOCK), 0) == lane

    def dot_t(a, b):
        return lax.dot_general(a, b, (((1,), (1,)), ((), ())), preferred_element_type=jnp.float32)

    def update(q, keys, values, live, state):
        top, total, acc = state
        s = dot_t(q, keys)
        col = lax.broadcasted_iota(jnp.int32, s.shape, 1)
        s = jnp.where(col < live, s, FLOOR)
        new_top = jnp.maximum(top, jnp.max(s, axis=1, keepdims=True))
        p = jnp.exp2((s - new_top) * SCALE)
        alpha = jnp.exp2((top - new_top) * SCALE)
        total = total * alpha + jnp.sum(p, axis=1, keepdims=True)
        acc = acc * alpha + jnp.dot(p.astype(jnp.bfloat16), values, preferred_element_type=jnp.float32)
        return new_top, total, acc

    def begin(unit):
        if first:
            return (
                jnp.full((BLOCK, 1), FLOOR, jnp.float32),
                jnp.zeros((BLOCK, 1), jnp.float32),
                jnp.zeros((BLOCK, HEAD), jnp.float32),
            )
        ml = ml_in[unit]
        return ml[:, :1], ml[:, HEAD // 2 : HEAD // 2 + 1], acc_in[unit]

    def keep(unit, state):
        top, total, acc = state
        acc_out[unit] = acc
        ml_out[unit] = jnp.where(lane < HEAD // 2, top, total)

    def run(unit, group, width, rows_of, key_flat, value_flat, rows):
        n = n_ref[stage, unit]
        q = q_ref[unit]

        def step(t, state):
            starts = []
            for i in range(group):
                starts += rows_of(stage * 24 + unit, jnp.minimum(group * t + i, n - 1))
            keys = jnp.concatenate([key_flat[pl.ds(r, rows), :] for r in starts], axis=0)
            values = jnp.concatenate([value_flat[pl.ds(r, rows), :] for r in starts], axis=0)
            return update(q, keys, values, (n - group * t) * width, state)

        return lax.fori_loop(0, lax.div(n + (group - 1), group), step, begin(unit))

    def main_rows(row, slot):
        return [pl.multiple_of(main_ref[row, slot], BLOCK)]

    def ext_rows(row, slot):
        return [pl.multiple_of(ref[row, slot], HALF) for ref in (ext0_ref, ext1_ref)]

    def main_unit(unit, carry):
        state = run(unit, 2 if last else 4, BLOCK, main_rows, k_flat, v_flat, BLOCK)
        if not last:
            keep(unit, state)
            return carry
        top, total, acc = state
        sb = lax.div(unit, 3)
        row = pl.multiple_of((unit - 3 * sb) * BLOCK, BLOCK)
        out_ref[sb, pl.ds(row, BLOCK), :] = (acc / total).astype(jnp.bfloat16)
        return carry

    def ext_unit(local, carry):
        unit = UNITS + local
        state = run(unit, 4 if last else 8, 2 * HALF, ext_rows, ke_flat, ve_flat, HALF)
        if not last:
            keep(unit, state)
            return carry
        top, total, acc = state
        sb = lax.div(local, 3)
        row = pl.multiple_of((local - 3 * sb) * BLOCK, BLOCK)
        out_ref[sb, pl.ds(SUPER + row, BLOCK), :] = (acc / total).astype(jnp.bfloat16)
        level = top * SCALE + jnp.log2(total)
        level = jnp.sum(jnp.where(eye, level, 0.0), axis=0, keepdims=True)
        high = level.astype(jnp.bfloat16).astype(jnp.float32)
        rest = level - high
        mid = rest.astype(jnp.bfloat16).astype(jnp.float32)
        low = rest - mid
        index = lax.broadcasted_iota(jnp.int32, (STATS, HEAD), 0)
        tile = jnp.where(index == 0, high, jnp.where(index == 1, mid, jnp.where(index == 2, low, 0.0)))
        at = pl.multiple_of(2 * SUPER + (local - 3 * sb) * STATS, STATS)
        out_ref[sb, pl.ds(at, STATS), :] = tile.astype(jnp.bfloat16)
        return carry

    lax.fori_loop(0, UNITS, main_unit, 0)
    lax.fori_loop(0, UNITS, ext_unit, 0)


def attend(stage, plans, q, state, sources, shapes):
    pieces = 1 + max(piece for parts in shapes for piece, _ in parts)
    copies = sum(len(parts) for parts in shapes)
    kept = jax.ShapeDtypeStruct((2 * UNITS, BLOCK, HEAD), jnp.float32)
    if stage == 2:
        out_shape = jax.ShapeDtypeStruct((4, 2 * SUPER + 3 * STATS, HEAD), jnp.bfloat16)
        out_specs = VMEM
    else:
        out_shape, out_specs = (kept, kept), (VMEM, VMEM)
    share = pieces / 8
    return pl.pallas_call(
        functools.partial(stage_kernel, stage, shapes),
        out_shape=out_shape,
        in_specs=[SMEM] * 4 + [VMEM] * (1 + len(state)) + [HBM] * len(sources),
        out_specs=out_specs,
        scratch_shapes=[
            pltpu.VMEM((pieces, 4, CHUNKS, ROWS, HEAD), jnp.bfloat16),
            pltpu.VMEM((pieces, 4, CHUNKS, ROWS, HEAD), jnp.bfloat16),
            pltpu.VMEM((pieces, 4, CHUNKS, EXT, HEAD), jnp.bfloat16),
            pltpu.VMEM((pieces, 4, CHUNKS, EXT, HEAD), jnp.bfloat16),
            pltpu.SemaphoreType.DMA((copies,)),
        ],
        compiler_params=pltpu.CompilerParams(vmem_limit_bytes=32 * 1024 * 1024),
        cost_estimate=pl.CostEstimate(
            flops=int(share * 20e9), bytes_accessed=int(share * 10e6), transcendentals=int(share * 4e6)
        ),
    )(*plans, q, *state, *sources)


def to_groups(main):
    rows = main.shape[0]
    return main.transpose(2, 1, 0, 3).reshape(16, rows, HEAD)


def shared_keys(rows, core):
    runs = jnp.pad(rows, ((0, 32), (0, 0), (0, 0))).reshape(2, 4, HALF, 4, HEAD)
    runs = jnp.where(core == 0, runs, jnp.roll(runs, 2, axis=1))
    return runs.transpose(1, 3, 0, 2, 4).reshape(16, EXT, HEAD)


def per_device(queries, key_rows, value_rows, block_list, block_count, w_out):
    xh, zh, zl, y, xl, c = [lax.axis_index(name) for name in NAMES]
    u = 2 * xl + c
    group = 2 * xh + zh
    k5 = key_rows.reshape(ROWS, 4, 5, HEAD)
    v5 = value_rows.reshape(ROWS, 4, 5, HEAD)
    q5 = queries.reshape(ROWS, 4, 5, HEAD)
    sent = jnp.concatenate(
        [
            to_groups(k5[:, :, :4]),
            to_groups(v5[:, :, :4]),
            shared_keys(k5[:, :, 4], c),
            shared_keys(v5[:, :, 4], c),
            to_groups(q5[:, :, :4]),
            to_groups(jnp.broadcast_to(q5[:, :, 4:], (ROWS, 4, 4, HEAD))),
        ],
        axis=1,
    )
    got = lax.all_to_all(sent, SPREAD, 0, 0, tiled=True).reshape(4, CHUNKS, KV + 2 * ROWS, HEAD)
    kv = got[:, :, :KV]

    where = jnp.stack([y, zl, 5 * u + group, 5 * u + 4, group]).astype(jnp.int32)
    plans = plan(where, block_count, block_list)
    q = got[:, :, KV:].reshape(4, CHUNKS, 2, ROWS, HEAD)
    q = q.transpose(2, 0, 1, 3, 4).reshape(2 * UNITS, BLOCK, HEAD)

    a01, am0, ap0 = swap(kv), ring_up(kv), ring_down(kv)
    a01, am0, ap0, q, plans = lax.optimization_barrier((a01, am0, ap0, q, plans))
    a11, am1, a20 = swap(ap0), ring_up(a01), ring_down(ap0)
    whole = lambda piece: tuple((piece, name) for name in "kvab")
    state = attend(0, plans, q, (), (kv, a01, am0, ap0), tuple(whole(i) for i in range(4)))
    a11, am1, a20, state = lax.optimization_barrier((a11, am1, a20, state))
    last_k = swap(a20[:, :, :ROWS])
    last_v = ring_up(am1[:, :, ROWS : 2 * ROWS])
    last_e = ring_down(a11[:, :, 2 * ROWS :])
    state = attend(1, plans, q, state, (a11, am1, a20), tuple(whole(i) for i in range(3)))
    out = attend(
        2, plans, q, state, (last_k, last_v, last_e), (((0, "k"),), ((0, "v"),), ((0, "a"), (0, "b")))
    )
    out = lax.all_to_all(out, ("xh", "zh"), 0, 0, tiled=True)

    heads = out[:, :SUPER]
    shares = out[:, SUPER : 2 * SUPER].astype(jnp.float32)
    level = out[:, 2 * SUPER :].reshape(4, 3, STATS, BLOCK)[:, :, :3].astype(jnp.float32)
    level = jnp.sum(level, axis=2).reshape(4, SUPER, 1)
    weight = jnp.exp2(level - jnp.max(level, axis=0, keepdims=True))
    shared = jnp.sum(shares * weight, axis=0) / jnp.sum(weight, axis=0)
    attended = jnp.concatenate(
        [heads.transpose(1, 0, 2).reshape(SUPER, 4 * HEAD), shared.astype(jnp.bfloat16)], axis=1
    )
    return lax.psum_scatter(
        jnp.dot(attended, w_out, preferred_element_type=jnp.float32).astype(jnp.bfloat16),
        ("xl", "c"),
        scatter_dimension=0,
        tiled=True,
    )


def solution(mesh):
    fine = Mesh(mesh.devices.reshape(SIZES), GRID)
    rows = P(NAMES, None)
    return jax.shard_map(
        per_device,
        mesh=fine,
        in_specs=(rows, rows, rows, P(), P(), P(("xl", "c"), None)),
        out_specs=rows,
        check_vma=False,
    )
```

time: 224 us -> 214 us (0.955)
  Pallas kernels: 22.6 us -> 60.6 us
  local copies, waits for them, and re-layouts: 35.7 us -> 8.58 us
  waiting for transfers between devices: 79.6 us -> 54.3 us
  blocking collectives: 43.8 us -> 57.9 us
  starting transfers between devices: 17.4 us -> 9.26 us
    pallas_call x1 -> x4, Pallas kernels: 22.6 us -> 60.6 us  [the longest x3 45.8 us: attend(): pl.pallas_call(functools.partial(stage_kernel, stage, shapes), out_shape=...]
    ppermute x3, waiting for transfers between devices: 24.7 us -> 2.68 us  [ring_down(): return lax.ppermute(x, 'y', [(i, (i - 1) % 4) for i in range(4)])]
    reshape x9 -> x0, local copies, waits for them, and re-layouts: 10.1 us -> none  [the longest x4 5.55 us: pick(): mine = mine.reshape((4, 8, 3) + mine.shape[1:])]
    all_to_all x1, blocking collectives: 26.3 us -> 34.5 us  [per_device(): lax.all_to_all(sent, SPREAD, 0, 0, tiled=True)]
    all_to_all x1 -> x0, starting transfers between devices: 6.2 us -> none  [per_device(): q = lax.all_to_all(q, SPREAD, 0, 0, tiled=True)]
    dynamic_slice x6 -> x0, local copies, waits for them, and re-layouts: 6.06 us -> none  [the longest x4 3.41 us: pick(): mine = lax.dynamic_index_in_dim(table, head, 0, keepdims=False)]
    all_to_all x1, blocking collectives: 17.5 us -> 23.4 us  [per_device(): out = lax.all_to_all(out, ('xh', 'zh'), 0, 0, tiled=True)]
    ppermute x3, waiting for transfers between devices: 10.5 us -> 7.66 us  [ring_up(): return lax.ppermute(x, 'y', [(i, (i + 1) % 4) for i in range(4)])]
  transfers between devices with their start and end apart: 11 -> 10, of which waited for: 6 -> 5; matrix products, arithmetic and copies ran while one was open for 14% -> 2% of each run, Pallas kernels for 0% -> 22%
where the time goes in v2:
time: 214 us
  Pallas kernels  60.6 us (28%)
  blocking collectives  57.9 us (27%)
  waiting for transfers between devices  54.3 us (25%)
  between operations  13.8 us (6%)
  starting transfers between devices  9.26 us (4%)
  local copies, waits for them, and re-layouts  8.58 us (4%)
  matrix products  8 us (4%)
    pallas_call x3, Pallas kernels, attend(): pl.pallas_call(functools.partial(stage_kernel, stage, shapes), out_shape=...  45.8 us
    reduce_scatter x1, waiting for transfers between devices, per_device(): lax.psum_scatter(jnp.dot(attended, w_out, preferred_element_type=jnp.floa...  43.2 us
    all_to_all x1, blocking collectives, per_device(): lax.all_to_all(sent, SPREAD, 0, 0, tiled=True)  34.5 us
    all_to_all x1, blocking collectives, per_device(): out = lax.all_to_all(out, ('xh', 'zh'), 0, 0, tiled=True)  23.4 us
    pallas_call x1, Pallas kernels, plan(): pl.pallas_call(plan_kernel, out_shape=(lists, lists, lists, jax.ShapeDtyp...  14.8 us
    dot_general x1, matrix products, per_device(): jnp.dot(attended, w_out, preferred_element_type=jnp.float32)  8 us
    ppermute x3, waiting for transfers between devices, ring_up(): return lax.ppermute(x, 'y', [(i, (i + 1) % 4) for i in range(4)])  7.66 us
    ppermute x3, starting transfers between devices, ring_down(): return lax.ppermute(x, 'y', [(i, (i - 1) % 4) for i in range(4)])  7.04 us
  transfers between devices with their start and end apart: 10, of which 5 were waited for; matrix products, arithmetic and copies ran while one was open for 2% of the time, Pallas kernels for 22%

profile of v2, /device:TPU:1, one launch (start us, length us, event | category | flops | bytes accessed | tf_op | source)
XLA Modules:
  0.0 213.8 jit_solution(10157309273184939271)
XLA Ops:
  6.5 0.0 reduce-scatter.2.cloned.1.call-start
  6.5 1.4 copy.60
  8.0 0.0 copy-start.6
  8.0 0.0 copy-done.5
  8.0 0.3 copy.48
  8.4 0.5 copy-done.6
  9.0 0.3 copy.50
  9.4 0.2 copy.61
  9.6 0.1 copy.62
  9.8 0.2 copy.49
  10.0 0.1 copy.52
  10.2 0.2 copy.51
  10.4 0.1 copy.56
  10.6 0.6 fusion.6
  11.3 0.1 constant_dynamic-update-slice_fusion.4
  11.3 1.0 maximum_select_fusion
  12.3 0.1 constant_dynamic-update-slice_fusion.1
  12.4 0.1 broadcast_in_dim.9
  12.4 0.1 constant_dynamic-update-slice_fusion
  12.5 34.5 %all_to_all.10 = bf16[16,448,128]{2,1,0:T(8,128)(2,1)S(1)} all-to-all(bf16[16,448,128]{2,1,0:T(8,128)(2,1)S(1)} %constant_dynamic-update-slice_fusion), channel_id=1, replica_groups=mesh['xl'=2,'c'=2,'xh'=2,'zh'=2,'zl'=2,'y'=4] {'xh','zh','xl','c'}, dimensions={0} | all-to-all | bytes 3670016 | tf_op jit(solution)/shard_map/all_to_all | solution.py:293
  47.0 0.1 slice.88.refs_5_
  47.1 2.8 %collective-permute-start.2 = (bf16[4,4,256,128]{3,2,1,0:T(8,128)(2,1)S(1)}, bf16[4,4,256,128]{3,2,1,0:T(8,128)(2,1)S(1)}, u32[]{:S(2)}, u32[]{:S(2)}) collective-permute-start(bf16[4,4,256,128]{3,2,1,0:T(8,128)(2,1)S(1)} %slice.88.refs_5_), channel_id=1, source_target_pairs={{0,3},{1,0},{2,1},{3,2},{4,7},{5,4},{6,5},{7,6},{8,11},{9,8},{10,9... | collective-permute-start | bytes 3145736 | tf_op jit(solution)/shard_map/ppermute | solution.py:38
  49.9 0.0 copy-done.4
  49.9 0.0 collective-permute-start.1
  49.9 0.7 collective-permute-start
  50.6 0.0 copy-done.7
  50.6 1.3 copy.64.table_ref
  51.9 0.7 stack.23.where_ref
  52.5 14.8 %shard_map.64 = (s32[72,16]{1,0:T(8,128)}, s32[72,16]{1,0:T(8,128)}, s32[72,16]{1,0:T(8,128)}, s32[3,24]{1,0:T(4,128)}) custom-call(s32[5]{0:T(128)} %stack.23.where_ref, s32[20,96]{1,0:T(8,128)} %count_ref.1, s32[20,96,16]{2,1,0:T(8,128)} %copy.64.table_ref), custom_call_target="tpu_custom_call" | custom-call | flops 8000000000 | bytes 100000 | tf_op jit(solution)/shard_map/pallas_call | solution.py:100
  67.3 0.0 copy-start
  67.4 0.0 copy-start.1
  67.4 0.0 copy-start.2
  67.4 0.0 copy-start.3
  67.4 1.2 slice.89
  68.6 0.1 copy.63
  68.7 2.7 %collective-permute-done.2.refs_8_ = bf16[4,4,256,128]{3,2,1,0:T(8,128)(2,1)S(1)} collective-permute-done((bf16[4,4,256,128]{3,2,1,0:T(8,128)(2,1)S(1)}, bf16[4,4,256,128]{3,2,1,0:T(8,128)(2,1)S(1)}, u32[]{:S(2)}, u32[]{:S(2)}) %collective-permute-start.2) | collective-permute-done | bytes 1048608 | tf_op jit(solution)/shard_map/ppermute | solution.py:38
  71.3 3.1 %collective-permute-done.1.refs_7_ = bf16[4,4,256,128]{3,2,1,0:T(8,128)(2,1)S(1)} collective-permute-done((bf16[4,4,256,128]{3,2,1,0:T(8,128)(2,1)S(1)}, bf16[4,4,256,128]{3,2,1,0:T(8,128)(2,1)S(1)}, u32[]{:S(2)}, u32[]{:S(2)}) %collective-permute-start.1) | collective-permute-done | bytes 1048608 | tf_op jit(solution)/shard_map/ppermute | solution.py:34
  74.5 0.0 collective-permute-done.refs_6_
  74.5 0.0 collective-permute-start.4
  74.5 2.7 %collective-permute-start.5 = (bf16[4,4,256,128]{3,2,1,0:T(8,128)(2,1)S(1)}, bf16[4,4,256,128]{3,2,1,0:T(8,128)(2,1)S(1)}, u32[]{:S(2)}, u32[]{:S(2)}) collective-permute-start(bf16[4,4,256,128]{3,2,1,0:T(8,128)(2,1)S(1)} %collective-permute-done.2.refs_8_), channel_id=1, source_target_pairs={{0,3},{1,0},{2,1},{3,2},{4,7},{5,4},{6,5},{7,6},{8,11},{9,8},{10,9... | collective-permute-start | bytes 3145736 | tf_op jit(solution)/shard_map/ppermute | solution.py:38
  77.2 0.7 collective-permute-start.3
  77.9 0.0 copy-done
  77.9 0.0 copy-done.1
  77.9 0.0 copy-done.3
  77.9 15.9 %shard_map.65 = (f32[24,128,128]{2,1,0:T(8,128)S(1)}, f32[24,128,128]{2,1,0:T(8,128)S(1)}) custom-call(s32[72,16]{1,0:T(8,128)S(1)} %copy-done, s32[72,16]{1,0:T(8,128)S(1)} %copy-done.1, s32[72,16]{1,0:T(8,128)S(1)} %copy-done.2, s32[3,24]{1,0:T(4,128)S(1)} %copy-done.3, bf16[24,128,128]{2,1,0:T(8,128)(2,1)S(1)} %bitcast.50, ...), custom_call_target="tpu_custom_call" | custom-call | flops 10000000000 | bytes 5000000 | tf_op jit(solution)/shard_map/pallas_call | solution.py:245
  93.8 4.5 %collective-permute-done.4.refs_8_ = bf16[4,4,256,128]{3,2,1,0:T(8,128)(2,1)S(1)} collective-permute-done((bf16[4,4,256,128]{3,2,1,0:T(8,128)(2,1)}, bf16[4,4,256,128]{3,2,1,0:T(8,128)(2,1)S(1)}, u32[]{:S(2)}, u32[]{:S(2)}) %collective-permute-start.4) | collective-permute-done | bytes 1048608 | tf_op jit(solution)/shard_map/ppermute | solution.py:34
  98.4 0.0 collective-permute-done.5.refs_9_
  98.4 0.7 collective-permute-done.3.refs_7_
  99.2 1.6 collective-permute-start.8
  100.7 0.0 collective-permute-start.7
  100.7 0.7 collective-permute-start.6
  101.5 17.2 %shard_map.66 = (f32[24,128,128]{2,1,0:T(8,128)S(1)}, f32[24,128,128]{2,1,0:T(8,128)S(1)}) custom-call(s32[72,16]{1,0:T(8,128)S(1)} %copy-done, s32[72,16]{1,0:T(8,128)S(1)} %copy-done.1, s32[72,16]{1,0:T(8,128)S(1)} %copy-done.2, s32[3,24]{1,0:T(4,128)S(1)} %copy-done.3, bf16[24,128,128]{2,1,0:T(8,128)(2,1)S(1)} %bitcast.51, ...), custom_call_target="tpu_custom_call" | custom-call | flops 7500000256 | bytes 3750000 | tf_op jit(solution)/shard_map/pallas_call | solution.py:245
  118.7 0.0 collective-permute-done.8.refs_9_
  118.7 0.0 collective-permute-done.7.refs_8_
  118.7 0.0 collective-permute-done.6.refs_7_
  118.7 12.7 %shard_map.67 = bf16[4,816,128]{2,1,0:T(8,128)(2,1)S(1)} custom-call(s32[72,16]{1,0:T(8,128)S(1)} %copy-done, s32[72,16]{1,0:T(8,128)S(1)} %copy-done.1, s32[72,16]{1,0:T(8,128)S(1)} %copy-done.2, s32[3,24]{1,0:T(4,128)S(1)} %copy-done.3, bf16[24,128,128]{2,1,0:T(8,128)(2,1)S(1)} %bitcast.52, f32[24,128,128]{2,1,0:T(8,128)S(1)} %get-tuple-element.45.refs_5_, ...), custom_call_target="tpu_custom_call" | custom-call | flops 2500000000 | bytes 1250000 | tf_op jit(solution)/shard_map/pallas_call | solution.py:245
  131.4 23.4 %all_to_all.11 = bf16[4,816,128]{2,1,0:T(8,128)(2,1)S(1)} all-to-all(bf16[4,816,128]{2,1,0:T(8,128)(2,1)S(1)} %shard_map.67), channel_id=1, replica_groups=mesh['xl'=2,'c'=2,'xh'=2,'zh'=2,'zl'=2,'y'=4] {'xh','zh'}, dimensions={0} | all-to-all | bytes 1671168 | tf_op jit(solution)/shard_map/all_to_all | solution.py:314
  154.9 0.3 multiply_reduce_fusion
  155.2 0.1 divide_convert_fusion
  155.3 0.1 copy.66
  155.5 0.2 copy.65
  155.7 8.0 %convolution_convert_fusion = bf16[384,5120]{1,0:T(8,128)(2,1)} fusion(bf16[640,5120]{1,0:T(8,128)(2,1)} %param.11, bf16[384,128]{0,1:T(8,128)(2,1)S(1)} %copy.66, bf16[384,512]{0,1:T(8,128)(2,1)S(1)} %bitcast.62), kind=kOutput, calls=%fused_computation | convolution fusion | flops 2519531520 | bytes 10977280 | tf_op jit(solution)/shard_map/dot_general | solution.py:326
  163.7 0.0 reduce-scatter.2.cloned.1.call-update
  163.7 43.2 %reduce-scatter.2.cloned.1.call-done = bf16[96,5120]{1,0:T(8,128)(2,1)} async-done(((bf16[384,5120]{1,0:T(8,128)(2,1)}), bf16[96,5120]{1,0:T(8,128)(2,1)}) %reduce-scatter.2.cloned.1.call-update) | async-done | bytes 983056 | tf_op jit(solution)/shard_map/reduce_scatter | solution.py:325
  (25 shorter events, 0.5 us)
Async XLA Ops:
  6.5 1.5 copy-start.5
  6.5 200.4 %reduce-scatter.2.cloned.1.call-start = ((), (), s32[]{:S(2)}) async-start(), calls=%async_computation.3 | async-start | bytes 4915200 | tf_op jit(solution)/shard_map/reduce_scatter | solution.py:325
  8.0 1.0 copy-start.6
  47.0 2.9 %copy-start.4 = (bf16[16,448,128]{2,1,0:T(8,128)(2,1)}, bf16[16,448,128]{2,1,0:T(8,128)(2,1)S(1)}, u32[]{:S(2)}) copy-start(bf16[16,448,128]{2,1,0:T(8,128)(2,1)S(1)} %all_to_all.10) | copy-start | bytes 5505028
  47.0 3.6 %copy-start.7 = (s32[20,96,16]{1,2,0:T(8,128)S(1)}, s32[20,96,16]{1,2,0:T(8,128)}, u32[]{:S(2)}) copy-start(s32[20,96,16]{1,2,0:T(8,128)} %param.9) | copy-start | bytes 368644
  47.1 24.3 %collective-permute-start.2 = (bf16[4,4,256,128]{3,2,1,0:T(8,128)(2,1)S(1)}, bf16[4,4,256,128]{3,2,1,0:T(8,128)(2,1)S(1)}, u32[]{:S(2)}, u32[]{:S(2)}) collective-permute-start(bf16[4,4,256,128]{3,2,1,0:T(8,128)(2,1)S(1)} %slice.88.refs_5_), channel_id=1, source_target_pairs={{0,3},{1,0},{2,1},{3,2},{4,7},{5,4},{6,5},{7,6},{8,11},{9,8},{10,9... | collective-permute-start | bytes 3145736 | tf_op jit(solution)/shard_map/ppermute | solution.py:38
  49.9 24.6 %collective-permute-start.1 = (bf16[4,4,256,128]{3,2,1,0:T(8,128)(2,1)S(1)}, bf16[4,4,256,128]{3,2,1,0:T(8,128)(2,1)S(1)}, u32[]{:S(2)}, u32[]{:S(2)}) collective-permute-start(bf16[4,4,256,128]{3,2,1,0:T(8,128)(2,1)S(1)} %slice.88.refs_5_), channel_id=1, source_target_pairs={{0,1},{1,2},{2,3},{3,0},{4,5},{5,6},{6,7},{7,4},{8,9},{9,10},{10,1... | collective-permute-start | bytes 3145736 | tf_op jit(solution)/shard_map/ppermute | solution.py:34
  49.9 24.6 %collective-permute-start = (bf16[4,4,256,128]{3,2,1,0:T(8,128)(2,1)S(1)}, bf16[4,4,256,128]{3,2,1,0:T(8,128)(2,1)}, u32[]{:S(2)}, u32[]{:S(2)}) collective-permute-start(bf16[4,4,256,128]{3,2,1,0:T(8,128)(2,1)S(1)} %slice.88.refs_5_), channel_id=1, source_target_pairs={{0,4},{4,0},{1,5},{5,1},{2,6},{6,2},{3,7},{7,3},{8,12},{12,8},{9,1... | collective-permute-start | bytes 3145736 | tf_op jit(solution)/shard_map/ppermute | solution.py:42
  67.3 10.5 %copy-start = (s32[72,16]{1,0:T(8,128)S(1)}, s32[72,16]{1,0:T(8,128)}, u32[]{:S(2)}) copy-start(s32[72,16]{1,0:T(8,128)} %get-tuple-element.30.refs_0_) | copy-start | bytes 13828
  67.4 10.5 %copy-start.1 = (s32[72,16]{1,0:T(8,128)S(1)}, s32[72,16]{1,0:T(8,128)}, u32[]{:S(2)}) copy-start(s32[72,16]{1,0:T(8,128)} %get-tuple-element.31.refs_1_) | copy-start | bytes 13828
  67.4 10.5 %copy-start.2 = (s32[72,16]{1,0:T(8,128)S(1)}, s32[72,16]{1,0:T(8,128)}, u32[]{:S(2)}) copy-start(s32[72,16]{1,0:T(8,128)} %get-tuple-element.32.refs_2_) | copy-start | bytes 13828
  67.4 10.5 %copy-start.3 = (s32[3,24]{1,0:T(4,128)S(1)}, s32[3,24]{1,0:T(4,128)}, u32[]{:S(2)}) copy-start(s32[3,24]{1,0:T(4,128)} %get-tuple-element.33.refs_3_) | copy-start | bytes 868
  74.5 23.9 %collective-permute-start.4 = (bf16[4,4,256,128]{3,2,1,0:T(8,128)(2,1)}, bf16[4,4,256,128]{3,2,1,0:T(8,128)(2,1)S(1)}, u32[]{:S(2)}, u32[]{:S(2)}) collective-permute-start(bf16[4,4,256,128]{3,2,1,0:T(8,128)(2,1)} %collective-permute-done.refs_6_), channel_id=1, source_target_pairs={{0,1},{1,2},{2,3},{3,0},{4,5},{5,6},{6,7},{7,4},{8,9},{9,10},{10,1... | collective-permute-start | bytes 3145736 | tf_op jit(solution)/shard_map/ppermute | solution.py:34
  74.5 23.9 %collective-permute-start.5 = (bf16[4,4,256,128]{3,2,1,0:T(8,128)(2,1)S(1)}, bf16[4,4,256,128]{3,2,1,0:T(8,128)(2,1)S(1)}, u32[]{:S(2)}, u32[]{:S(2)}) collective-permute-start(bf16[4,4,256,128]{3,2,1,0:T(8,128)(2,1)S(1)} %collective-permute-done.2.refs_8_), channel_id=1, source_target_pairs={{0,3},{1,0},{2,1},{3,2},{4,7},{5,4},{6,5},{7,6},{8,11},{9,8},{10,9... | collective-permute-start | bytes 3145736 | tf_op jit(solution)/shard_map/ppermute | solution.py:38
  77.2 21.9 %collective-permute-start.3 = (bf16[4,4,256,128]{3,2,1,0:T(8,128)(2,1)S(1)}, bf16[4,4,256,128]{3,2,1,0:T(8,128)(2,1)S(1)}, u32[]{:S(2)}, u32[]{:S(2)}) collective-permute-start(bf16[4,4,256,128]{3,2,1,0:T(8,128)(2,1)S(1)} %collective-permute-done.2.refs_8_), channel_id=1, source_target_pairs={{0,4},{4,0},{1,5},{5,1},{2,6},{6,2},{3,7},{7,3},{8,12},{12,8},{9,1... | collective-permute-start | bytes 3145736 | tf_op jit(solution)/shard_map/ppermute | solution.py:42
  99.2 19.5 %collective-permute-start.8 = (bf16[4,4,64,128]{3,2,1,0:T(8,128)(2,1)S(1)}, bf16[4,4,64,128]{3,2,1,0:T(8,128)(2,1)S(1)}, u32[]{:S(2)}, u32[]{:S(2)}) collective-permute-start(bf16[4,4,64,128]{3,2,1,0:T(8,128)(2,1)S(1)} %slice.73), channel_id=1, source_target_pairs={{0,3},{1,0},{2,1},{3,2},{4,7},{5,4},{6,5},{7,6},{8,11},{9,8},{10,9... | collective-permute-start | bytes 786440 | tf_op jit(solution)/shard_map/ppermute | solution.py:38
  100.7 17.9 %collective-permute-start.7 = (bf16[4,4,96,128]{3,2,1,0:T(8,128)(2,1)S(1)}, bf16[4,4,96,128]{3,2,1,0:T(8,128)(2,1)S(1)}, u32[]{:S(2)}, u32[]{:S(2)}) collective-permute-start(bf16[4,4,96,128]{3,2,1,0:T(8,128)(2,1)S(1)} %slice.72), channel_id=1, source_target_pairs={{0,1},{1,2},{2,3},{3,0},{4,5},{5,6},{6,7},{7,4},{8,9},{9,10},{10,1... | collective-permute-start | bytes 1179656 | tf_op jit(solution)/shard_map/ppermute | solution.py:34
  100.7 18.0 %collective-permute-start.6 = (bf16[4,4,96,128]{3,2,1,0:T(8,128)(2,1)S(1)}, bf16[4,4,96,128]{3,2,1,0:T(8,128)(2,1)S(1)}, u32[]{:S(2)}, u32[]{:S(2)}) collective-permute-start(bf16[4,4,96,128]{3,2,1,0:T(8,128)(2,1)S(1)} %slice.71), channel_id=1, source_target_pairs={{0,4},{4,0},{1,5},{5,1},{2,6},{6,2},{3,7},{7,3},{8,12},{12,8},{9,1... | collective-permute-start | bytes 1179656 | tf_op jit(solution)/shard_map/ppermute | solution.py:42
Sparse Core Ops, SparseCore 0:
  163.9 43.0 reduce-scatter.1

commit v3 on v2

--- a/solution.py
+++ b/solution.py
@@ -25,6 +25,10 @@
 STATS = 16
 UNITS = 12
 SLOTS = 16
+MAIN_UNROLL = (12, 12, 12)
+MAIN_GROUP = (2, 2, 2)
+EXT_UNROLL = (12, 12, 12)
+EXT_GROUP = (4, 4, 4)
 SMEM = pl.BlockSpec(memory_space=pltpu.SMEM)
 VMEM = pl.BlockSpec(memory_space=pltpu.VMEM)
 HBM = pl.BlockSpec(memory_space=pl.ANY)
@@ -61,6 +65,8 @@
         count = count_ref[jnp.where(which == 0, head, shared), row]
         for stage in range(3):
             n_ref[stage, unit] = 0
+            for ref in (main_ref, ext0_ref, ext1_ref):
+                ref[stage * 24 + unit, 0] = 0
 
         def slot_step(slot, carry):
             block = lists[which, row, slot]
@@ -112,16 +118,15 @@
     main_ref, ext0_ref, ext1_ref, n_ref, q_ref = refs[:5]
     refs = refs[5:]
     if not first:
-        acc_in, ml_in = refs[:2]
-        refs = refs[2:]
+        before = refs[:3]
+        refs = refs[3:]
     sources, refs = refs[: len(shapes)], refs[len(shapes) :]
     if last:
         out_ref = refs[0]
         refs = refs[1:]
+        k_main, v_main, k_ext, v_ext, sem, top_ref, tot_ref, acc_ref = refs
     else:
-        acc_out, ml_out = refs[:2]
-        refs = refs[2:]
-    k_main, v_main, k_ext, v_ext, sem = refs
+        top_ref, tot_ref, acc_ref, k_main, v_main, k_ext, v_ext, sem = refs
     copies = []
     for source, parts in zip(sources, shapes):
         lo = 0
@@ -134,6 +139,18 @@
             copy.start()
             copies.append(copy)
             lo += rows
+
+    def begin(unit, carry):
+        if first:
+            top_ref[unit] = jnp.full((BLOCK, HEAD), FLOOR, jnp.float32)
+            tot_ref[unit] = jnp.zeros((BLOCK, HEAD), jnp.float32)
+            acc_ref[unit] = jnp.zeros((BLOCK, HEAD), jnp.float32)
+        else:
+            for old, new in zip(before, (top_ref, tot_ref, acc_ref)):
+                new[unit] = old[unit]
+        return carry
+
+    lax.fori_loop(0, 2 * UNITS, begin, 0)
     for copy in copies:
         copy.wait()
 
@@ -148,112 +165,112 @@
     def dot_t(a, b):
         return lax.dot_general(a, b, (((1,), (1,)), ((), ())), preferred_element_type=jnp.float32)
 
-    def update(q, keys, values, live, state):
-        top, total, acc = state
-        s = dot_t(q, keys)
-        col = lax.broadcasted_iota(jnp.int32, s.shape, 1)
-        s = jnp.where(col < live, s, FLOOR)
-        new_top = jnp.maximum(top, jnp.max(s, axis=1, keepdims=True))
-        p = jnp.exp2((s - new_top) * SCALE)
-        alpha = jnp.exp2((top - new_top) * SCALE)
-        total = total * alpha + jnp.sum(p, axis=1, keepdims=True)
-        acc = acc * alpha + jnp.dot(p.astype(jnp.bfloat16), values, preferred_element_type=jnp.float32)
-        return new_top, total, acc
-
-    def begin(unit):
-        if first:
-            return (
-                jnp.full((BLOCK, 1), FLOOR, jnp.float32),
-                jnp.zeros((BLOCK, 1), jnp.float32),
-                jnp.zeros((BLOCK, HEAD), jnp.float32),
-            )
-        ml = ml_in[unit]
-        return ml[:, :1], ml[:, HEAD // 2 : HEAD // 2 + 1], acc_in[unit]
-
-    def keep(unit, state):
-        top, total, acc = state
-        acc_out[unit] = acc
-        ml_out[unit] = jnp.where(lane < HEAD // 2, top, total)
-
-    def run(unit, group, width, rows_of, key_flat, value_flat, rows):
-        n = n_ref[stage, unit]
-        q = q_ref[unit]
-
-        def step(t, state):
-            starts = []
-            for i in range(group):
-                starts += rows_of(stage * 24 + unit, jnp.minimum(group * t + i, n - 1))
-            keys = jnp.concatenate([key_flat[pl.ds(r, rows), :] for r in starts], axis=0)
-            values = jnp.concatenate([value_flat[pl.ds(r, rows), :] for r in starts], axis=0)
-            return update(q, keys, values, (n - group * t) * width, state)
-
-        return lax.fori_loop(0, lax.div(n + (group - 1), group), step, begin(unit))
-
     def main_rows(row, slot):
         return [pl.multiple_of(main_ref[row, slot], BLOCK)]
 
     def ext_rows(row, slot):
         return [pl.multiple_of(ref[row, slot], HALF) for ref in (ext0_ref, ext1_ref)]
 
-    def main_unit(unit, carry):
-        state = run(unit, 2 if last else 4, BLOCK, main_rows, k_flat, v_flat, BLOCK)
-        if not last:
-            keep(unit, state)
+    def run(units, group, rows_of, key_flat, value_flat, rows):
+        width = len(rows_of(0, 0)) * rows
+        ns = [n_ref[stage, unit] for unit in units]
+        most = functools.reduce(jnp.maximum, ns)
+
+        def step(t, carry):
+            col = lax.broadcasted_iota(jnp.int32, (BLOCK, group * width), 1)
+            values, scores = [], []
+            for unit, n in zip(units, ns):
+                starts = []
+                for i in range(group):
+                    slot = jnp.maximum(jnp.minimum(group * t + i, n - 1), 0)
+                    starts += rows_of(stage * 24 + unit, slot)
+                keys = jnp.concatenate([key_flat[pl.ds(r, rows), :] for r in starts], axis=0)
+                values.append(
+                    jnp.concatenate([value_flat[pl.ds(r, rows), :] for r in starts], axis=0)
+                )
+                s = dot_t(q_ref[unit], keys)
+                scores.append(jnp.where(col < (n - group * t) * width, s, 2 * FLOOR))
+            for unit, s, v in zip(units, scores, values):
+                top = top_ref[unit][:, :1]
+                new_top = jnp.maximum(top, jnp.max(s, axis=1, keepdims=True))
+                p = jnp.exp2((s - new_top) * SCALE)
+                alpha = jnp.exp2((top - new_top) * SCALE)
+                part = functools.reduce(
+                    jnp.add, [p[:, i : i + HEAD] for i in range(0, group * width, HEAD)]
+                )
+                product = jnp.dot(p.astype(jnp.bfloat16), v, preferred_element_type=jnp.float32)
+                top_ref[unit] = jnp.broadcast_to(new_top, (BLOCK, HEAD))
+                tot_ref[unit] = tot_ref[unit] * alpha + part
+                acc_ref[unit] = acc_ref[unit] * alpha + product
             return carry
-        top, total, acc = state
-        sb = lax.div(unit, 3)
-        row = pl.multiple_of((unit - 3 * sb) * BLOCK, BLOCK)
-        out_ref[sb, pl.ds(row, BLOCK), :] = (acc / total).astype(jnp.bfloat16)
+
+        lax.fori_loop(0, lax.div(most + (group - 1), group), step, 0)
+
+    def finish(unit):
+        total = jnp.sum(tot_ref[unit], axis=1, keepdims=True)
+        return top_ref[unit][:, :1], total, (acc_ref[unit] / total).astype(jnp.bfloat16)
+
+    def main_units(index, carry):
+        units = [index * MAIN_UNROLL[stage] + i for i in range(MAIN_UNROLL[stage])]
+        run(units, MAIN_GROUP[stage], main_rows, k_flat, v_flat, BLOCK)
+        if last:
+            for unit in units:
+                sb = lax.div(unit, 3)
+                row = pl.multiple_of((unit - 3 * sb) * BLOCK, BLOCK)
+                out_ref[sb, pl.ds(row, BLOCK), :] = finish(unit)[2]
         return carry
 
-    def ext_unit(local, carry):
-        unit = UNITS + local
-        state = run(unit, 4 if last else 8, 2 * HALF, ext_rows, ke_flat, ve_flat, HALF)
-        if not last:
-            keep(unit, state)
-            return carry
-        top, total, acc = state
-        sb = lax.div(local, 3)
-        row = pl.multiple_of((local - 3 * sb) * BLOCK, BLOCK)
-        out_ref[sb, pl.ds(SUPER + row, BLOCK), :] = (acc / total).astype(jnp.bfloat16)
-        level = top * SCALE + jnp.log2(total)
-        level = jnp.sum(jnp.where(eye, level, 0.0), axis=0, keepdims=True)
-        high = level.astype(jnp.bfloat16).astype(jnp.float32)
-        rest = level - high
-        mid = rest.astype(jnp.bfloat16).astype(jnp.float32)
-        low = rest - mid
-        index = lax.broadcasted_iota(jnp.int32, (STATS, HEAD), 0)
-        tile = jnp.where(index == 0, high, jnp.where(index == 1, mid, jnp.where(index == 2, low, 0.0)))
-        at = pl.multiple_of(2 * SUPER + (local - 3 * sb) * STATS, STATS)
-        out_ref[sb, pl.ds(at, STATS), :] = tile.astype(jnp.bfloat16)
+    def ext_units(index, carry):
+        locals_ = [index * EXT_UNROLL[stage] + i for i in range(EXT_UNROLL[stage])]
+        run([UNITS + i for i in locals_], EXT_GROUP[stage], ext_rows, ke_flat, ve_flat, HALF)
+        if last:
+            for local in locals_:
+                top, total, value = finish(UNITS + local)
+                sb = lax.div(local, 3)
+                row = pl.multiple_of((local - 3 * sb) * BLOCK, BLOCK)
+                out_ref[sb, pl.ds(SUPER + row, BLOCK), :] = value
+                level = top * SCALE + jnp.log2(total)
+                level = jnp.sum(jnp.where(eye, level, 0.0), axis=0, keepdims=True)
+                high = level.astype(jnp.bfloat16).astype(jnp.float32)
+                rest = level - high
+                mid = rest.astype(jnp.bfloat16).astype(jnp.float32)
+                low = rest - mid
+                index_ = lax.broadcasted_iota(jnp.int32, (STATS, HEAD), 0)
+                tile = jnp.where(
+                    index_ == 0, high, jnp.where(index_ == 1, mid, jnp.where(index_ == 2, low, 0.0))
+                )
+                at = pl.multiple_of(2 * SUPER + (local - 3 * sb) * STATS, STATS)
+                out_ref[sb, pl.ds(at, STATS), :] = tile.astype(jnp.bfloat16)
         return carry
 
-    lax.fori_loop(0, UNITS, main_unit, 0)
-    lax.fori_loop(0, UNITS, ext_unit, 0)
+    lax.fori_loop(0, UNITS // MAIN_UNROLL[stage], main_units, 0)
+    lax.fori_loop(0, UNITS // EXT_UNROLL[stage], ext_units, 0)
 
 
 def attend(stage, plans, q, state, sources, shapes):
     pieces = 1 + max(piece for parts in shapes for piece, _ in parts)
     copies = sum(len(parts) for parts in shapes)
     kept = jax.ShapeDtypeStruct((2 * UNITS, BLOCK, HEAD), jnp.float32)
+    scratch = [
+        pltpu.VMEM((pieces, 4, CHUNKS, ROWS, HEAD), jnp.bfloat16),
+        pltpu.VMEM((pieces, 4, CHUNKS, ROWS, HEAD), jnp.bfloat16),
+        pltpu.VMEM((pieces, 4, CHUNKS, EXT, HEAD), jnp.bfloat16),
+        pltpu.VMEM((pieces, 4, CHUNKS, EXT, HEAD), jnp.bfloat16),
+        pltpu.SemaphoreType.DMA((copies,)),
+    ]
     if stage == 2:
         out_shape = jax.ShapeDtypeStruct((4, 2 * SUPER + 3 * STATS, HEAD), jnp.bfloat16)
         out_specs = VMEM
+        scratch += [pltpu.VMEM(kept.shape, kept.dtype)] * 3
     else:
-        out_shape, out_specs = (kept, kept), (VMEM, VMEM)
+        out_shape, out_specs = (kept,) * 3, (VMEM,) * 3
     share = pieces / 8
     return pl.pallas_call(
         functools.partial(stage_kernel, stage, shapes),
         out_shape=out_shape,
         in_specs=[SMEM] * 4 + [VMEM] * (1 + len(state)) + [HBM] * len(sources),
         out_specs=out_specs,
-        scratch_shapes=[
-            pltpu.VMEM((pieces, 4, CHUNKS, ROWS, HEAD), jnp.bfloat16),
-            pltpu.VMEM((pieces, 4, CHUNKS, ROWS, HEAD), jnp.bfloat16),
-            pltpu.VMEM((pieces, 4, CHUNKS, EXT, HEAD), jnp.bfloat16),
-            pltpu.VMEM((pieces, 4, CHUNKS, EXT, HEAD), jnp.bfloat16),
-            pltpu.SemaphoreType.DMA((copies,)),
-        ],
+        scratch_shapes=scratch,
         compiler_params=pltpu.CompilerParams(vmem_limit_bytes=32 * 1024 * 1024),
         cost_estimate=pl.CostEstimate(
             flops=int(share * 20e9), bytes_accessed=int(share * 10e6), transcendentals=int(share * 4e6)

time: 214 us -> 196 us (0.916)
  Pallas kernels: 60.6 us -> 46.4 us
  blocking collectives: 57.9 us -> 52.9 us
    pallas_call x3, Pallas kernels: 45.8 us -> 28.4 us  [attend(): pl.pallas_call(functools.partial(stage_kernel, stage, shapes), out_shape=...]
    all_to_all x1, blocking collectives: 23.4 us -> 18.5 us  [per_device(): out = lax.all_to_all(out, ('xh', 'zh'), 0, 0, tiled=True)]
    ppermute x3, waiting for transfers between devices: 7.66 us -> 11.2 us  [ring_up(): return lax.ppermute(x, 'y', [(i, (i + 1) % 4) for i in range(4)])]
    pallas_call x1, Pallas kernels: 14.8 us -> 18 us  [plan(): pl.pallas_call(plan_kernel, out_shape=(lists, lists, lists, jax.ShapeDtyp...]
    ppermute x3, waiting for transfers between devices: 2.68 us -> 0.01 us  [ring_down(): return lax.ppermute(x, 'y', [(i, (i - 1) % 4) for i in range(4)])]
  transfers between devices with their start and end apart: 10 -> 10, of which waited for: 5 -> 4; matrix products, arithmetic and copies ran while one was open for 2% -> 2% of each run, Pallas kernels for 22% -> 20%
where the time goes in v3:
time: 196 us; the launch traced here: 195 us
  waiting for transfers between devices  55 us (28%)
  blocking collectives  52.9 us (27%)
  Pallas kernels  46.4 us (24%)
  between operations  13.8 us (7%)
  starting transfers between devices  9.26 us (5%)
  local copies, waits for them, and re-layouts  8.58 us (4%)
  matrix products  8 us (4%)
    reduce_scatter x1, waiting for transfers between devices, per_device(): lax.psum_scatter(jnp.dot(attended, w_out, preferred_element_type=jnp.floa...  43.1 us
    all_to_all x1, blocking collectives, per_device(): lax.all_to_all(sent, SPREAD, 0, 0, tiled=True)  34.5 us
    pallas_call x3, Pallas kernels, attend(): pl.pallas_call(functools.partial(stage_kernel, stage, shapes), out_shape=...  28.4 us
    all_to_all x1, blocking collectives, per_device(): out = lax.all_to_all(out, ('xh', 'zh'), 0, 0, tiled=True)  18.5 us
    pallas_call x1, Pallas kernels, plan(): pl.pallas_call(plan_kernel, out_shape=(lists, lists, lists, jax.ShapeDtyp...  18 us
    ppermute x3, waiting for transfers between devices, ring_up(): return lax.ppermute(x, 'y', [(i, (i + 1) % 4) for i in range(4)])  11.2 us
    dot_general x1, matrix products, per_device(): jnp.dot(attended, w_out, preferred_element_type=jnp.float32)  8 us
    ppermute x3, starting transfers between devices, ring_down(): return lax.ppermute(x, 'y', [(i, (i - 1) % 4) for i in range(4)])  7.04 us
  transfers between devices with their start and end apart: 10, of which 4 were waited for; matrix products, arithmetic and copies ran while one was open for 2% of the time, Pallas kernels for 20%

profile of v3, /device:TPU:1, one launch (start us, length us, event | category | flops | bytes accessed | tf_op | source)
XLA Modules:
  0.0 195.4 jit_solution(7086255465525757562)
XLA Ops:
  6.5 0.0 reduce-scatter.2.cloned.1.call-start
  6.5 1.4 copy.60
  8.0 0.0 copy-start.6
  8.0 0.0 copy-done.5
  8.0 0.3 copy.48
  8.4 0.5 copy-done.6
  9.0 0.3 copy.50
  9.4 0.2 copy.61
  9.6 0.1 copy.62
  9.8 0.2 copy.49
  10.0 0.1 copy.52
  10.2 0.2 copy.51
  10.4 0.1 copy.56
  10.6 0.6 fusion.6
  11.3 0.1 constant_dynamic-update-slice_fusion.4
  11.3 1.0 maximum_select_fusion
  12.3 0.1 constant_dynamic-update-slice_fusion.1
  12.4 0.1 broadcast_in_dim.9
  12.4 0.1 constant_dynamic-update-slice_fusion
  12.5 34.5 %all_to_all.10 = bf16[16,448,128]{2,1,0:T(8,128)(2,1)S(1)} all-to-all(bf16[16,448,128]{2,1,0:T(8,128)(2,1)S(1)} %constant_dynamic-update-slice_fusion), channel_id=1, replica_groups=mesh['xl'=2,'c'=2,'xh'=2,'zh'=2,'zl'=2,'y'=4] {'xh','zh','xl','c'}, dimensions={0} | all-to-all | bytes 3670016 | tf_op jit(solution)/shard_map/all_to_all | solution.py:310
  47.0 0.1 slice.88.refs_5_
  47.1 2.8 %collective-permute-start.2 = (bf16[4,4,256,128]{3,2,1,0:T(8,128)(2,1)S(1)}, bf16[4,4,256,128]{3,2,1,0:T(8,128)(2,1)S(1)}, u32[]{:S(2)}, u32[]{:S(2)}) collective-permute-start(bf16[4,4,256,128]{3,2,1,0:T(8,128)(2,1)S(1)} %slice.88.refs_5_), channel_id=1, source_target_pairs={{0,3},{1,0},{2,1},{3,2},{4,7},{5,4},{6,5},{7,6},{8,11},{9,8},{10,9... | collective-permute-start | bytes 3145736 | tf_op jit(solution)/shard_map/ppermute | solution.py:42
  49.9 0.0 copy-done.4
  49.9 0.0 collective-permute-start.1
  49.9 0.7 collective-permute-start
  50.6 0.0 copy-done.7
  50.6 1.3 copy.64.table_ref
  51.9 0.7 stack.23.where_ref
  52.5 18.0 %shard_map.64 = (s32[72,16]{1,0:T(8,128)}, s32[72,16]{1,0:T(8,128)}, s32[72,16]{1,0:T(8,128)}, s32[3,24]{1,0:T(4,128)}) custom-call(s32[5]{0:T(128)} %stack.23.where_ref, s32[20,96]{1,0:T(8,128)} %count_ref.1, s32[20,96,16]{2,1,0:T(8,128)} %copy.64.table_ref), custom_call_target="tpu_custom_call" | custom-call | flops 8000000000 | bytes 100000 | tf_op jit(solution)/shard_map/pallas_call | solution.py:106
  70.6 0.0 copy-start
  70.6 0.0 copy-start.1
  70.6 0.0 copy-start.2
  70.6 0.0 copy-start.3
  70.6 1.2 slice.89
  71.8 0.1 copy.63
  71.9 0.0 collective-permute-done.2.refs_8_
  71.9 2.6 %collective-permute-done.1.refs_7_ = bf16[4,4,256,128]{3,2,1,0:T(8,128)(2,1)S(1)} collective-permute-done((bf16[4,4,256,128]{3,2,1,0:T(8,128)(2,1)S(1)}, bf16[4,4,256,128]{3,2,1,0:T(8,128)(2,1)S(1)}, u32[]{:S(2)}, u32[]{:S(2)}) %collective-permute-start.1) | collective-permute-done | bytes 1048608 | tf_op jit(solution)/shard_map/ppermute | solution.py:38
  74.5 0.0 collective-permute-done.refs_6_
  74.5 0.0 collective-permute-start.4
  74.5 2.7 %collective-permute-start.5 = (bf16[4,4,256,128]{3,2,1,0:T(8,128)(2,1)S(1)}, bf16[4,4,256,128]{3,2,1,0:T(8,128)(2,1)S(1)}, u32[]{:S(2)}, u32[]{:S(2)}) collective-permute-start(bf16[4,4,256,128]{3,2,1,0:T(8,128)(2,1)S(1)} %collective-permute-done.2.refs_8_), channel_id=1, source_target_pairs={{0,3},{1,0},{2,1},{3,2},{4,7},{5,4},{6,5},{7,6},{8,11},{9,8},{10,9... | collective-permute-start | bytes 3145736 | tf_op jit(solution)/shard_map/ppermute | solution.py:42
  77.2 0.7 collective-permute-start.3
  77.9 0.0 copy-done
  77.9 0.0 copy-done.1
  77.9 0.0 copy-done.2
  77.9 11.8 %shard_map.65 = (f32[24,128,128]{2,1,0:T(8,128)S(1)}, f32[24,128,128]{2,1,0:T(8,128)S(1)}, f32[24,128,128]{2,1,0:T(8,128)S(1)}) custom-call(s32[72,16]{1,0:T(8,128)S(1)} %copy-done, s32[72,16]{1,0:T(8,128)S(1)} %copy-done.1, s32[72,16]{1,0:T(8,128)S(1)} %copy-done.2, s32[3,24]{1,0:T(4,128)S(1)} %copy-done.3, bf16[24,128,128]{2,1,0:T(8,128)(2,1)S(1)} %bitcast.50, ...), custom_call_target="tpu_custom_call" | custom-call | flops 10000000000 | bytes 5000000 | tf_op jit(solution)/shard_map/pallas_call | solution.py:268
  89.7 8.6 %collective-permute-done.4.refs_9_ = bf16[4,4,256,128]{3,2,1,0:T(8,128)(2,1)S(1)} collective-permute-done((bf16[4,4,256,128]{3,2,1,0:T(8,128)(2,1)}, bf16[4,4,256,128]{3,2,1,0:T(8,128)(2,1)S(1)}, u32[]{:S(2)}, u32[]{:S(2)}) %collective-permute-start.4) | collective-permute-done | bytes 1048608 | tf_op jit(solution)/shard_map/ppermute | solution.py:38
  98.4 0.0 collective-permute-done.5.refs_10_
  98.4 0.7 collective-permute-done.3.refs_8_
  99.2 1.6 collective-permute-start.8
  100.7 0.0 collective-permute-start.7
  100.7 0.7 collective-permute-start.6
  101.5 9.0 %shard_map.66 = (f32[24,128,128]{2,1,0:T(8,128)S(1)}, f32[24,128,128]{2,1,0:T(8,128)S(1)}, f32[24,128,128]{2,1,0:T(8,128)S(1)}) custom-call(s32[72,16]{1,0:T(8,128)S(1)} %copy-done, s32[72,16]{1,0:T(8,128)S(1)} %copy-done.1, s32[72,16]{1,0:T(8,128)S(1)} %copy-done.2, s32[3,24]{1,0:T(4,128)S(1)} %copy-done.3, bf16[24,128,128]{2,1,0:T(8,128)(2,1)S(1)} %bitcast.51, ...), custom_call_target="tpu_custom_call" | custom-call | flops 7500000256 | bytes 3750000 | tf_op jit(solution)/shard_map/pallas_call | solution.py:268
  110.4 0.0 collective-permute-done.8.refs_10_
  110.5 0.0 collective-permute-done.7.refs_9_
  110.5 0.0 collective-permute-done.6.refs_8_
  110.5 7.6 %shard_map.67 = bf16[4,816,128]{2,1,0:T(8,128)(2,1)S(1)} custom-call(s32[72,16]{1,0:T(8,128)S(1)} %copy-done, s32[72,16]{1,0:T(8,128)S(1)} %copy-done.1, s32[72,16]{1,0:T(8,128)S(1)} %copy-done.2, s32[3,24]{1,0:T(4,128)S(1)} %copy-done.3, bf16[24,128,128]{2,1,0:T(8,128)(2,1)S(1)} %bitcast.52, f32[24,128,128]{2,1,0:T(8,128)S(1)} %get-tuple-element.50.refs_5_, ...), custom_call_target="tpu_custom_call" | custom-call | flops 2500000000 | bytes 1250000 | tf_op jit(solution)/shard_map/pallas_call | solution.py:268
  118.1 18.5 %all_to_all.11 = bf16[4,816,128]{2,1,0:T(8,128)(2,1)S(1)} all-to-all(bf16[4,816,128]{2,1,0:T(8,128)(2,1)S(1)} %shard_map.67), channel_id=1, replica_groups=mesh['xl'=2,'c'=2,'xh'=2,'zh'=2,'zl'=2,'y'=4] {'xh','zh'}, dimensions={0} | all-to-all | bytes 1671168 | tf_op jit(solution)/shard_map/all_to_all | solution.py:331
  136.7 0.3 multiply_reduce_fusion
  137.0 0.1 divide_convert_fusion
  137.1 0.1 copy.66
  137.3 0.2 copy.65
  137.5 8.0 %convolution_convert_fusion = bf16[384,5120]{1,0:T(8,128)(2,1)} fusion(bf16[640,5120]{1,0:T(8,128)(2,1)} %param.11, bf16[384,128]{0,1:T(8,128)(2,1)S(1)} %copy.66, bf16[384,512]{0,1:T(8,128)(2,1)S(1)} %bitcast.62), kind=kOutput, calls=%fused_computation | convolution fusion | flops 2519531520 | bytes 10977280 | tf_op jit(solution)/shard_map/dot_general | solution.py:343
  145.5 0.0 reduce-scatter.2.cloned.1.call-update
  145.5 43.1 %reduce-scatter.2.cloned.1.call-done = bf16[96,5120]{1,0:T(8,128)(2,1)} async-done(((bf16[384,5120]{1,0:T(8,128)(2,1)}), bf16[96,5120]{1,0:T(8,128)(2,1)}) %reduce-scatter.2.cloned.1.call-update) | async-done | bytes 983056 | tf_op jit(solution)/shard_map/reduce_scatter | solution.py:342
  (25 shorter events, 0.5 us)
Async XLA Ops:
  6.5 1.5 copy-start.5
  6.5 182.0 %reduce-scatter.2.cloned.1.call-start = ((), (), s32[]{:S(2)}) async-start(), calls=%async_computation.3 | async-start | bytes 4915200 | tf_op jit(solution)/shard_map/reduce_scatter | solution.py:342
  8.0 1.0 copy-start.6
  47.0 2.9 %copy-start.4 = (bf16[16,448,128]{2,1,0:T(8,128)(2,1)}, bf16[16,448,128]{2,1,0:T(8,128)(2,1)S(1)}, u32[]{:S(2)}) copy-start(bf16[16,448,128]{2,1,0:T(8,128)(2,1)S(1)} %all_to_all.10) | copy-start | bytes 5505028
  47.0 3.6 %copy-start.7 = (s32[20,96,16]{1,2,0:T(8,128)S(1)}, s32[20,96,16]{1,2,0:T(8,128)}, u32[]{:S(2)}) copy-start(s32[20,96,16]{1,2,0:T(8,128)} %param.9) | copy-start | bytes 368644
  47.1 24.8 %collective-permute-start.2 = (bf16[4,4,256,128]{3,2,1,0:T(8,128)(2,1)S(1)}, bf16[4,4,256,128]{3,2,1,0:T(8,128)(2,1)S(1)}, u32[]{:S(2)}, u32[]{:S(2)}) collective-permute-start(bf16[4,4,256,128]{3,2,1,0:T(8,128)(2,1)S(1)} %slice.88.refs_5_), channel_id=1, source_target_pairs={{0,3},{1,0},{2,1},{3,2},{4,7},{5,4},{6,5},{7,6},{8,11},{9,8},{10,9... | collective-permute-start | bytes 3145736 | tf_op jit(solution)/shard_map/ppermute | solution.py:42
  49.9 24.6 %collective-permute-start.1 = (bf16[4,4,256,128]{3,2,1,0:T(8,128)(2,1)S(1)}, bf16[4,4,256,128]{3,2,1,0:T(8,128)(2,1)S(1)}, u32[]{:S(2)}, u32[]{:S(2)}) collective-permute-start(bf16[4,4,256,128]{3,2,1,0:T(8,128)(2,1)S(1)} %slice.88.refs_5_), channel_id=1, source_target_pairs={{0,1},{1,2},{2,3},{3,0},{4,5},{5,6},{6,7},{7,4},{8,9},{9,10},{10,1... | collective-permute-start | bytes 3145736 | tf_op jit(solution)/shard_map/ppermute | solution.py:38
  49.9 24.6 %collective-permute-start = (bf16[4,4,256,128]{3,2,1,0:T(8,128)(2,1)S(1)}, bf16[4,4,256,128]{3,2,1,0:T(8,128)(2,1)}, u32[]{:S(2)}, u32[]{:S(2)}) collective-permute-start(bf16[4,4,256,128]{3,2,1,0:T(8,128)(2,1)S(1)} %slice.88.refs_5_), channel_id=1, source_target_pairs={{0,4},{4,0},{1,5},{5,1},{2,6},{6,2},{3,7},{7,3},{8,12},{12,8},{9,1... | collective-permute-start | bytes 3145736 | tf_op jit(solution)/shard_map/ppermute | solution.py:46
  70.6 7.3 %copy-start = (s32[72,16]{1,0:T(8,128)S(1)}, s32[72,16]{1,0:T(8,128)}, u32[]{:S(2)}) copy-start(s32[72,16]{1,0:T(8,128)} %get-tuple-element.33.refs_0_) | copy-start | bytes 13828
  70.6 7.3 %copy-start.1 = (s32[72,16]{1,0:T(8,128)S(1)}, s32[72,16]{1,0:T(8,128)}, u32[]{:S(2)}) copy-start(s32[72,16]{1,0:T(8,128)} %get-tuple-element.34.refs_1_) | copy-start | bytes 13828
  70.6 7.3 %copy-start.2 = (s32[72,16]{1,0:T(8,128)S(1)}, s32[72,16]{1,0:T(8,128)}, u32[]{:S(2)}) copy-start(s32[72,16]{1,0:T(8,128)} %get-tuple-element.35.refs_2_) | copy-start | bytes 13828
  70.6 7.3 %copy-start.3 = (s32[3,24]{1,0:T(4,128)S(1)}, s32[3,24]{1,0:T(4,128)}, u32[]{:S(2)}) copy-start(s32[3,24]{1,0:T(4,128)} %get-tuple-element.36.refs_3_) | copy-start | bytes 868
  74.5 23.9 %collective-permute-start.4 = (bf16[4,4,256,128]{3,2,1,0:T(8,128)(2,1)}, bf16[4,4,256,128]{3,2,1,0:T(8,128)(2,1)S(1)}, u32[]{:S(2)}, u32[]{:S(2)}) collective-permute-start(bf16[4,4,256,128]{3,2,1,0:T(8,128)(2,1)} %collective-permute-done.refs_6_), channel_id=1, source_target_pairs={{0,1},{1,2},{2,3},{3,0},{4,5},{5,6},{6,7},{7,4},{8,9},{9,10},{10,1... | collective-permute-start | bytes 3145736 | tf_op jit(solution)/shard_map/ppermute | solution.py:38
  74.5 23.9 %collective-permute-start.5 = (bf16[4,4,256,128]{3,2,1,0:T(8,128)(2,1)S(1)}, bf16[4,4,256,128]{3,2,1,0:T(8,128)(2,1)S(1)}, u32[]{:S(2)}, u32[]{:S(2)}) collective-permute-start(bf16[4,4,256,128]{3,2,1,0:T(8,128)(2,1)S(1)} %collective-permute-done.2.refs_8_), channel_id=1, source_target_pairs={{0,3},{1,0},{2,1},{3,2},{4,7},{5,4},{6,5},{7,6},{8,11},{9,8},{10,9... | collective-permute-start | bytes 3145736 | tf_op jit(solution)/shard_map/ppermute | solution.py:42
  77.2 21.9 %collective-permute-start.3 = (bf16[4,4,256,128]{3,2,1,0:T(8,128)(2,1)S(1)}, bf16[4,4,256,128]{3,2,1,0:T(8,128)(2,1)S(1)}, u32[]{:S(2)}, u32[]{:S(2)}) collective-permute-start(bf16[4,4,256,128]{3,2,1,0:T(8,128)(2,1)S(1)} %collective-permute-done.2.refs_8_), channel_id=1, source_target_pairs={{0,4},{4,0},{1,5},{5,1},{2,6},{6,2},{3,7},{7,3},{8,12},{12,8},{9,1... | collective-permute-start | bytes 3145736 | tf_op jit(solution)/shard_map/ppermute | solution.py:46
  99.2 11.3 %collective-permute-start.8 = (bf16[4,4,64,128]{3,2,1,0:T(8,128)(2,1)S(1)}, bf16[4,4,64,128]{3,2,1,0:T(8,128)(2,1)S(1)}, u32[]{:S(2)}, u32[]{:S(2)}) collective-permute-start(bf16[4,4,64,128]{3,2,1,0:T(8,128)(2,1)S(1)} %slice.73), channel_id=1, source_target_pairs={{0,3},{1,0},{2,1},{3,2},{4,7},{5,4},{6,5},{7,6},{8,11},{9,8},{10,9... | collective-permute-start | bytes 786440 | tf_op jit(solution)/shard_map/ppermute | solution.py:42
  100.7 9.7 %collective-permute-start.7 = (bf16[4,4,96,128]{3,2,1,0:T(8,128)(2,1)S(1)}, bf16[4,4,96,128]{3,2,1,0:T(8,128)(2,1)S(1)}, u32[]{:S(2)}, u32[]{:S(2)}) collective-permute-start(bf16[4,4,96,128]{3,2,1,0:T(8,128)(2,1)S(1)} %slice.72), channel_id=1, source_target_pairs={{0,1},{1,2},{2,3},{3,0},{4,5},{5,6},{6,7},{7,4},{8,9},{9,10},{10,1... | collective-permute-start | bytes 1179656 | tf_op jit(solution)/shard_map/ppermute | solution.py:38
  100.7 9.7 %collective-permute-start.6 = (bf16[4,4,96,128]{3,2,1,0:T(8,128)(2,1)S(1)}, bf16[4,4,96,128]{3,2,1,0:T(8,128)(2,1)S(1)}, u32[]{:S(2)}, u32[]{:S(2)}) collective-permute-start(bf16[4,4,96,128]{3,2,1,0:T(8,128)(2,1)S(1)} %slice.71), channel_id=1, source_target_pairs={{0,4},{4,0},{1,5},{5,1},{2,6},{6,2},{3,7},{7,3},{8,12},{12,8},{9,1... | collective-permute-start | bytes 1179656 | tf_op jit(solution)/shard_map/ppermute | solution.py:46
Sparse Core Ops, SparseCore 0:
  145.6 42.8 reduce-scatter.1

commit v4 on v3

--- a/solution.py
+++ b/solution.py
@@ -23,11 +23,10 @@
 SIZES = (2, 2, 2, 2, 2, 4)
 SPREAD = ("xh", "zh", "xl", "c")
 STATS = 16
+WIDTH = 1280
 UNITS = 12
 SLOTS = 16
-MAIN_UNROLL = (12, 12, 12)
 MAIN_GROUP = (2, 2, 2)
-EXT_UNROLL = (12, 12, 12)
 EXT_GROUP = (4, 4, 4)
 SMEM = pl.BlockSpec(memory_space=pltpu.SMEM)
 VMEM = pl.BlockSpec(memory_space=pltpu.VMEM)
@@ -115,8 +114,9 @@
 
 def stage_kernel(stage, shapes, *refs):
     first, last = stage == 0, stage == 2
-    main_ref, ext0_ref, ext1_ref, n_ref, q_ref = refs[:5]
-    refs = refs[5:]
+    where_ref, main_ref, ext0_ref, ext1_ref, n_ref, q_ref = refs[:6]
+    refs = refs[6:]
+    xl = where_ref[5]
     if not first:
         before = refs[:3]
         refs = refs[3:]
@@ -210,44 +210,43 @@
         total = jnp.sum(tot_ref[unit], axis=1, keepdims=True)
         return top_ref[unit][:, :1], total, (acc_ref[unit] / total).astype(jnp.bfloat16)
 
-    def main_units(index, carry):
-        units = [index * MAIN_UNROLL[stage] + i for i in range(MAIN_UNROLL[stage])]
-        run(units, MAIN_GROUP[stage], main_rows, k_flat, v_flat, BLOCK)
-        if last:
-            for unit in units:
-                sb = lax.div(unit, 3)
-                row = pl.multiple_of((unit - 3 * sb) * BLOCK, BLOCK)
-                out_ref[sb, pl.ds(row, BLOCK), :] = finish(unit)[2]
-        return carry
-
-    def ext_units(index, carry):
-        locals_ = [index * EXT_UNROLL[stage] + i for i in range(EXT_UNROLL[stage])]
-        run([UNITS + i for i in locals_], EXT_GROUP[stage], ext_rows, ke_flat, ve_flat, HALF)
-        if last:
-            for local in locals_:
-                top, total, value = finish(UNITS + local)
-                sb = lax.div(local, 3)
-                row = pl.multiple_of((local - 3 * sb) * BLOCK, BLOCK)
-                out_ref[sb, pl.ds(SUPER + row, BLOCK), :] = value
-                level = top * SCALE + jnp.log2(total)
-                level = jnp.sum(jnp.where(eye, level, 0.0), axis=0, keepdims=True)
-                high = level.astype(jnp.bfloat16).astype(jnp.float32)
-                rest = level - high
-                mid = rest.astype(jnp.bfloat16).astype(jnp.float32)
-                low = rest - mid
-                index_ = lax.broadcasted_iota(jnp.int32, (STATS, HEAD), 0)
-                tile = jnp.where(
-                    index_ == 0, high, jnp.where(index_ == 1, mid, jnp.where(index_ == 2, low, 0.0))
-                )
-                at = pl.multiple_of(2 * SUPER + (local - 3 * sb) * STATS, STATS)
-                out_ref[sb, pl.ds(at, STATS), :] = tile.astype(jnp.bfloat16)
-        return carry
-
-    lax.fori_loop(0, UNITS // MAIN_UNROLL[stage], main_units, 0)
-    lax.fori_loop(0, UNITS // EXT_UNROLL[stage], ext_units, 0)
-
-
-def attend(stage, plans, q, state, sources, shapes):
+    def store(sb, r, top, value):
+        for i in range(4):
+            granule = 4 * r + i
+            chunk = granule // 3
+            to = sb if chunk in (0, 3) else jnp.where(xl == 2 - chunk, sb ^ 2, sb)
+            place = lax.rem(chunk + 4 - 2 * xl, 4)
+            row = pl.multiple_of(top + place * ROWS + (granule % 3) * 32, 32)
+            out_ref[to, pl.ds(row, 32), :] = value[32 * i : 32 * i + 32]
+
+    units = list(range(UNITS))
+    run(units, MAIN_GROUP[stage], main_rows, k_flat, v_flat, BLOCK)
+    if last:
+        for unit in units:
+            store(unit // 3, unit % 3, 0, finish(unit)[2])
+    run([UNITS + unit for unit in units], EXT_GROUP[stage], ext_rows, ke_flat, ve_flat, HALF)
+    if last:
+        levels = []
+        for unit in units:
+            top, total, value = finish(UNITS + unit)
+            store(unit // 3, unit % 3, SUPER, value)
+            level = top * SCALE + jnp.log2(total)
+            levels.append(jnp.sum(jnp.where(eye, level, 0.0), axis=0, keepdims=True))
+        index = lax.broadcasted_iota(jnp.int32, (STATS, HEAD), 0)
+        column = lax.broadcasted_iota(jnp.int32, (1, HEAD), 1)
+        for unit in units:
+            sb, r = unit // 3, unit % 3
+            chunk = (r * BLOCK + column) // ROWS
+            level = jnp.where(chunk == 2 - xl, levels[3 * (sb ^ 2) + r], levels[unit])
+            high = level.astype(jnp.bfloat16).astype(jnp.float32)
+            rest = level - high
+            mid = rest.astype(jnp.bfloat16).astype(jnp.float32)
+            low = rest - mid
+            tile = jnp.where(index == 0, high, jnp.where(index == 1, mid, jnp.where(index == 2, low, 0.0)))
+            out_ref[sb, pl.ds(2 * SUPER + r * STATS, STATS), :] = tile.astype(jnp.bfloat16)
+
+
+def attend(stage, where, plans, q, state, sources, shapes):
     pieces = 1 + max(piece for parts in shapes for piece, _ in parts)
     copies = sum(len(parts) for parts in shapes)
     kept = jax.ShapeDtypeStruct((2 * UNITS, BLOCK, HEAD), jnp.float32)
@@ -268,14 +267,58 @@
     return pl.pallas_call(
         functools.partial(stage_kernel, stage, shapes),
         out_shape=out_shape,
-        in_specs=[SMEM] * 4 + [VMEM] * (1 + len(state)) + [HBM] * len(sources),
+        in_specs=[SMEM] * 5 + [VMEM] * (1 + len(state)) + [HBM] * len(sources),
         out_specs=out_specs,
         scratch_shapes=scratch,
         compiler_params=pltpu.CompilerParams(vmem_limit_bytes=32 * 1024 * 1024),
         cost_estimate=pl.CostEstimate(
             flops=int(share * 20e9), bytes_accessed=int(share * 10e6), transcendentals=int(share * 4e6)
         ),
-    )(*plans, q, *state, *sources)
+    )(where, *plans, q, *state, *sources)
+
+
+def around(x, step):
+    index = lambda at: (at % 2) * 2 + at % 4 // 2
+    return lax.ppermute(x, ("xl", "xh"), [(index(i), index(i + step)) for i in range(4)])
+
+
+def project_kernel(parts, rows_ref, w_ref, *outs):
+    for (chunk, lo, count), out in zip(parts, outs):
+        rows = rows_ref[pl.ds(lo, count), :]
+        for at in range(0, WIDTH, 256):
+            product = jnp.dot(
+                rows, w_ref[:, pl.ds(chunk * WIDTH + at, 256)], preferred_element_type=jnp.float32
+            )
+            out[:, pl.ds(at, 256)] = product.astype(out.dtype)
+
+
+def project_parts(rows, w, parts):
+    return pl.pallas_call(
+        functools.partial(project_kernel, parts),
+        out_shape=tuple(
+            jax.ShapeDtypeStruct((count, WIDTH), jnp.float32 if lo == 0 else jnp.bfloat16)
+            for _, lo, count in parts
+        ),
+        in_specs=[VMEM, VMEM],
+        out_specs=(VMEM,) * len(parts),
+        compiler_params=pltpu.CompilerParams(vmem_limit_bytes=24 * 1024 * 1024),
+        cost_estimate=pl.CostEstimate(
+            flops=sum(2 * count * WIDTH * 640 for _, _, count in parts),
+            bytes_accessed=4_000_000,
+            transcendentals=0,
+        ),
+    )(rows, w)
+
+
+def project(rows, w):
+    chunks = w.shape[1] // WIDTH
+    sides = lambda k: [(k, 2 * ROWS, ROWS), (k, 3 * ROWS, ROWS)]
+    own = lambda k: [(k, 0, 2 * ROWS)]
+    first = project_parts(rows, w, sides(0))
+    rest = project_parts(rows, w, sum([sides(k) for k in range(1, chunks)], []))
+    owns = project_parts(rows, w, sum([own(k) for k in range(chunks)], []))
+    sent = first + rest
+    return sent[0::2], sent[1::2], owns
 
 
 def to_groups(main):
@@ -310,7 +353,7 @@
     got = lax.all_to_all(sent, SPREAD, 0, 0, tiled=True).reshape(4, CHUNKS, KV + 2 * ROWS, HEAD)
     kv = got[:, :, :KV]
 
-    where = jnp.stack([y, zl, 5 * u + group, 5 * u + 4, group]).astype(jnp.int32)
+    where = jnp.stack([y, zl, 5 * u + group, 5 * u + 4, group, xl]).astype(jnp.int32)
     plans = plan(where, block_count, block_list)
     q = got[:, :, KV:].reshape(4, CHUNKS, 2, ROWS, HEAD)
     q = q.transpose(2, 0, 1, 3, 4).reshape(2 * UNITS, BLOCK, HEAD)
@@ -319,32 +362,36 @@
     a01, am0, ap0, q, plans = lax.optimization_barrier((a01, am0, ap0, q, plans))
     a11, am1, a20 = swap(ap0), ring_up(a01), ring_down(ap0)
     whole = lambda piece: tuple((piece, name) for name in "kvab")
-    state = attend(0, plans, q, (), (kv, a01, am0, ap0), tuple(whole(i) for i in range(4)))
+    state = attend(0, where, plans, q, (), (kv, a01, am0, ap0), tuple(whole(i) for i in range(4)))
     a11, am1, a20, state = lax.optimization_barrier((a11, am1, a20, state))
     last_k = swap(a20[:, :, :ROWS])
     last_v = ring_up(am1[:, :, ROWS : 2 * ROWS])
     last_e = ring_down(a11[:, :, 2 * ROWS :])
-    state = attend(1, plans, q, state, (a11, am1, a20), tuple(whole(i) for i in range(3)))
+    state = attend(1, where, plans, q, state, (a11, am1, a20), tuple(whole(i) for i in range(3)))
     out = attend(
-        2, plans, q, state, (last_k, last_v, last_e), (((0, "k"),), ((0, "v"),), ((0, "a"), (0, "b")))
+        2, where, plans, q, state, (last_k, last_v, last_e), (((0, "k"),), ((0, "v"),), ((0, "a"), (0, "b")))
     )
     out = lax.all_to_all(out, ("xh", "zh"), 0, 0, tiled=True)
 
     heads = out[:, :SUPER]
     shares = out[:, SUPER : 2 * SUPER].astype(jnp.float32)
     level = out[:, 2 * SUPER :].reshape(4, 3, STATS, BLOCK)[:, :, :3].astype(jnp.float32)
-    level = jnp.sum(level, axis=2).reshape(4, SUPER, 1)
+    level = jnp.sum(level, axis=2).reshape(4, SUPER)
+    level = jnp.where(xl == 0, level, jnp.roll(level, 2 * ROWS, axis=1))[:, :, None]
     weight = jnp.exp2(level - jnp.max(level, axis=0, keepdims=True))
     shared = jnp.sum(shares * weight, axis=0) / jnp.sum(weight, axis=0)
     attended = jnp.concatenate(
         [heads.transpose(1, 0, 2).reshape(SUPER, 4 * HEAD), shared.astype(jnp.bfloat16)], axis=1
     )
-    return lax.psum_scatter(
-        jnp.dot(attended, w_out, preferred_element_type=jnp.float32).astype(jnp.bfloat16),
-        ("xl", "c"),
-        scatter_dimension=0,
-        tiled=True,
-    )
+    lows, highs, owns = project(attended, w_out)
+    total = []
+    for low, high, own in zip(lows, highs, owns):
+        first = own[:ROWS] + around(low, -1).astype(jnp.float32)
+        second = own[ROWS:] + around(high, 1).astype(jnp.float32)
+        keep = jnp.where(c == 0, first, second)
+        give = jnp.where(c == 0, second, first).astype(jnp.bfloat16)
+        total.append((keep + lax.ppermute(give, "c", [(0, 1), (1, 0)])).astype(jnp.bfloat16))
+    return jnp.concatenate(total, axis=1)
 
 
 def solution(mesh):

time: 196 us -> 174 us (0.89)
  starting transfers between devices: 9.26 us -> 35.3 us
  blocking collectives: 52.9 us -> 34.5 us
  between operations: 13.8 us -> 0.5 us
  waiting for transfers between devices: 55 us -> 43 us
  matrix products: 8 us -> 0 us
  local copies, waits for them, and re-layouts: 8.58 us -> 11.1 us
  Pallas kernels: 46.4 us -> 44.1 us
  other arithmetic: 1.42 us -> 3.58 us
    reduce_scatter x1 -> x0, waiting for transfers between devices: 43.1 us -> none  [per_device(): lax.psum_scatter(jnp.dot(attended, w_out, preferred_element_type=jnp.floa...]
    all_to_all x1 -> x0, blocking collectives: 18.5 us -> none  [per_device(): out = lax.all_to_all(out, ('xh', 'zh'), 0, 0, tiled=True)]
    ppermute x0 -> x12, starting transfers between devices: none -> 17.8 us  [the longest x8 12.2 us: around(): lax.ppermute(x, ('xl', 'xh'), [(index(i), index(i + step)) for i in range...]
    ppermute x0 -> x12, waiting for transfers between devices: none -> 16.2 us  [the longest x8 15.1 us: around(): lax.ppermute(x, ('xl', 'xh'), [(index(i), index(i + step)) for i in range...]
    all_to_all x0 -> x1, waiting for transfers between devices: none -> 9.59 us  [per_device(): out = lax.all_to_all(out, ('xh', 'zh'), 0, 0, tiled=True)]
    all_to_all x0 -> x1, starting transfers between devices: none -> 8.22 us  [per_device(): out = lax.all_to_all(out, ('xh', 'zh'), 0, 0, tiled=True)]
    dot_general x1 -> x0, matrix products: 8 us -> none  [per_device(): jnp.dot(attended, w_out, preferred_element_type=jnp.float32)]
    pallas_call x0 -> x3, Pallas kernels: none -> 4.25 us  [project_parts(): pl.pallas_call(functools.partial(project_kernel, parts), out_shape=tuple(...]
  transfers between devices with their start and end apart: 10 -> 22, of which waited for: 4 -> 9; matrix products, arithmetic and copies ran while one was open for 2% -> 2% of each run, Pallas kernels for 20% -> 20%
where the time goes in v4:
time: 174 us; the launch traced here: 172 us
  Pallas kernels  44.1 us (25%)
  waiting for transfers between devices  43 us (25%)
  starting transfers between devices  35.3 us (20%)
  blocking collectives  34.5 us (20%)
  local copies, waits for them, and re-layouts  11.1 us (6%)
  other arithmetic  3.58 us (2%)
    all_to_all x1, blocking collectives, per_device(): lax.all_to_all(sent, SPREAD, 0, 0, tiled=True)  34.5 us
    pallas_call x3, Pallas kernels, attend(): pl.pallas_call(functools.partial(stage_kernel, stage, shapes), out_shape=...  25.1 us
    ppermute x8, waiting for transfers between devices, around(): lax.ppermute(x, ('xl', 'xh'), [(index(i), index(i + step)) for i in range...  15.1 us
    pallas_call x1, Pallas kernels, plan(): pl.pallas_call(plan_kernel, out_shape=(lists, lists, lists, jax.ShapeDtyp...  14.8 us
    ppermute x3, waiting for transfers between devices, ring_up(): return lax.ppermute(x, 'y', [(i, (i + 1) % 4) for i in range(4)])  13.8 us
    ppermute x8, starting transfers between devices, around(): lax.ppermute(x, ('xl', 'xh'), [(index(i), index(i + step)) for i in range...  12.2 us
    all_to_all x1, waiting for transfers between devices, per_device(): out = lax.all_to_all(out, ('xh', 'zh'), 0, 0, tiled=True)  9.59 us
    all_to_all x1, starting transfers between devices, per_device(): out = lax.all_to_all(out, ('xh', 'zh'), 0, 0, tiled=True)  8.22 us
  transfers between devices with their start and end apart: 22, of which 9 were waited for; matrix products, arithmetic and copies ran while one was open for 2% of the time, Pallas kernels for 20%

profile of v4, /device:TPU:1, one launch (start us, length us, event | category | flops | bytes accessed | tf_op | source)
XLA Modules:
  0.0 172.2 jit_solution(2368184733561275617)
XLA Ops:
  0.0 1.4 copy.61
  1.5 0.3 copy.49
  1.9 0.5 copy-done.8
  2.5 0.3 copy.51
  2.9 0.2 copy.62
  3.1 0.1 copy.63
  3.2 0.2 copy.50
  3.5 0.1 copy.53
  3.6 0.2 copy.52
  3.9 0.1 copy.57
  4.0 0.7 fusion.4
  4.8 1.0 maximum_select_fusion
  6.0 34.5 %all_to_all.10 = bf16[16,448,128]{2,1,0:T(8,128)(2,1)S(1)} all-to-all(bf16[16,448,128]{2,1,0:T(8,128)(2,1)S(1)} %constant_dynamic-update-slice_fusion), channel_id=1, replica_groups=mesh['xl'=2,'c'=2,'xh'=2,'zh'=2,'zl'=2,'y'=4] {'xh','zh','xl','c'}, dimensions={0} | all-to-all | bytes 3670016 | tf_op jit(solution)/shard_map/all_to_all | solution.py:353
  40.5 2.8 %collective-permute-start.2 = (bf16[4,4,256,128]{3,2,1,0:T(8,128)(2,1)S(1)}, bf16[4,4,256,128]{3,2,1,0:T(8,128)(2,1)S(1)}, u32[]{:S(2)}, u32[]{:S(2)}) collective-permute-start(bf16[4,4,256,128]{3,2,1,0:T(8,128)(2,1)S(1)} %slice.130.refs_6_), channel_id=1, source_target_pairs={{0,3},{1,0},{2,1},{3,2},{4,7},{5,4},{6,5},{7,6},{8,11},{9,8},{10,9... | collective-permute-start | bytes 3145736 | tf_op jit(solution)/shard_map/ppermute | solution.py:41
  43.3 0.7 collective-permute-start
  44.1 1.3 copy.65.table_ref
  45.3 0.6 stack.27.where_ref.refs_0_
  46.0 14.8 %shard_map.64 = (s32[72,16]{1,0:T(8,128)}, s32[72,16]{1,0:T(8,128)}, s32[72,16]{1,0:T(8,128)}, s32[3,24]{1,0:T(4,128)}) custom-call(s32[6]{0:T(128)} %stack.27.where_ref.refs_0_, s32[20,96]{1,0:T(8,128)} %count_ref.1, s32[20,96,16]{2,1,0:T(8,128)} %copy.65.table_ref), custom_call_target="tpu_custom_call" | custom-call | flops 8000000000 | bytes 100000 | tf_op jit(solution)/shard_map/pallas_call | solution.py:105
  60.8 1.2 slice.131
  62.0 2.8 %collective-permute-done.2.refs_9_ = bf16[4,4,256,128]{3,2,1,0:T(8,128)(2,1)S(1)} collective-permute-done((bf16[4,4,256,128]{3,2,1,0:T(8,128)(2,1)S(1)}, bf16[4,4,256,128]{3,2,1,0:T(8,128)(2,1)S(1)}, u32[]{:S(2)}, u32[]{:S(2)}) %collective-permute-start.2) | collective-permute-done | bytes 1048608 | tf_op jit(solution)/shard_map/ppermute | solution.py:41
  64.8 3.1 %collective-permute-done.1.refs_8_ = bf16[4,4,256,128]{3,2,1,0:T(8,128)(2,1)S(1)} collective-permute-done((bf16[4,4,256,128]{3,2,1,0:T(8,128)(2,1)S(1)}, bf16[4,4,256,128]{3,2,1,0:T(8,128)(2,1)S(1)}, u32[]{:S(2)}, u32[]{:S(2)}) %collective-permute-start.1) | collective-permute-done | bytes 1048608 | tf_op jit(solution)/shard_map/ppermute | solution.py:37
  67.9 2.7 %collective-permute-start.5 = (bf16[4,4,256,128]{3,2,1,0:T(8,128)(2,1)S(1)}, bf16[4,4,256,128]{3,2,1,0:T(8,128)(2,1)S(1)}, u32[]{:S(2)}, u32[]{:S(2)}) collective-permute-start(bf16[4,4,256,128]{3,2,1,0:T(8,128)(2,1)S(1)} %collective-permute-done.2.refs_9_), channel_id=1, source_target_pairs={{0,3},{1,0},{2,1},{3,2},{4,7},{5,4},{6,5},{7,6},{8,11},{9,8},{10,9... | collective-permute-start | bytes 3145736 | tf_op jit(solution)/shard_map/ppermute | solution.py:41
  70.6 0.7 collective-permute-start.3
  71.4 9.8 %shard_map.65 = (f32[24,128,128]{2,1,0:T(8,128)S(1)}, f32[24,128,128]{2,1,0:T(8,128)S(1)}, f32[24,128,128]{2,1,0:T(8,128)S(1)}) custom-call(s32[6]{0:T(128)S(1)} %copy-done.1, s32[72,16]{1,0:T(8,128)S(1)} %copy-done.2, s32[72,16]{1,0:T(8,128)S(1)} %copy-done.3, s32[72,16]{1,0:T(8,128)S(1)} %copy-done.4, s32[3,24]{1,0:T(4,128)S(1)} %copy-done.5, ...), custom_call_target="tpu_custom_call" | custom-call | flops 10000000000 | bytes 5000000 | tf_op jit(solution)/shard_map/pallas_call | solution.py:267
  81.1 10.7 %collective-permute-done.4.refs_10_ = bf16[4,4,256,128]{3,2,1,0:T(8,128)(2,1)S(1)} collective-permute-done((bf16[4,4,256,128]{3,2,1,0:T(8,128)(2,1)}, bf16[4,4,256,128]{3,2,1,0:T(8,128)(2,1)S(1)}, u32[]{:S(2)}, u32[]{:S(2)}) %collective-permute-start.4) | collective-permute-done | bytes 1048608 | tf_op jit(solution)/shard_map/ppermute | solution.py:37
  91.8 0.7 collective-permute-done.3.refs_9_
  92.6 1.6 collective-permute-start.8
  94.2 0.7 collective-permute-start.6
  94.9 8.0 %shard_map.66 = (f32[24,128,128]{2,1,0:T(8,128)S(1)}, f32[24,128,128]{2,1,0:T(8,128)S(1)}, f32[24,128,128]{2,1,0:T(8,128)S(1)}) custom-call(s32[6]{0:T(128)S(1)} %copy-done.1, s32[72,16]{1,0:T(8,128)S(1)} %copy-done.2, s32[72,16]{1,0:T(8,128)S(1)} %copy-done.3, s32[72,16]{1,0:T(8,128)S(1)} %copy-done.4, s32[3,24]{1,0:T(4,128)S(1)} %copy-done.5, ...), custom_call_target="tpu_custom_call" | custom-call | flops 7500000256 | bytes 3750000 | tf_op jit(solution)/shard_map/pallas_call | solution.py:267
  103.0 7.4 %shard_map.67 = bf16[4,816,128]{2,1,0:T(8,128)(2,1)} custom-call(s32[6]{0:T(128)S(1)} %copy-done.1, s32[72,16]{1,0:T(8,128)S(1)} %copy-done.2, s32[72,16]{1,0:T(8,128)S(1)} %copy-done.3, s32[72,16]{1,0:T(8,128)S(1)} %copy-done.4, s32[3,24]{1,0:T(4,128)S(1)} %copy-done.5, bf16[24,128,128]{2,1,0:T(8,128)(2,1)S(1)} %bitcast.56, ...), custom_call_target="tpu_custom_call" | custom-call | flops 2500000000 | bytes 1250000 | tf_op jit(solution)/shard_map/pallas_call | solution.py:267
  110.4 8.2 %all-to-all-start.1 = ((bf16[4,816,128]{2,1,0:T(8,128)(2,1)}), bf16[4,816,128]{2,1,0:T(8,128)(2,1)S(1)}, u32[]{:S(2)}, u32[]{:S(2)}) async-start(bf16[4,816,128]{2,1,0:T(8,128)(2,1)} %shard_map.67), calls=%async_computation.1 | async-start | bytes 1671168 | tf_op jit(solution)/shard_map/all_to_all | solution.py:374
  118.6 9.6 %all-to-all-done.1 = bf16[4,816,128]{2,1,0:T(8,128)(2,1)S(1)} async-done(((bf16[4,816,128]{2,1,0:T(8,128)(2,1)}), bf16[4,816,128]{2,1,0:T(8,128)(2,1)S(1)}, u32[]{:S(2)}, u32[]{:S(2)}) %all-to-all-start.1) | async-done | bytes 835616 | tf_op jit(solution)/shard_map/all_to_all | solution.py:374
  128.2 0.1 slice_bitcast_fusion.5
  128.3 0.1 fusion.3
  128.4 0.1 exponential_reduce_fusion
  128.5 0.1 fusion.2
  128.6 0.3 multiply_reduce_fusion
  128.9 0.1 divide_convert_fusion
  129.1 2.9 %copy-done = bf16[640,5120]{1,0:T(8,128)(2,1)S(1)} copy-done((bf16[640,5120]{1,0:T(8,128)(2,1)S(1)}, bf16[640,5120]{1,0:T(8,128)(2,1)}, u32[]{:S(2)}) %copy-start) | copy-done | bytes 6553624
  131.9 1.8 %shard_map.70 = (bf16[96,1280]{1,0:T(8,128)(2,1)S(1)}, bf16[96,1280]{1,0:T(8,128)(2,1)S(1)}, bf16[96,1280]{1,0:T(8,128)(2,1)S(1)}, bf16[96,1280]{1,0:T(8,128)(2,...) custom-call(bf16[384,640]{1,0:T(8,128)(2,1)S(1)} %pad_maximum_fusion.1.rows_ref, ...), custom_call_target="tpu_custom_call" | custom-call | flops 943718400 | bytes 4000000 | tf_op jit(solution)/shard_map/pallas_call | solution.py:296
  133.8 5.2 %collective-permute-start.18 = (bf16[96,1280]{1,0:T(8,128)(2,1)S(1)}, bf16[96,1280]{1,0:T(8,128)(2,1)S(1)}, u32[]{:S(2)}, u32[]{:S(2)}) collective-permute-start(bf16[96,1280]{1,0:T(8,128)(2,1)S(1)} %get-tuple-element.75), channel_id=1, source_target_pairs={{0,80},{64,0},{16,64},{80,16},{1,81},{65,1},{17,65},{81,17},{2,82}... | collective-permute-start | bytes 737288 | tf_op jit(solution)/shard_map/ppermute | solution.py:282
  139.0 0.7 shard_map.69
  139.7 2.7 %collective-permute-start.9 = (bf16[96,1280]{1,0:T(8,128)(2,1)S(1)}, bf16[96,1280]{1,0:T(8,128)(2,1)S(1)}, u32[]{:S(2)}, u32[]{:S(2)}) collective-permute-start(bf16[96,1280]{1,0:T(8,128)(2,1)S(1)} %get-tuple-element.66), channel_id=1, source_target_pairs={{0,80},{64,0},{16,64},{80,16},{1,81},{65,1},{17,65},{81,17},{2,82}... | collective-permute-start | bytes 737288 | tf_op jit(solution)/shard_map/ppermute | solution.py:282
  142.5 2.7 %collective-permute-start.12 = (bf16[96,1280]{1,0:T(8,128)(2,1)S(1)}, bf16[96,1280]{1,0:T(8,128)(2,1)S(1)}, u32[]{:S(2)}, u32[]{:S(2)}) collective-permute-start(bf16[96,1280]{1,0:T(8,128)(2,1)S(1)} %get-tuple-element.69), channel_id=1, source_target_pairs={{0,80},{64,0},{16,64},{80,16},{1,81},{65,1},{17,65},{81,17},{2,82}... | collective-permute-start | bytes 737288 | tf_op jit(solution)/shard_map/ppermute | solution.py:282
  145.2 1.7 shard_map.68
  146.9 0.1 collective-permute-start.15
  147.0 1.4 collective-permute-start.16
  148.4 0.1 select_convert_fusion
  148.5 10.3 %collective-permute-done.15 = bf16[96,1280]{1,0:T(8,128)(2,1)S(1)} collective-permute-done((bf16[96,1280]{1,0:T(8,128)(2,1)S(1)}, bf16[96,1280]{1,0:T(8,128)(2,1)S(1)}, u32[]{:S(2)}, u32[]{:S(2)}) %collective-permute-start.15) | collective-permute-done | bytes 245792 | tf_op jit(solution)/shard_map/ppermute | solution.py:282
  158.9 2.6 %collective-permute-start.20 = (bf16[96,1280]{1,0:T(8,128)(2,1)S(1)}, bf16[96,1280]{1,0:T(8,128)(2,1)S(1)}, u32[]{:S(2)}, u32[]{:S(2)}) collective-permute-start(bf16[96,1280]{1,0:T(8,128)(2,1)S(1)} %select_convert_fusion), channel_id=1, source_target_pairs={{0,32},{32,0},{1,33},{33,1},{2,34},{34,2},{3,35},{35,3},{4,36},{36... | collective-permute-start | bytes 737288 | tf_op jit(solution)/shard_map/ppermute | solution.py:393
  161.5 0.1 select_convert_fusion.1
  161.6 0.1 collective-permute-start.17
  161.7 4.7 %collective-permute-done.13 = bf16[96,1280]{1,0:T(8,128)(2,1)S(1)} collective-permute-done((bf16[96,1280]{1,0:T(8,128)(2,1)S(1)}, bf16[96,1280]{1,0:T(8,128)(2,1)S(1)}, u32[]{:S(2)}, u32[]{:S(2)}) %collective-permute-start.13) | collective-permute-done | bytes 245792 | tf_op jit(solution)/shard_map/ppermute | solution.py:282
  166.4 0.1 select_convert_fusion.2
  166.5 2.9 %collective-permute-start.14 = (bf16[96,1280]{1,0:T(8,128)(2,1)S(1)}, bf16[96,1280]{1,0:T(8,128)(2,1)S(1)}, u32[]{:S(2)}, u32[]{:S(2)}) collective-permute-start(bf16[96,1280]{1,0:T(8,128)(2,1)S(1)} %select_convert_fusion.2), channel_id=1, source_target_pairs={{0,32},{32,0},{1,33},{33,1},{2,34},{34,2},{3,35},{35,3},{4,36},{36... | collective-permute-start | bytes 737288 | tf_op jit(solution)/shard_map/ppermute | solution.py:393
  169.3 0.1 select_convert_fusion.3
  169.4 0.1 collective-permute-start.11
  169.6 0.1 add_convert_fusion
  169.7 0.1 add_convert_fusion.1
  169.8 0.7 collective-permute-done.14
  170.5 0.1 add_convert_fusion.2
  170.6 0.4 collective-permute-done.11
  171.0 0.1 add_convert_fusion.3
  171.2 1.0 pad_maximum_fusion
  (64 shorter events, 0.9 us)
Async XLA Ops:
  0.0 1.5 copy-start.7
  1.4 1.0 copy-start.8
  40.4 2.9 %copy-start.6 = (bf16[16,448,128]{2,1,0:T(8,128)(2,1)}, bf16[16,448,128]{2,1,0:T(8,128)(2,1)S(1)}, u32[]{:S(2)}) copy-start(bf16[16,448,128]{2,1,0:T(8,128)(2,1)S(1)} %all_to_all.10) | copy-start | bytes 5505028
  40.4 3.6 %copy-start.9 = (s32[20,96,16]{1,2,0:T(8,128)S(1)}, s32[20,96,16]{1,2,0:T(8,128)}, u32[]{:S(2)}) copy-start(s32[20,96,16]{1,2,0:T(8,128)} %param.9) | copy-start | bytes 368644
  40.5 24.3 %collective-permute-start.2 = (bf16[4,4,256,128]{3,2,1,0:T(8,128)(2,1)S(1)}, bf16[4,4,256,128]{3,2,1,0:T(8,128)(2,1)S(1)}, u32[]{:S(2)}, u32[]{:S(2)}) collective-permute-start(bf16[4,4,256,128]{3,2,1,0:T(8,128)(2,1)S(1)} %slice.130.refs_6_), channel_id=1, source_target_pairs={{0,3},{1,0},{2,1},{3,2},{4,7},{5,4},{6,5},{7,6},{8,11},{9,8},{10,9... | collective-permute-start | bytes 3145736 | tf_op jit(solution)/shard_map/ppermute | solution.py:41
  43.3 24.6 %collective-permute-start.1 = (bf16[4,4,256,128]{3,2,1,0:T(8,128)(2,1)S(1)}, bf16[4,4,256,128]{3,2,1,0:T(8,128)(2,1)S(1)}, u32[]{:S(2)}, u32[]{:S(2)}) collective-permute-start(bf16[4,4,256,128]{3,2,1,0:T(8,128)(2,1)S(1)} %slice.130.refs_6_), channel_id=1, source_target_pairs={{0,1},{1,2},{2,3},{3,0},{4,5},{5,6},{6,7},{7,4},{8,9},{9,10},{10,1... | collective-permute-start | bytes 3145736 | tf_op jit(solution)/shard_map/ppermute | solution.py:37
  43.3 24.6 %collective-permute-start = (bf16[4,4,256,128]{3,2,1,0:T(8,128)(2,1)S(1)}, bf16[4,4,256,128]{3,2,1,0:T(8,128)(2,1)}, u32[]{:S(2)}, u32[]{:S(2)}) collective-permute-start(bf16[4,4,256,128]{3,2,1,0:T(8,128)(2,1)S(1)} %slice.130.refs_6_), channel_id=1, source_target_pairs={{0,4},{4,0},{1,5},{5,1},{2,6},{6,2},{3,7},{7,3},{8,12},{12,8},{9,1... | collective-permute-start | bytes 3145736 | tf_op jit(solution)/shard_map/ppermute | solution.py:45
  60.7 10.6 %copy-start.1 = (s32[6]{0:T(128)S(1)}, s32[6]{0:T(128)}, u32[]{:S(2)}) copy-start(s32[6]{0:T(128)} %stack.27.where_ref.refs_0_) | copy-start | bytes 76
  60.7 10.6 %copy-start.2 = (s32[72,16]{1,0:T(8,128)S(1)}, s32[72,16]{1,0:T(8,128)}, u32[]{:S(2)}) copy-start(s32[72,16]{1,0:T(8,128)} %get-tuple-element.45.refs_1_) | copy-start | bytes 13828
  60.7 10.6 %copy-start.3 = (s32[72,16]{1,0:T(8,128)S(1)}, s32[72,16]{1,0:T(8,128)}, u32[]{:S(2)}) copy-start(s32[72,16]{1,0:T(8,128)} %get-tuple-element.46.refs_2_) | copy-start | bytes 13828
  60.8 10.6 %copy-start.4 = (s32[72,16]{1,0:T(8,128)S(1)}, s32[72,16]{1,0:T(8,128)}, u32[]{:S(2)}) copy-start(s32[72,16]{1,0:T(8,128)} %get-tuple-element.47.refs_3_) | copy-start | bytes 13828
  60.8 10.6 %copy-start.5 = (s32[3,24]{1,0:T(4,128)S(1)}, s32[3,24]{1,0:T(4,128)}, u32[]{:S(2)}) copy-start(s32[3,24]{1,0:T(4,128)} %get-tuple-element.48.refs_4_) | copy-start | bytes 868
  67.9 23.9 %collective-permute-start.4 = (bf16[4,4,256,128]{3,2,1,0:T(8,128)(2,1)}, bf16[4,4,256,128]{3,2,1,0:T(8,128)(2,1)S(1)}, u32[]{:S(2)}, u32[]{:S(2)}) collective-permute-start(bf16[4,4,256,128]{3,2,1,0:T(8,128)(2,1)} %collective-permute-done.refs_7_), channel_id=1, source_target_pairs={{0,1},{1,2},{2,3},{3,0},{4,5},{5,6},{6,7},{7,4},{8,9},{9,10},{10,1... | collective-permute-start | bytes 3145736 | tf_op jit(solution)/shard_map/ppermute | solution.py:37
  67.9 23.9 %collective-permute-start.5 = (bf16[4,4,256,128]{3,2,1,0:T(8,128)(2,1)S(1)}, bf16[4,4,256,128]{3,2,1,0:T(8,128)(2,1)S(1)}, u32[]{:S(2)}, u32[]{:S(2)}) collective-permute-start(bf16[4,4,256,128]{3,2,1,0:T(8,128)(2,1)S(1)} %collective-permute-done.2.refs_9_), channel_id=1, source_target_pairs={{0,3},{1,0},{2,1},{3,2},{4,7},{5,4},{6,5},{7,6},{8,11},{9,8},{10,9... | collective-permute-start | bytes 3145736 | tf_op jit(solution)/shard_map/ppermute | solution.py:41
  70.6 21.9 %collective-permute-start.3 = (bf16[4,4,256,128]{3,2,1,0:T(8,128)(2,1)S(1)}, bf16[4,4,256,128]{3,2,1,0:T(8,128)(2,1)S(1)}, u32[]{:S(2)}, u32[]{:S(2)}) collective-permute-start(bf16[4,4,256,128]{3,2,1,0:T(8,128)(2,1)S(1)} %collective-permute-done.2.refs_9_), channel_id=1, source_target_pairs={{0,4},{4,0},{1,5},{5,1},{2,6},{6,2},{3,7},{7,3},{8,12},{12,8},{9,1... | collective-permute-start | bytes 3145736 | tf_op jit(solution)/shard_map/ppermute | solution.py:45
  92.6 10.3 %collective-permute-start.8 = (bf16[4,4,64,128]{3,2,1,0:T(8,128)(2,1)S(1)}, bf16[4,4,64,128]{3,2,1,0:T(8,128)(2,1)S(1)}, u32[]{:S(2)}, u32[]{:S(2)}) collective-permute-start(bf16[4,4,64,128]{3,2,1,0:T(8,128)(2,1)S(1)} %slice.105), channel_id=1, source_target_pairs={{0,3},{1,0},{2,1},{3,2},{4,7},{5,4},{6,5},{7,6},{8,11},{9,8},{10,9... | collective-permute-start | bytes 786440 | tf_op jit(solution)/shard_map/ppermute | solution.py:41
  94.2 8.7 %collective-permute-start.7 = (bf16[4,4,96,128]{3,2,1,0:T(8,128)(2,1)S(1)}, bf16[4,4,96,128]{3,2,1,0:T(8,128)(2,1)S(1)}, u32[]{:S(2)}, u32[]{:S(2)}) collective-permute-start(bf16[4,4,96,128]{3,2,1,0:T(8,128)(2,1)S(1)} %slice.104), channel_id=1, source_target_pairs={{0,1},{1,2},{2,3},{3,0},{4,5},{5,6},{6,7},{7,4},{8,9},{9,10},{10,1... | collective-permute-start | bytes 1179656 | tf_op jit(solution)/shard_map/ppermute | solution.py:37
  94.2 8.8 %collective-permute-start.6 = (bf16[4,4,96,128]{3,2,1,0:T(8,128)(2,1)S(1)}, bf16[4,4,96,128]{3,2,1,0:T(8,128)(2,1)S(1)}, u32[]{:S(2)}, u32[]{:S(2)}) collective-permute-start(bf16[4,4,96,128]{3,2,1,0:T(8,128)(2,1)S(1)} %slice.103), channel_id=1, source_target_pairs={{0,4},{4,0},{1,5},{5,1},{2,6},{6,2},{3,7},{7,3},{8,12},{12,8},{9,1... | collective-permute-start | bytes 1179656 | tf_op jit(solution)/shard_map/ppermute | solution.py:45
  110.4 17.8 %all-to-all-start.1 = ((bf16[4,816,128]{2,1,0:T(8,128)(2,1)}), bf16[4,816,128]{2,1,0:T(8,128)(2,1)S(1)}, u32[]{:S(2)}, u32[]{:S(2)}) async-start(bf16[4,816,128]{2,1,0:T(8,128)(2,1)} %shard_map.67), calls=%async_computation.1 | async-start | bytes 1671168 | tf_op jit(solution)/shard_map/all_to_all | solution.py:374
  129.1 2.9 %copy-start = (bf16[640,5120]{1,0:T(8,128)(2,1)S(1)}, bf16[640,5120]{1,0:T(8,128)(2,1)}, u32[]{:S(2)}) copy-start(bf16[640,5120]{1,0:T(8,128)(2,1)} %w_ref.5) | copy-start | bytes 19660804
  133.8 13.1 %collective-permute-start.18 = (bf16[96,1280]{1,0:T(8,128)(2,1)S(1)}, bf16[96,1280]{1,0:T(8,128)(2,1)S(1)}, u32[]{:S(2)}, u32[]{:S(2)}) collective-permute-start(bf16[96,1280]{1,0:T(8,128)(2,1)S(1)} %get-tuple-element.75), channel_id=1, source_target_pairs={{0,80},{64,0},{16,64},{80,16},{1,81},{65,1},{17,65},{81,17},{2,82}... | collective-permute-start | bytes 737288 | tf_op jit(solution)/shard_map/ppermute | solution.py:282
  139.0 7.9 %collective-permute-start.19 = (bf16[96,1280]{1,0:T(8,128)(2,1)S(1)}, bf16[96,1280]{1,0:T(8,128)(2,1)S(1)}, u32[]{:S(2)}, u32[]{:S(2)}) collective-permute-start(bf16[96,1280]{1,0:T(8,128)(2,1)S(1)} %get-tuple-element.76), channel_id=1, source_target_pairs={{0,64},{64,16},{16,80},{80,0},{1,65},{65,17},{17,81},{81,1},{2,66}... | collective-permute-start | bytes 737288 | tf_op jit(solution)/shard_map/ppermute | solution.py:282
  139.7 29.6 %collective-permute-start.9 = (bf16[96,1280]{1,0:T(8,128)(2,1)S(1)}, bf16[96,1280]{1,0:T(8,128)(2,1)S(1)}, u32[]{:S(2)}, u32[]{:S(2)}) collective-permute-start(bf16[96,1280]{1,0:T(8,128)(2,1)S(1)} %get-tuple-element.66), channel_id=1, source_target_pairs={{0,80},{64,0},{16,64},{80,16},{1,81},{65,1},{17,65},{81,17},{2,82}... | collective-permute-start | bytes 737288 | tf_op jit(solution)/shard_map/ppermute | solution.py:282
  142.5 26.9 %collective-permute-start.10 = (bf16[96,1280]{1,0:T(8,128)(2,1)S(1)}, bf16[96,1280]{1,0:T(8,128)(2,1)S(1)}, u32[]{:S(2)}, u32[]{:S(2)}) collective-permute-start(bf16[96,1280]{1,0:T(8,128)(2,1)S(1)} %get-tuple-element.67), channel_id=1, source_target_pairs={{0,64},{64,16},{16,80},{80,0},{1,65},{65,17},{17,81},{81,1},{2,66}... | collective-permute-start | bytes 737288 | tf_op jit(solution)/shard_map/ppermute | solution.py:282
  142.5 19.1 %collective-permute-start.12 = (bf16[96,1280]{1,0:T(8,128)(2,1)S(1)}, bf16[96,1280]{1,0:T(8,128)(2,1)S(1)}, u32[]{:S(2)}, u32[]{:S(2)}) collective-permute-start(bf16[96,1280]{1,0:T(8,128)(2,1)S(1)} %get-tuple-element.69), channel_id=1, source_target_pairs={{0,80},{64,0},{16,64},{80,16},{1,81},{65,1},{17,65},{81,17},{2,82}... | collective-permute-start | bytes 737288 | tf_op jit(solution)/shard_map/ppermute | solution.py:282
  146.9 12.0 %collective-permute-start.15 = (bf16[96,1280]{1,0:T(8,128)(2,1)S(1)}, bf16[96,1280]{1,0:T(8,128)(2,1)S(1)}, u32[]{:S(2)}, u32[]{:S(2)}) collective-permute-start(bf16[96,1280]{1,0:T(8,128)(2,1)S(1)} %get-tuple-element.72), channel_id=1, source_target_pairs={{0,80},{64,0},{16,64},{80,16},{1,81},{65,1},{17,65},{81,17},{2,82}... | collective-permute-start | bytes 737288 | tf_op jit(solution)/shard_map/ppermute | solution.py:282
  147.0 11.9 %collective-permute-start.16 = (bf16[96,1280]{1,0:T(8,128)(2,1)S(1)}, bf16[96,1280]{1,0:T(8,128)(2,1)S(1)}, u32[]{:S(2)}, u32[]{:S(2)}) collective-permute-start(bf16[96,1280]{1,0:T(8,128)(2,1)S(1)} %get-tuple-element.73), channel_id=1, source_target_pairs={{0,64},{64,16},{16,80},{80,0},{1,65},{65,17},{17,81},{81,1},{2,66}... | collective-permute-start | bytes 737288 | tf_op jit(solution)/shard_map/ppermute | solution.py:282
  158.9 7.5 %collective-permute-start.13 = (bf16[96,1280]{1,0:T(8,128)(2,1)S(1)}, bf16[96,1280]{1,0:T(8,128)(2,1)S(1)}, u32[]{:S(2)}, u32[]{:S(2)}) collective-permute-start(bf16[96,1280]{1,0:T(8,128)(2,1)S(1)} %get-tuple-element.70), channel_id=1, source_target_pairs={{0,64},{64,16},{16,80},{80,0},{1,65},{65,17},{17,81},{81,1},{2,66}... | collective-permute-start | bytes 737288 | tf_op jit(solution)/shard_map/ppermute | solution.py:282
  158.9 10.7 %collective-permute-start.20 = (bf16[96,1280]{1,0:T(8,128)(2,1)S(1)}, bf16[96,1280]{1,0:T(8,128)(2,1)S(1)}, u32[]{:S(2)}, u32[]{:S(2)}) collective-permute-start(bf16[96,1280]{1,0:T(8,128)(2,1)S(1)} %select_convert_fusion), channel_id=1, source_target_pairs={{0,32},{32,0},{1,33},{33,1},{2,34},{34,2},{3,35},{35,3},{4,36},{36... | collective-permute-start | bytes 737288 | tf_op jit(solution)/shard_map/ppermute | solution.py:393
  161.6 8.1 %collective-permute-start.17 = (bf16[96,1280]{1,0:T(8,128)(2,1)S(1)}, bf16[96,1280]{1,0:T(8,128)(2,1)S(1)}, u32[]{:S(2)}, u32[]{:S(2)}) collective-permute-start(bf16[96,1280]{1,0:T(8,128)(2,1)S(1)} %select_convert_fusion.1), channel_id=1, source_target_pairs={{0,32},{32,0},{1,33},{33,1},{2,34},{34,2},{3,35},{35,3},{4,36},{36... | collective-permute-start | bytes 737288 | tf_op jit(solution)/shard_map/ppermute | solution.py:393
  166.5 4.0 %collective-permute-start.14 = (bf16[96,1280]{1,0:T(8,128)(2,1)S(1)}, bf16[96,1280]{1,0:T(8,128)(2,1)S(1)}, u32[]{:S(2)}, u32[]{:S(2)}) collective-permute-start(bf16[96,1280]{1,0:T(8,128)(2,1)S(1)} %select_convert_fusion.2), channel_id=1, source_target_pairs={{0,32},{32,0},{1,33},{33,1},{2,34},{34,2},{3,35},{35,3},{4,36},{36... | collective-permute-start | bytes 737288 | tf_op jit(solution)/shard_map/ppermute | solution.py:393
  169.4 1.6 collective-permute-start.11

commit v5 on v4

v5 whole, which is shorter than its diff:
```python
import functools

import jax
import jax.numpy as jnp
from jax import lax
from jax.experimental import pallas as pl
from jax.experimental.pallas import tpu as pltpu
from jax.sharding import Mesh, PartitionSpec as P

HEAD = 128
BLOCK = 128
ROWS = 96
CHUNKS = 4
SUPER = ROWS * CHUNKS
RUN = 16
MAIN = ROWS // 2
EXT = RUN
PART = MAIN + EXT
KV = 2 * PART
LOG2E = 1.4426950408889634
SCALE = HEAD ** -0.5 * LOG2E
FLOOR = -1e30
NAMES = ("xh", "zh", "zl", "y", "xl", "c")
GRID = ("xl", "c", "xh", "zh", "zl", "y")
SIZES = (2, 2, 2, 2, 2, 4)
SPREAD = ("xh", "zh", "zl", "xl", "c")
COLS = 8
UNITS = 3 * COLS
SLOTS = 16
MAIN_GROUP = 4
EXT_GROUP = 8
BATCH = 12
STATS = 16
WIDTH = 1280
SMEM = pl.BlockSpec(memory_space=pltpu.SMEM)
VMEM = pl.BlockSpec(memory_space=pltpu.VMEM)
HBM = pl.BlockSpec(memory_space=pl.ANY)


def ring_up(x):
    return lax.ppermute(x, "y", [(i, (i + 1) % 4) for i in range(4)])


def ring_down(x):
    return lax.ppermute(x, "y", [(i, (i - 1) % 4) for i in range(4)])


def plan_kernel(where_ref, count_ref, table_ref, start_ref, n_ref, lists, sem):
    y, head, shared, share = [where_ref[i] for i in range(4)]
    copies = [
        pltpu.make_async_copy(table_ref.at[h], lists.at[i], sem.at[i])
        for i, h in enumerate((head, shared))
    ]
    for copy in copies:
        copy.start()
    for copy in copies:
        copy.wait()

    for which, h in enumerate((head, shared)):

        def unit_step(local, carry):
            unit = which * UNITS + local
            column = (local * 171) >> 9
            row = (column * 4 + y) * 3 + (local - 3 * column)
            start_ref[unit, 0] = 0
            start_ref[2 * UNITS + unit, 0] = 0

            def slot_step(slot, found):
                block = lists[which, row, slot]
                sb = (block * 171) >> 9
                r = block - 3 * sb
                dy = ((sb & 3) + 4 - y) & 3
                late = dy == 2
                place = jnp.where(late, 0, (4 - dy) & 3) - jnp.where(dy == 1, 1, 0)
                place = place * COLS + (sb >> 2)
                if which == 0:
                    start = place * (CHUNKS * MAIN) + r * (BLOCK // 2)
                else:
                    chunk = ((r * 8 + share) * 43) >> 8
                    start = (place * CHUNKS + chunk) * EXT
                early_n, late_n = found
                start_ref[jnp.where(late, 2 * UNITS, 0) + unit, jnp.where(late, late_n, early_n)] = start
                step = late.astype(jnp.int32)
                return early_n + 1 - step, late_n + step

            zero = jnp.int32(0)
            early_n, late_n = lax.fori_loop(0, count_ref[h, row], slot_step, (zero, zero))
            n_ref[0, unit] = early_n
            n_ref[1, unit] = late_n
            return carry

        lax.fori_loop(0, UNITS, unit_step, 0)


def plan(where, counts, table):
    return pl.pallas_call(
        plan_kernel,
        out_shape=(
            jax.ShapeDtypeStruct((4 * UNITS, SLOTS), jnp.int32),
            jax.ShapeDtypeStruct((2, 2 * UNITS), jnp.int32),
        ),
        in_specs=[SMEM, SMEM, HBM],
        out_specs=(SMEM, SMEM),
        scratch_shapes=[pltpu.SMEM((2, 96, SLOTS), jnp.int32), pltpu.SemaphoreType.DMA((2,))],
        cost_estimate=pl.CostEstimate(flops=8_000_000_000, bytes_accessed=100_000, transcendentals=0),
    )(where, counts, table)


def stage_kernel(last, pieces, *refs):
    where_ref, start_ref, n_ref, q_ref = refs[:4]
    refs = refs[4:]
    xl = where_ref[4]
    if last:
        before, (last_k, last_v, out_ref), refs = refs[:3], refs[3:6], refs[6:]
        k_main, v_main, k_ext, v_ext, sem, top_ref, tot_ref, acc_ref = refs
        loads = [(last_k, 0, 0, k_main, k_ext), (last_v, 0, 0, v_main, v_ext)]
    else:
        sources, refs = refs[:pieces], refs[pieces:]
        top_ref, tot_ref, acc_ref, k_main, v_main, k_ext, v_ext, sem = refs
        loads = []
        for i, source in enumerate(sources):
            loads += [(source, 0, i, k_main, k_ext), (source, PART, i, v_main, v_ext)]
    stage = 1 if last else 0
    first = not last
    copies = []
    for source, lo, piece, main, ext in loads:
        for target, at, rows in ((main, lo, MAIN), (ext, lo + MAIN, EXT)):
            copy = pltpu.make_async_copy(
                source.at[:, :, pl.ds(at, rows)], target.at[piece], sem.at[len(copies)]
            )
            copy.start()
            copies.append(copy)

    def begin(unit, carry):
        if first:
            top_ref[unit] = jnp.full((BLOCK, HEAD), FLOOR, jnp.float32)
            tot_ref[unit] = jnp.zeros((BLOCK, HEAD), jnp.float32)
            acc_ref[unit] = jnp.zeros((BLOCK, HEAD), jnp.float32)
        else:
            for old, new in zip(before, (top_ref, tot_ref, acc_ref)):
                new[unit] = old[unit]
        return carry

    lax.fori_loop(0, 2 * UNITS, begin, 0)
    for copy in copies:
        copy.wait()

    k_flat = k_main.reshape(pieces * COLS * CHUNKS * MAIN, HEAD)
    v_flat = v_main.reshape(pieces * COLS * CHUNKS * MAIN, HEAD)
    ke_flat = k_ext.reshape(pieces * COLS * CHUNKS * EXT, HEAD)
    ve_flat = v_ext.reshape(pieces * COLS * CHUNKS * EXT, HEAD)
    lane = lax.broadcasted_iota(jnp.int32, (BLOCK, HEAD), 1)
    eye = lax.broadcasted_iota(jnp.int32, (BLOCK, BLOCK), 0) == lane

    def dot_t(a, b):
        return lax.dot_general(a, b, (((1,), (1,)), ((), ())), preferred_element_type=jnp.float32)

    def run(units, group, key_flat, value_flat, width):
        ns = [n_ref[stage, unit] for unit in units]
        most = functools.reduce(jnp.maximum, ns)

        def step(t, carry):
            col = lax.broadcasted_iota(jnp.int32, (BLOCK, group * width), 1)
            values, scores = [], []
            for unit, n in zip(units, ns):
                starts = []
                for i in range(group):
                    slot = jnp.maximum(jnp.minimum(group * t + i, n - 1), 0)
                    start = start_ref[stage * 2 * UNITS + unit, slot]
                    starts.append(pl.multiple_of(start, width))
                keys = jnp.concatenate([key_flat[pl.ds(r, width), :] for r in starts], axis=0)
                values.append(
                    jnp.concatenate([value_flat[pl.ds(r, width), :] for r in starts], axis=0)
                )
                s = dot_t(q_ref[unit], keys)
                scores.append(jnp.where(col < (n - group * t) * width, s, 2 * FLOOR))
            for unit, s, v in zip(units, scores, values):
                top = top_ref[unit][:, :1]
                new_top = jnp.maximum(top, jnp.max(s, axis=1, keepdims=True))
                p = jnp.exp2((s - new_top) * SCALE)
                alpha = jnp.exp2((top - new_top) * SCALE)
                part = functools.reduce(
                    jnp.add, [p[:, i : i + HEAD] for i in range(0, group * width, HEAD)]
                )
                product = jnp.dot(p.astype(jnp.bfloat16), v, preferred_element_type=jnp.float32)
                top_ref[unit] = jnp.broadcast_to(new_top, (BLOCK, HEAD))
                tot_ref[unit] = tot_ref[unit] * alpha + part
                acc_ref[unit] = acc_ref[unit] * alpha + product
            return carry

        lax.fori_loop(0, lax.div(most + (group - 1), group), step, 0)

    def finish(unit):
        total = jnp.sum(tot_ref[unit], axis=1, keepdims=True)
        return top_ref[unit][:, :1], total, (acc_ref[unit] / total).astype(jnp.bfloat16)

    def store(sb, r, top, value):
        for i in range(4):
            granule = 4 * r + i
            chunk = granule // 3
            to = sb if chunk in (0, 3) else jnp.where(xl == 2 - chunk, sb ^ 4, sb)
            place = lax.rem(chunk + 4 - 2 * xl, 4)
            row = pl.multiple_of(top + place * ROWS + (granule % 3) * 32, 32)
            out_ref[to, pl.ds(row, 32), :] = value[32 * i : 32 * i + 32]

    levels = [[], []]
    for which in range(2):
        for lo in range(0, UNITS, BATCH):
            units = range(which * UNITS + lo, which * UNITS + lo + BATCH)
            if which == 0:
                run(units, MAIN_GROUP, k_flat, v_flat, BLOCK // 2)
            else:
                run(units, EXT_GROUP, ke_flat, ve_flat, RUN)
            if not last:
                continue
            for unit in units:
                top, total, value = finish(unit)
                local = unit - which * UNITS
                store(local // 3, local % 3, which * SUPER, value)
                level = top * SCALE + jnp.log2(total)
                levels[which].append(jnp.sum(jnp.where(eye, level, 0.0), axis=0, keepdims=True))
    if not last:
        return
    index = lax.broadcasted_iota(jnp.int32, (STATS, HEAD), 0)
    column = lax.broadcasted_iota(jnp.int32, (1, HEAD), 1)
    for unit in range(UNITS):
        sb, r = unit // 3, unit % 3
        chunk = (r * BLOCK + column) // ROWS
        tile = jnp.zeros((STATS, HEAD), jnp.float32)
        for which in range(2):
            level = jnp.where(chunk == 2 - xl, levels[which][3 * (sb ^ 4) + r], levels[which][unit])
            for i in range(3):
                term = level.astype(jnp.bfloat16).astype(jnp.float32)
                tile = jnp.where(index == 3 * which + i, term, tile)
                level = level - term
        out_ref[sb, pl.ds(2 * SUPER + r * STATS, STATS), :] = tile.astype(jnp.bfloat16)


def attend(last, where, plans, q, state, sources):
    pieces = 1 if last else len(sources)
    kept = jax.ShapeDtypeStruct((2 * UNITS, BLOCK, HEAD), jnp.float32)
    scratch = [
        pltpu.VMEM((pieces, COLS, CHUNKS, MAIN, HEAD), jnp.bfloat16),
        pltpu.VMEM((pieces, COLS, CHUNKS, MAIN, HEAD), jnp.bfloat16),
        pltpu.VMEM((pieces, COLS, CHUNKS, EXT, HEAD), jnp.bfloat16),
        pltpu.VMEM((pieces, COLS, CHUNKS, EXT, HEAD), jnp.bfloat16),
        pltpu.SemaphoreType.DMA((4 * pieces,)),
    ]
    if last:
        out_shape = jax.ShapeDtypeStruct((COLS, 2 * SUPER + 3 * STATS, HEAD), jnp.bfloat16)
        out_specs = VMEM
        scratch += [pltpu.VMEM(kept.shape, kept.dtype)] * 3
    else:
        out_shape, out_specs = (kept,) * 3, (VMEM,) * 3
    return pl.pallas_call(
        functools.partial(stage_kernel, last, pieces),
        out_shape=out_shape,
        in_specs=[SMEM] * 3 + [VMEM] * (1 + len(state)) + [HBM] * len(sources),
        out_specs=out_specs,
        scratch_shapes=scratch,
        compiler_params=pltpu.CompilerParams(vmem_limit_bytes=32 * 1024 * 1024),
        cost_estimate=pl.CostEstimate(
            flops=pieces * 5_000_000_000, bytes_accessed=pieces * 2_000_000, transcendentals=1_000_000
        ),
    )(where, *plans, q, *state, *sources)


def around(x, step):
    index = lambda at: (at % 2) * 2 + at % 4 // 2
    return lax.ppermute(x, ("xl", "xh"), [(index(i), index(i + step)) for i in range(4)])


def project_kernel(parts, rows_ref, w_ref, *outs):
    for (chunk, lo, count), out in zip(parts, outs):
        rows = rows_ref[pl.ds(lo, count), :]
        for at in range(0, WIDTH, 256):
            product = jnp.dot(
                rows, w_ref[:, pl.ds(chunk * WIDTH + at, 256)], preferred_element_type=jnp.float32
            )
            out[:, pl.ds(at, 256)] = product.astype(out.dtype)


def project_parts(rows, w, parts):
    return pl.pallas_call(
        functools.partial(project_kernel, parts),
        out_shape=tuple(
            jax.ShapeDtypeStruct((count, WIDTH), jnp.float32 if lo == 0 else jnp.bfloat16)
            for _, lo, count in parts
        ),
        in_specs=[VMEM, VMEM],
        out_specs=(VMEM,) * len(parts),
        compiler_params=pltpu.CompilerParams(vmem_limit_bytes=24 * 1024 * 1024),
        cost_estimate=pl.CostEstimate(
            flops=sum(2 * count * WIDTH * 640 for _, _, count in parts),
            bytes_accessed=4_000_000,
            transcendentals=0,
        ),
    )(rows, w)


def project(rows, w):
    chunks = w.shape[1] // WIDTH
    sides = lambda k: [(k, 2 * ROWS, ROWS), (k, 3 * ROWS, ROWS)]
    own = lambda k: [(k, 0, 2 * ROWS)]
    first = project_parts(rows, w, sides(0))
    rest = project_parts(rows, w, sum([sides(k) for k in range(1, chunks)], []))
    owns = project_parts(rows, w, sum([own(k) for k in range(chunks)], []))
    sent = first + rest
    return sent[0::2], sent[1::2], owns


def main_keys(rows):
    runs = rows.reshape(3, 2, RUN, 4, 4, HEAD).transpose(4, 1, 3, 0, 2, 5)
    return runs.reshape(32, MAIN, HEAD)


def shared_keys(rows, xl, c):
    runs = jnp.pad(rows, ((0, 32), (0, 0), (0, 0))).reshape(8, RUN, 4, HEAD)
    runs = jnp.where(xl == 0, runs, jnp.roll(runs, -4, axis=0))
    runs = jnp.where(c == 0, runs, jnp.roll(runs, -2, axis=0))
    return runs.transpose(0, 2, 1, 3).reshape(32, EXT, HEAD)


def merge(shares, levels):
    weights = jnp.exp2(levels - jnp.max(levels, axis=1, keepdims=True))
    weights = weights / jnp.sum(weights, axis=1, keepdims=True)
    return jnp.sum(shares.astype(jnp.float32) * weights[..., None], axis=1).astype(jnp.bfloat16)


def per_device(queries, key_rows, value_rows, block_list, block_count, w_out):
    xh, zh, zl, y, xl, c = [lax.axis_index(name) for name in NAMES]
    u = 2 * xl + c
    j = 2 * xh + zh
    k5 = key_rows.reshape(ROWS, 4, 5, HEAD)
    v5 = value_rows.reshape(ROWS, 4, 5, HEAD)
    q5 = queries.reshape(ROWS, 4, 5, HEAD)
    sent = jnp.concatenate(
        [
            main_keys(k5[:, :, :4]),
            shared_keys(k5[:, :, 4], xl, c),
            main_keys(v5[:, :, :4]),
            shared_keys(v5[:, :, 4], xl, c),
        ],
        axis=1,
    )
    kv = lax.all_to_all(sent, SPREAD, 0, 0, tiled=True).reshape(COLS, CHUNKS, KV, HEAD)

    q = jnp.stack([q5[:, :, :4], jnp.broadcast_to(q5[:, :, 4:], (ROWS, 4, 4, HEAD))])
    q = jnp.broadcast_to(q.transpose(3, 2, 0, 1, 4)[:, None], (4, 2, 4, 2, ROWS, HEAD))
    q = lax.all_to_all(q.reshape(32, 2, ROWS, HEAD), SPREAD, 0, 0, tiled=True)
    q = q.reshape(COLS, CHUNKS, 2, ROWS, HEAD).transpose(2, 0, 1, 3, 4).reshape(2 * UNITS, BLOCK, HEAD)

    where = jnp.stack([y, 5 * u + j, 5 * u + 4, 2 * j + zl, xl]).astype(jnp.int32)
    plans = plan(where, block_count, block_list)

    below, above = ring_up(kv), ring_down(kv)
    below, above, q, plans = lax.optimization_barrier((below, above, q, plans))
    last_k = ring_down(above[:, :, :PART])
    last_v = ring_up(below[:, :, PART:])
    state = attend(False, where, plans, q, (), (kv, below, above))
    out = attend(True, where, plans, q, state, (last_k, last_v))
    out = lax.all_to_all(out, ("xh", "zh", "zl"), 0, 0, tiled=True)

    levels = out[:, 2 * SUPER :].reshape(COLS, 3, STATS, BLOCK)[:, :, :6].astype(jnp.float32)
    levels = jnp.sum(levels.reshape(COLS, 3, 2, 3, BLOCK), axis=3).transpose(2, 0, 1, 3)
    levels = levels.reshape(2, COLS, SUPER)
    levels = jnp.where(xl == 0, levels, jnp.roll(levels, 2 * ROWS, axis=2))
    heads = merge(out[:, :SUPER].reshape(4, 2, SUPER, HEAD), levels[0].reshape(4, 2, SUPER))
    shared = merge(out[None, :, SUPER : 2 * SUPER], levels[1][None])
    attended = jnp.concatenate([heads, shared], axis=0).transpose(1, 0, 2).reshape(SUPER, 5 * HEAD)

    lows, highs, owns = project(attended, w_out)
    total = []
    for low, high, own in zip(lows, highs, owns):
        first = own[:ROWS] + around(low, -1).astype(jnp.float32)
        second = own[ROWS:] + around(high, 1).astype(jnp.float32)
        keep = jnp.where(c == 0, first, second)
        give = jnp.where(c == 0, second, first).astype(jnp.bfloat16)
        total.append((keep + lax.ppermute(give, "c", [(0, 1), (1, 0)])).astype(jnp.bfloat16))
    return jnp.concatenate(total, axis=1)


def solution(mesh):
    fine = Mesh(mesh.devices.reshape(SIZES), GRID)
    rows = P(NAMES, None)
    return jax.shard_map(
        per_device,
        mesh=fine,
        in_specs=(rows, rows, rows, P(), P(), P(("xl", "c"), None)),
        out_specs=rows,
        check_vma=False,
    )
```

time: 174 us -> 156 us (0.90)
  waiting for transfers between devices: 43 us -> 24.8 us
  starting transfers between devices: 35.3 us -> 43.1 us
  Pallas kernels: 44.1 us -> 39.6 us
  blocking collectives: 34.5 us -> 30 us
    ppermute x8, waiting for transfers between devices: 15.1 us -> 1.39 us  [around(): lax.ppermute(x, ('xl', 'xh'), [(index(i), index(i + step)) for i in range...]
    ppermute x3 -> x2, waiting for transfers between devices: 13.8 us -> 1.71 us  [ring_up(): return lax.ppermute(x, 'y', [(i, (i + 1) % 4) for i in range(4)])]
    all_to_all x1 -> x2, waiting for transfers between devices: 9.59 us -> 21 us  [the longest x1 15.4 us: per_device(): lax.all_to_all(sent, SPREAD, 0, 0, tiled=True)]
    ppermute x4, starting transfers between devices: 5.67 us -> 11.7 us  [per_device(): lax.ppermute(give, 'c', [(0, 1), (1, 0)])]
    all_to_all x1 -> x2, starting transfers between devices: 8.22 us -> 14.2 us  [the longest x1 9.43 us: per_device(): lax.all_to_all(sent, SPREAD, 0, 0, tiled=True)]
    pallas_call x4 -> x3, Pallas kernels: 39.9 us -> 35.4 us  [the longest x2 22.9 us: attend(): pl.pallas_call(functools.partial(stage_kernel, last, pieces), out_shape=o...]
    all_to_all x1, blocking collectives: 34.5 us -> 30 us  [per_device(): out = lax.all_to_all(out, ('xh', 'zh', 'zl'), 0, 0, tiled=True)]
    ppermute x3 -> x2, starting transfers between devices: 7.04 us -> 4.11 us  [ring_down(): return lax.ppermute(x, 'y', [(i, (i - 1) % 4) for i in range(4)])]
  transfers between devices with their start and end apart: 22 -> 18, of which waited for: 9 -> 7; matrix products, arithmetic and copies ran while one was open for 2% -> 4% of each run, Pallas kernels for 20% -> 18%
where the time goes in v5:
time: 156 us; the launch traced here: 155 us
  starting transfers between devices  43.1 us (28%)
  Pallas kernels  39.6 us (25%)
  blocking collectives  30 us (19%)
  waiting for transfers between devices  24.8 us (16%)
  local copies, waits for them, and re-layouts  12.6 us (8%)
  other arithmetic  4.5 us (3%)
    all_to_all x1, blocking collectives, per_device(): out = lax.all_to_all(out, ('xh', 'zh', 'zl'), 0, 0, tiled=True)  30 us
    pallas_call x2, Pallas kernels, attend(): pl.pallas_call(functools.partial(stage_kernel, last, pieces), out_shape=o...  22.9 us
    all_to_all x1, waiting for transfers between devices, per_device(): lax.all_to_all(sent, SPREAD, 0, 0, tiled=True)  15.4 us
    pallas_call x1, Pallas kernels, plan(): pl.pallas_call(plan_kernel, out_shape=(jax.ShapeDtypeStruct((4 * UNITS, S...  12.4 us
    ppermute x4, starting transfers between devices, per_device(): lax.ppermute(give, 'c', [(0, 1), (1, 0)])  11.7 us
    ppermute x8, starting transfers between devices, around(): lax.ppermute(x, ('xl', 'xh'), [(index(i), index(i + step)) for i in range...  11.6 us
    all_to_all x1, starting transfers between devices, per_device(): lax.all_to_all(sent, SPREAD, 0, 0, tiled=True)  9.43 us
    unnamed x19, local copies, waits for them, and re-layouts  6.22 us
  transfers between devices with their start and end apart: 18, of which 7 were waited for; matrix products, arithmetic and copies ran while one was open for 4% of the time, Pallas kernels for 18%

profile of v5, /device:TPU:1, one launch (start us, length us, event | category | flops | bytes accessed | tf_op | source)
XLA Modules:
  0.0 155.2 jit_solution(5222146177810842983)
XLA Ops:
  0.0 1.4 copy.100
  1.4 0.1 copy.103
  1.6 0.3 copy.106
  2.0 0.1 copy.109
  2.1 0.1 copy.104
  2.3 0.1 copy.110
  2.7 0.2 copy.107
  3.0 0.2 copy.101
  3.2 0.0 copy-start.5
  3.3 1.1 pad_maximum_fusion
  4.4 9.4 %all-to-all-start = ((bf16[32,128,128]{2,1,0:T(8,128)(2,1)}), bf16[32,128,128]{2,1,0:T(8,128)(2,1)S(1)}, u32[]{:S(2)}, u32[]{:S(2)}) async-start(bf16[32,128,128]{2,1,0:T(8,128)(2,1)} %pad_maximum_fusion), calls=%async_computation | async-start | bytes 2097152 | tf_op jit(solution)/shard_map/all_to_all | solution.py:346
  13.8 0.3 copy.112
  14.2 0.1 stack_broadcast_in_dim.8
  14.3 0.2 maximum_bitcast_fusion
  14.6 0.6 copy.115
  15.2 15.4 %all-to-all-done = bf16[32,128,128]{2,1,0:T(8,128)(2,1)S(1)} async-done(((bf16[32,128,128]{2,1,0:T(8,128)(2,1)}), bf16[32,128,128]{2,1,0:T(8,128)(2,1)S(1)}, u32[]{:S(2)}, u32[]{:S(2)}) %all-to-all-start) | async-done | bytes 1048608 | tf_op jit(solution)/shard_map/all_to_all | solution.py:346
  30.6 1.5 broadcast_in_dim.2
  32.1 4.8 %all-to-all-start.1 = ((bf16[32,2,96,128]{3,2,1,0:T(8,128)(2,1)}), bf16[32,2,96,128]{3,2,1,0:T(8,128)(2,1)}, u32[]{:S(2)}, u32[]{:S(2)}) async-start(bf16[32,2,96,128]{3,2,1,0:T(8,128)(2,1)} %bitcast.30), calls=%async_computation.1 | async-start | bytes 3145728 | tf_op jit(solution)/shard_map/all_to_all | solution.py:350
  36.9 1.4 collective-permute-start
  38.2 1.5 collective-permute-start.1
  39.7 1.3 copy.117.table_ref
  41.0 0.7 stack.29.where_ref.refs_0_
  41.7 12.4 %shard_map.64 = (s32[96,16]{1,0:T(8,128)}, s32[2,48]{1,0:T(2,128)}) custom-call(s32[5]{0:T(128)} %stack.29.where_ref.refs_0_, s32[20,96]{1,0:T(8,128)} %count_ref.1, s32[20,96,16]{2,1,0:T(8,128)} %copy.117.table_ref), custom_call_target="tpu_custom_call" | custom-call | flops 8000000000 | bytes 100000 | tf_op jit(solution)/shard_map/pallas_call | solution.py:96
  54.1 5.6 %all-to-all-done.1 = bf16[32,2,96,128]{3,2,1,0:T(8,128)(2,1)} async-done(((bf16[32,2,96,128]{3,2,1,0:T(8,128)(2,1)}), bf16[32,2,96,128]{3,2,1,0:T(8,128)(2,1)}, u32[]{:S(2)}, u32[]{:S(2)}) %all-to-all-start.1) | async-done | bytes 1572896 | tf_op jit(solution)/shard_map/all_to_all | solution.py:350
  59.7 1.6 %copy.116 = bf16[8,4,2,96,128]{4,3,1,0,2:T(8,128)(2,1)S(1)} copy(bf16[8,4,2,96,128]{4,3,2,1,0:T(8,128)(2,1)} %bitcast.31) | data formatting | bytes 3145728 | tf_op jit(solution)/shard_map/reshape | solution.py:351
  61.3 1.3 collective-permute-done.refs_5_
  62.6 2.6 %collective-permute-start.2 = (bf16[8,4,64,128]{3,2,1,0:T(8,128)(2,1)S(1)}, bf16[8,4,64,128]{3,2,1,0:T(8,128)(2,1)S(1)}, u32[]{:S(2)}, u32[]{:S(2)}) collective-permute-start(bf16[8,4,64,128]{3,2,1,0:T(8,128)(2,1)S(1)} %slice.138), channel_id=1, source_target_pairs={{0,3},{1,0},{2,1},{3,2},{4,7},{5,4},{6,5},{7,6},{8,11},{9,8},{10,9... | collective-permute-start | bytes 1572872 | tf_op jit(solution)/shard_map/ppermute | solution.py:45
  65.3 0.1 collective-permute-start.3
  65.4 12.5 %shard_map.65 = (f32[48,128,128]{2,1,0:T(8,128)S(1)}, f32[48,128,128]{2,1,0:T(8,128)S(1)}, f32[48,128,128]{2,1,0:T(8,128)S(1)}) custom-call(s32[5]{0:T(128)S(1)} %copy-done.1, s32[96,16]{1,0:T(8,128)S(1)} %copy-done.2, s32[2,48]{1,0:T(2,128)S(1)} %copy-done.3, bf16[48,128,128]{2,1,0:T(8,128)(2,1)S(1)} %bitcast.66, bf16[8,4,128,128]{3,2,1,0:T(8,128)(2,1)S(1)} %bitcast.70, ...), custom_call_target="tpu_custom_call" | custom-call | flops 15000000512 | bytes 6000000 | tf_op jit(solution)/shard_map/pallas_call | solution.py:255
  77.9 0.4 collective-permute-done.3.refs_8_
  78.3 10.4 %shard_map.66 = bf16[8,816,128]{2,1,0:T(8,128)(2,1)S(1)} custom-call(s32[5]{0:T(128)S(1)} %copy-done.1, s32[96,16]{1,0:T(8,128)S(1)} %copy-done.2, s32[2,48]{1,0:T(2,128)S(1)} %copy-done.3, bf16[48,128,128]{2,1,0:T(8,128)(2,1)S(1)} %bitcast.67, f32[48,128,128]{2,1,0:T(8,128)S(1)} %get-tuple-element.34.refs_4_, ...), custom_call_target="tpu_custom_call" | custom-call | flops 5000000000 | bytes 2000000 | tf_op jit(solution)/shard_map/pallas_call | solution.py:255
  88.7 30.0 %all_to_all.15 = bf16[8,816,128]{2,1,0:T(8,128)(2,1)S(1)} all-to-all(bf16[8,816,128]{2,1,0:T(8,128)(2,1)S(1)} %shard_map.66), channel_id=1, replica_groups=mesh['xl'=2,'c'=2,'xh'=2,'zh'=2,'zl'=2,'y'=4] {'xh','zh','zl'}, dimensions={0} | all-to-all | bytes 3342336 | tf_op jit(solution)/shard_map/all_to_all | solution.py:362
  118.8 0.1 fusion.12
  118.9 0.1 maximum_select_fusion.4
  119.1 0.5 fusion.1
  119.6 0.5 multiply_reduce_fusion
  120.1 0.3 copy.120
  120.4 0.3 copy.121.rows_ref
  120.7 2.9 %copy-done = bf16[640,5120]{1,0:T(8,128)(2,1)S(1)} copy-done((bf16[640,5120]{1,0:T(8,128)(2,1)S(1)}, bf16[640,5120]{1,0:T(8,128)(2,1)}, u32[]{:S(2)}) %copy-start) | copy-done | bytes 6553624
  123.5 0.7 shard_map.68
  124.2 3.1 %collective-permute-start.4 = (bf16[96,1280]{1,0:T(8,128)(2,1)S(1)}, bf16[96,1280]{1,0:T(8,128)(2,1)S(1)}, u32[]{:S(2)}, u32[]{:S(2)}) collective-permute-start(bf16[96,1280]{1,0:T(8,128)(2,1)S(1)} %get-tuple-element.38), channel_id=1, source_target_pairs={{0,80},{64,0},{16,64},{80,16},{1,81},{65,1},{17,65},{81,17},{2,82}... | collective-permute-start | bytes 737288 | tf_op jit(solution)/shard_map/ppermute | solution.py:270
  127.4 1.8 %shard_map.69 = (bf16[96,1280]{1,0:T(8,128)(2,1)S(1)}, bf16[96,1280]{1,0:T(8,128)(2,1)S(1)}, bf16[96,1280]{1,0:T(8,128)(2,1)S(1)}, bf16[96,1280]{1,0:T(8,128)(2,...) custom-call(bf16[384,640]{1,0:T(8,128)(2,1)S(1)} %copy.121.rows_ref, bf16[640,5120]{1,0:T(8,128)(2,1)S(1)} %copy-done), custom_call_target="tpu_custom_call" | custom-call | flops 943718400 | bytes 4000000 | tf_op jit(solution)/shard_map/pallas_call | solution.py:284
  129.2 2.7 %collective-permute-start.7 = (bf16[96,1280]{1,0:T(8,128)(2,1)S(1)}, bf16[96,1280]{1,0:T(8,128)(2,1)S(1)}, u32[]{:S(2)}, u32[]{:S(2)}) collective-permute-start(bf16[96,1280]{1,0:T(8,128)(2,1)S(1)} %get-tuple-element.41), channel_id=1, source_target_pairs={{0,80},{64,0},{16,64},{80,16},{1,81},{65,1},{17,65},{81,17},{2,82}... | collective-permute-start | bytes 737288 | tf_op jit(solution)/shard_map/ppermute | solution.py:270
  132.0 2.7 %collective-permute-start.10 = (bf16[96,1280]{1,0:T(8,128)(2,1)S(1)}, bf16[96,1280]{1,0:T(8,128)(2,1)S(1)}, u32[]{:S(2)}, u32[]{:S(2)}) collective-permute-start(bf16[96,1280]{1,0:T(8,128)(2,1)S(1)} %get-tuple-element.44), channel_id=1, source_target_pairs={{0,80},{64,0},{16,64},{80,16},{1,81},{65,1},{17,65},{81,17},{2,82}... | collective-permute-start | bytes 737288 | tf_op jit(solution)/shard_map/ppermute | solution.py:270
  134.6 1.7 %shard_map.67 = (f32[192,1280]{1,0:T(8,128)S(1)}, f32[192,1280]{1,0:T(8,128)S(1)}, f32[192,1280]{1,0:T(8,128)S(1)}, f32[192,1280]{1,0:T(8,128)S(1)}) custom-call(bf16[384,640]{1,0:T(8,128)(2,1)S(1)} %copy.121.rows_ref, bf16[640,5120]{1,0:T(8,128)(2,1)S(1)} %copy-done), custom_call_target="tpu_custom_call" | custom-call | flops 1258291200 | bytes 4000000 | tf_op jit(solution)/shard_map/pallas_call | solution.py:284
  136.4 0.3 collective-permute-start.11
  136.7 2.7 %collective-permute-start.13 = (bf16[96,1280]{1,0:T(8,128)(2,1)S(1)}, bf16[96,1280]{1,0:T(8,128)(2,1)S(1)}, u32[]{:S(2)}, u32[]{:S(2)}) collective-permute-start(bf16[96,1280]{1,0:T(8,128)(2,1)S(1)} %get-tuple-element.47), channel_id=1, source_target_pairs={{0,80},{64,0},{16,64},{80,16},{1,81},{65,1},{17,65},{81,17},{2,82}... | collective-permute-start | bytes 737288 | tf_op jit(solution)/shard_map/ppermute | solution.py:270
  139.3 0.1 select_convert_fusion.3
  139.4 0.1 collective-permute-start.14
  139.5 0.4 collective-permute-done.8
  139.9 3.5 %collective-permute-start.6 = (bf16[96,1280]{1,0:T(8,128)(2,1)S(1)}, bf16[96,1280]{1,0:T(8,128)(2,1)S(1)}, u32[]{:S(2)}, u32[]{:S(2)}) collective-permute-start(bf16[96,1280]{1,0:T(8,128)(2,1)S(1)} %select_convert_fusion.3), channel_id=1, source_target_pairs={{0,32},{32,0},{1,33},{33,1},{2,34},{34,2},{3,35},{35,3},{4,36},{36... | collective-permute-start | bytes 737288 | tf_op jit(solution)/shard_map/ppermute | solution.py:379
  143.4 0.1 select_convert_fusion.2
  143.5 2.9 %collective-permute-start.9 = (bf16[96,1280]{1,0:T(8,128)(2,1)S(1)}, bf16[96,1280]{1,0:T(8,128)(2,1)S(1)}, u32[]{:S(2)}, u32[]{:S(2)}) collective-permute-start(bf16[96,1280]{1,0:T(8,128)(2,1)S(1)} %select_convert_fusion.2), channel_id=1, source_target_pairs={{0,32},{32,0},{1,33},{33,1},{2,34},{34,2},{3,35},{35,3},{4,36},{36... | collective-permute-start | bytes 737288 | tf_op jit(solution)/shard_map/ppermute | solution.py:379
  146.4 0.1 select_convert_fusion.1
  146.5 3.1 %collective-permute-start.12 = (bf16[96,1280]{1,0:T(8,128)(2,1)S(1)}, bf16[96,1280]{1,0:T(8,128)(2,1)S(1)}, u32[]{:S(2)}, u32[]{:S(2)}) collective-permute-start(bf16[96,1280]{1,0:T(8,128)(2,1)S(1)} %select_convert_fusion.1), channel_id=1, source_target_pairs={{0,32},{32,0},{1,33},{33,1},{2,34},{34,2},{3,35},{35,3},{4,36},{36... | collective-permute-start | bytes 737288 | tf_op jit(solution)/shard_map/ppermute | solution.py:379
  149.5 1.0 collective-permute-done.14
  150.5 0.1 select_convert_fusion
  150.6 2.3 %collective-permute-start.15 = (bf16[96,1280]{1,0:T(8,128)(2,1)S(1)}, bf16[96,1280]{1,0:T(8,128)(2,1)S(1)}, u32[]{:S(2)}, u32[]{:S(2)}) collective-permute-start(bf16[96,1280]{1,0:T(8,128)(2,1)S(1)} %select_convert_fusion), channel_id=1, source_target_pairs={{0,32},{32,0},{1,33},{33,1},{2,34},{34,2},{3,35},{35,3},{4,36},{36... | collective-permute-start | bytes 737288 | tf_op jit(solution)/shard_map/ppermute | solution.py:379
  152.9 0.1 add_convert_fusion.3
  153.1 0.1 add_convert_fusion.2
  153.2 0.1 add_convert_fusion.1
  153.3 0.7 collective-permute-done.15
  154.1 0.1 add_convert_fusion
  154.2 1.0 pad_maximum_fusion.1
  (61 shorter events, 0.7 us)
Async XLA Ops:
  0.0 1.6 %copy-start.4 = (bf16[96,2560]{1,0:T(8,128)(2,1)S(1)}, bf16[96,2560]{1,0:T(8,128)(2,1)}, u32[]{:S(2)}) copy-start(bf16[96,2560]{1,0:T(8,128)(2,1)} %param.8) | copy-start | bytes 1474564
  3.2 10.6 %copy-start.5 = (bf16[96,2560]{1,0:T(8,128)(2,1)S(1)}, bf16[96,2560]{1,0:T(8,128)(2,1)}, u32[]{:S(2)}) copy-start(bf16[96,2560]{1,0:T(8,128)(2,1)} %param.6) | copy-start | bytes 1474564
  4.4 26.2 %all-to-all-start = ((bf16[32,128,128]{2,1,0:T(8,128)(2,1)}), bf16[32,128,128]{2,1,0:T(8,128)(2,1)S(1)}, u32[]{:S(2)}, u32[]{:S(2)}) async-start(bf16[32,128,128]{2,1,0:T(8,128)(2,1)} %pad_maximum_fusion), calls=%async_computation | async-start | bytes 2097152 | tf_op jit(solution)/shard_map/all_to_all | solution.py:346
  32.1 7.7 %copy-start.6 = (s32[20,96,16]{1,2,0:T(8,128)S(1)}, s32[20,96,16]{1,2,0:T(8,128)}, u32[]{:S(2)}) copy-start(s32[20,96,16]{1,2,0:T(8,128)} %param.9) | copy-start | bytes 368644
  32.1 27.6 %all-to-all-start.1 = ((bf16[32,2,96,128]{3,2,1,0:T(8,128)(2,1)}), bf16[32,2,96,128]{3,2,1,0:T(8,128)(2,1)}, u32[]{:S(2)}, u32[]{:S(2)}) async-start(bf16[32,2,96,128]{3,2,1,0:T(8,128)(2,1)} %bitcast.30), calls=%async_computation.1 | async-start | bytes 3145728 | tf_op jit(solution)/shard_map/all_to_all | solution.py:350
  36.9 25.7 %collective-permute-start = (bf16[8,4,128,128]{3,2,1,0:T(8,128)(2,1)S(1)}, bf16[8,4,128,128]{3,2,1,0:T(8,128)(2,1)S(1)}, u32[]{:S(2)}, u32[]{:S(2)}) collective-permute-start(bf16[8,4,128,128]{3,2,1,0:T(8,128)(2,1)S(1)} %bitcast.68), channel_id=1, source_target_pairs={{0,1},{1,2},{2,3},{3,0},{4,5},{5,6},{6,7},{7,4},{8,9},{9,10},{10,1... | collective-permute-start | bytes 3145736 | tf_op jit(solution)/shard_map/ppermute | solution.py:41
  38.2 24.4 %collective-permute-start.1 = (bf16[8,4,128,128]{3,2,1,0:T(8,128)(2,1)S(1)}, bf16[8,4,128,128]{3,2,1,0:T(8,128)(2,1)S(1)}, u32[]{:S(2)}, u32[]{:S(2)}) collective-permute-start(bf16[8,4,128,128]{3,2,1,0:T(8,128)(2,1)S(1)} %bitcast.69), channel_id=1, source_target_pairs={{0,3},{1,0},{2,1},{3,2},{4,7},{5,4},{6,5},{7,6},{8,11},{9,8},{10,9... | collective-permute-start | bytes 3145736 | tf_op jit(solution)/shard_map/ppermute | solution.py:45
  59.7 5.7 %copy-start.1 = (s32[5]{0:T(128)S(1)}, s32[5]{0:T(128)}, u32[]{:S(2)}) copy-start(s32[5]{0:T(128)} %stack.29.where_ref.refs_0_) | copy-start | bytes 64
  59.7 5.7 %copy-start.2 = (s32[96,16]{1,0:T(8,128)S(1)}, s32[96,16]{1,0:T(8,128)}, u32[]{:S(2)}) copy-start(s32[96,16]{1,0:T(8,128)} %get-tuple-element.29.refs_1_) | copy-start | bytes 18436
  59.7 5.7 %copy-start.3 = (s32[2,48]{1,0:T(2,128)S(1)}, s32[2,48]{1,0:T(2,128)}, u32[]{:S(2)}) copy-start(s32[2,48]{1,0:T(2,128)} %get-tuple-element.30.refs_2_) | copy-start | bytes 1156
  62.6 15.3 %collective-permute-start.2 = (bf16[8,4,64,128]{3,2,1,0:T(8,128)(2,1)S(1)}, bf16[8,4,64,128]{3,2,1,0:T(8,128)(2,1)S(1)}, u32[]{:S(2)}, u32[]{:S(2)}) collective-permute-start(bf16[8,4,64,128]{3,2,1,0:T(8,128)(2,1)S(1)} %slice.138), channel_id=1, source_target_pairs={{0,3},{1,0},{2,1},{3,2},{4,7},{5,4},{6,5},{7,6},{8,11},{9,8},{10,9... | collective-permute-start | bytes 1572872 | tf_op jit(solution)/shard_map/ppermute | solution.py:45
  65.3 13.0 %collective-permute-start.3 = (bf16[8,4,64,128]{3,2,1,0:T(8,128)(2,1)S(1)}, bf16[8,4,64,128]{3,2,1,0:T(8,128)(2,1)S(1)}, u32[]{:S(2)}, u32[]{:S(2)}) collective-permute-start(bf16[8,4,64,128]{3,2,1,0:T(8,128)(2,1)S(1)} %slice.139), channel_id=1, source_target_pairs={{0,1},{1,2},{2,3},{3,0},{4,5},{5,6},{6,7},{7,4},{8,9},{9,10},{10,1... | collective-permute-start | bytes 1572872 | tf_op jit(solution)/shard_map/ppermute | solution.py:41
  120.6 2.9 %copy-start = (bf16[640,5120]{1,0:T(8,128)(2,1)S(1)}, bf16[640,5120]{1,0:T(8,128)(2,1)}, u32[]{:S(2)}) copy-start(bf16[640,5120]{1,0:T(8,128)(2,1)} %w_ref.5) | copy-start | bytes 19660804
  124.2 12.1 %collective-permute-start.4 = (bf16[96,1280]{1,0:T(8,128)(2,1)S(1)}, bf16[96,1280]{1,0:T(8,128)(2,1)S(1)}, u32[]{:S(2)}, u32[]{:S(2)}) collective-permute-start(bf16[96,1280]{1,0:T(8,128)(2,1)S(1)} %get-tuple-element.38), channel_id=1, source_target_pairs={{0,80},{64,0},{16,64},{80,16},{1,81},{65,1},{17,65},{81,17},{2,82}... | collective-permute-start | bytes 737288 | tf_op jit(solution)/shard_map/ppermute | solution.py:270
  127.4 9.3 %collective-permute-start.5 = (bf16[96,1280]{1,0:T(8,128)(2,1)S(1)}, bf16[96,1280]{1,0:T(8,128)(2,1)S(1)}, u32[]{:S(2)}, u32[]{:S(2)}) collective-permute-start(bf16[96,1280]{1,0:T(8,128)(2,1)S(1)} %get-tuple-element.39), channel_id=1, source_target_pairs={{0,64},{64,16},{16,80},{80,0},{1,65},{65,17},{17,81},{81,1},{2,66}... | collective-permute-start | bytes 737288 | tf_op jit(solution)/shard_map/ppermute | solution.py:270
  129.2 10.2 %collective-permute-start.7 = (bf16[96,1280]{1,0:T(8,128)(2,1)S(1)}, bf16[96,1280]{1,0:T(8,128)(2,1)S(1)}, u32[]{:S(2)}, u32[]{:S(2)}) collective-permute-start(bf16[96,1280]{1,0:T(8,128)(2,1)S(1)} %get-tuple-element.41), channel_id=1, source_target_pairs={{0,80},{64,0},{16,64},{80,16},{1,81},{65,1},{17,65},{81,17},{2,82}... | collective-permute-start | bytes 737288 | tf_op jit(solution)/shard_map/ppermute | solution.py:270
  132.0 8.0 %collective-permute-start.8 = (bf16[96,1280]{1,0:T(8,128)(2,1)S(1)}, bf16[96,1280]{1,0:T(8,128)(2,1)S(1)}, u32[]{:S(2)}, u32[]{:S(2)}) collective-permute-start(bf16[96,1280]{1,0:T(8,128)(2,1)S(1)} %get-tuple-element.42), channel_id=1, source_target_pairs={{0,64},{64,16},{16,80},{80,0},{1,65},{65,17},{17,81},{81,1},{2,66}... | collective-permute-start | bytes 737288 | tf_op jit(solution)/shard_map/ppermute | solution.py:270
  132.0 11.5 %collective-permute-start.10 = (bf16[96,1280]{1,0:T(8,128)(2,1)S(1)}, bf16[96,1280]{1,0:T(8,128)(2,1)S(1)}, u32[]{:S(2)}, u32[]{:S(2)}) collective-permute-start(bf16[96,1280]{1,0:T(8,128)(2,1)S(1)} %get-tuple-element.44), channel_id=1, source_target_pairs={{0,80},{64,0},{16,64},{80,16},{1,81},{65,1},{17,65},{81,17},{2,82}... | collective-permute-start | bytes 737288 | tf_op jit(solution)/shard_map/ppermute | solution.py:270
  136.4 10.0 %collective-permute-start.11 = (bf16[96,1280]{1,0:T(8,128)(2,1)S(1)}, bf16[96,1280]{1,0:T(8,128)(2,1)S(1)}, u32[]{:S(2)}, u32[]{:S(2)}) collective-permute-start(bf16[96,1280]{1,0:T(8,128)(2,1)S(1)} %get-tuple-element.45), channel_id=1, source_target_pairs={{0,64},{64,16},{16,80},{80,0},{1,65},{65,17},{17,81},{81,1},{2,66}... | collective-permute-start | bytes 737288 | tf_op jit(solution)/shard_map/ppermute | solution.py:270
  136.7 12.9 %collective-permute-start.13 = (bf16[96,1280]{1,0:T(8,128)(2,1)S(1)}, bf16[96,1280]{1,0:T(8,128)(2,1)S(1)}, u32[]{:S(2)}, u32[]{:S(2)}) collective-permute-start(bf16[96,1280]{1,0:T(8,128)(2,1)S(1)} %get-tuple-element.47), channel_id=1, source_target_pairs={{0,80},{64,0},{16,64},{80,16},{1,81},{65,1},{17,65},{81,17},{2,82}... | collective-permute-start | bytes 737288 | tf_op jit(solution)/shard_map/ppermute | solution.py:270
  139.4 11.1 %collective-permute-start.14 = (bf16[96,1280]{1,0:T(8,128)(2,1)S(1)}, bf16[96,1280]{1,0:T(8,128)(2,1)S(1)}, u32[]{:S(2)}, u32[]{:S(2)}) collective-permute-start(bf16[96,1280]{1,0:T(8,128)(2,1)S(1)} %get-tuple-element.48), channel_id=1, source_target_pairs={{0,64},{64,16},{16,80},{80,0},{1,65},{65,17},{17,81},{81,1},{2,66}... | collective-permute-start | bytes 737288 | tf_op jit(solution)/shard_map/ppermute | solution.py:270
  139.9 13.0 %collective-permute-start.6 = (bf16[96,1280]{1,0:T(8,128)(2,1)S(1)}, bf16[96,1280]{1,0:T(8,128)(2,1)S(1)}, u32[]{:S(2)}, u32[]{:S(2)}) collective-permute-start(bf16[96,1280]{1,0:T(8,128)(2,1)S(1)} %select_convert_fusion.3), channel_id=1, source_target_pairs={{0,32},{32,0},{1,33},{33,1},{2,34},{34,2},{3,35},{35,3},{4,36},{36... | collective-permute-start | bytes 737288 | tf_op jit(solution)/shard_map/ppermute | solution.py:379
  143.5 9.5 %collective-permute-start.9 = (bf16[96,1280]{1,0:T(8,128)(2,1)S(1)}, bf16[96,1280]{1,0:T(8,128)(2,1)S(1)}, u32[]{:S(2)}, u32[]{:S(2)}) collective-permute-start(bf16[96,1280]{1,0:T(8,128)(2,1)S(1)} %select_convert_fusion.2), channel_id=1, source_target_pairs={{0,32},{32,0},{1,33},{33,1},{2,34},{34,2},{3,35},{35,3},{4,36},{36... | collective-permute-start | bytes 737288 | tf_op jit(solution)/shard_map/ppermute | solution.py:379
  146.5 6.7 %collective-permute-start.12 = (bf16[96,1280]{1,0:T(8,128)(2,1)S(1)}, bf16[96,1280]{1,0:T(8,128)(2,1)S(1)}, u32[]{:S(2)}, u32[]{:S(2)}) collective-permute-start(bf16[96,1280]{1,0:T(8,128)(2,1)S(1)} %select_convert_fusion.1), channel_id=1, source_target_pairs={{0,32},{32,0},{1,33},{33,1},{2,34},{34,2},{3,35},{35,3},{4,36},{36... | collective-permute-start | bytes 737288 | tf_op jit(solution)/shard_map/ppermute | solution.py:379
  150.6 3.5 %collective-permute-start.15 = (bf16[96,1280]{1,0:T(8,128)(2,1)S(1)}, bf16[96,1280]{1,0:T(8,128)(2,1)S(1)}, u32[]{:S(2)}, u32[]{:S(2)}) collective-permute-start(bf16[96,1280]{1,0:T(8,128)(2,1)S(1)} %select_convert_fusion), channel_id=1, source_target_pairs={{0,32},{32,0},{1,33},{33,1},{2,34},{34,2},{3,35},{35,3},{4,36},{36... | collective-permute-start | bytes 737288 | tf_op jit(solution)/shard_map/ppermute | solution.py:379

commit v6 on v5

--- a/solution.py
+++ b/solution.py
@@ -122,6 +122,7 @@
             loads += [(source, 0, i, k_main, k_ext), (source, PART, i, v_main, v_ext)]
     stage = 1 if last else 0
     first = not last
+    state = (top_ref, tot_ref, acc_ref)
     copies = []
     for source, lo, piece, main, ext in loads:
         for target, at, rows in ((main, lo, MAIN), (ext, lo + MAIN, EXT)):
@@ -131,17 +132,6 @@
             copy.start()
             copies.append(copy)
 
-    def begin(unit, carry):
-        if first:
-            top_ref[unit] = jnp.full((BLOCK, HEAD), FLOOR, jnp.float32)
-            tot_ref[unit] = jnp.zeros((BLOCK, HEAD), jnp.float32)
-            acc_ref[unit] = jnp.zeros((BLOCK, HEAD), jnp.float32)
-        else:
-            for old, new in zip(before, (top_ref, tot_ref, acc_ref)):
-                new[unit] = old[unit]
-        return carry
-
-    lax.fori_loop(0, 2 * UNITS, begin, 0)
     for copy in copies:
         copy.wait()
 
@@ -159,40 +149,48 @@
         ns = [n_ref[stage, unit] for unit in units]
         most = functools.reduce(jnp.maximum, ns)
 
-        def step(t, carry):
-            col = lax.broadcasted_iota(jnp.int32, (BLOCK, group * width), 1)
+        def step(t, carry, start=False):
+            col = lax.broadcasted_iota(jnp.int32, (1, group * width), 1)
             values, scores = [], []
             for unit, n in zip(units, ns):
                 starts = []
                 for i in range(group):
                     slot = jnp.maximum(jnp.minimum(group * t + i, n - 1), 0)
-                    start = start_ref[stage * 2 * UNITS + unit, slot]
-                    starts.append(pl.multiple_of(start, width))
+                    at = start_ref[stage * 2 * UNITS + unit, slot]
+                    starts.append(pl.multiple_of(at, width))
                 keys = jnp.concatenate([key_flat[pl.ds(r, width), :] for r in starts], axis=0)
                 values.append(
                     jnp.concatenate([value_flat[pl.ds(r, width), :] for r in starts], axis=0)
                 )
-                s = dot_t(q_ref[unit], keys)
-                scores.append(jnp.where(col < (n - group * t) * width, s, 2 * FLOOR))
+                bias = jnp.where(col < (n - group * t) * width, 0.0, 2 * FLOOR)
+                scores.append(dot_t(q_ref[unit], keys) + bias)
             for unit, s, v in zip(units, scores, values):
-                top = top_ref[unit][:, :1]
-                new_top = jnp.maximum(top, jnp.max(s, axis=1, keepdims=True))
-                p = jnp.exp2((s - new_top) * SCALE)
-                alpha = jnp.exp2((top - new_top) * SCALE)
-                part = functools.reduce(
-                    jnp.add, [p[:, i : i + HEAD] for i in range(0, group * width, HEAD)]
-                )
-                product = jnp.dot(p.astype(jnp.bfloat16), v, preferred_element_type=jnp.float32)
-                top_ref[unit] = jnp.broadcast_to(new_top, (BLOCK, HEAD))
-                tot_ref[unit] = tot_ref[unit] * alpha + part
-                acc_ref[unit] = acc_ref[unit] * alpha + product
+                parts = [s[:, i : i + HEAD] for i in range(0, group * width, HEAD)]
+                peak = jnp.max(functools.reduce(jnp.maximum, parts), axis=1, keepdims=True)
+                if start and first:
+                    new_top = jnp.maximum(jnp.broadcast_to(peak, (BLOCK, HEAD)), FLOOR)
+                else:
+                    top, tot, acc = [ref[unit] for ref in (before if start else state)]
+                    new_top = jnp.maximum(top, peak)
+                weights = [jnp.exp2((part - new_top) * SCALE) for part in parts]
+                low = jnp.concatenate([w.astype(jnp.bfloat16) for w in weights], axis=1)
+                product = jnp.dot(low, v, preferred_element_type=jnp.float32)
+                total = functools.reduce(jnp.add, weights)
+                if not (start and first):
+                    alpha = jnp.exp2((top - new_top) * SCALE)
+                    total = tot * alpha + total
+                    product = acc * alpha + product
+                top_ref[unit] = new_top
+                tot_ref[unit] = total
+                acc_ref[unit] = product
             return carry
 
-        lax.fori_loop(0, lax.div(most + (group - 1), group), step, 0)
+        step(0, 0, True)
+        lax.fori_loop(1, lax.div(most + (group - 1), group), step, 0)
 
     def finish(unit):
         total = jnp.sum(tot_ref[unit], axis=1, keepdims=True)
-        return top_ref[unit][:, :1], total, (acc_ref[unit] / total).astype(jnp.bfloat16)
+        return top_ref[unit], total, (acc_ref[unit] / total).astype(jnp.bfloat16)
 
     def store(sb, r, top, value):
         for i in range(4):
@@ -270,28 +268,45 @@
     return lax.ppermute(x, ("xl", "xh"), [(index(i), index(i + step)) for i in range(4)])
 
 
-def project_kernel(parts, rows_ref, w_ref, *outs):
-    for (chunk, lo, count), out in zip(parts, outs):
-        rows = rows_ref[pl.ds(lo, count), :]
-        for at in range(0, WIDTH, 256):
-            product = jnp.dot(
-                rows, w_ref[:, pl.ds(chunk * WIDTH + at, 256)], preferred_element_type=jnp.float32
-            )
-            out[:, pl.ds(at, 256)] = product.astype(out.dtype)
+def project_kernel(parts, rows_ref, w_ref, *refs):
+    outs, (w_buf, sem) = refs[:-2], refs[-2:]
+    chunks = sorted({chunk for chunk, _, _ in parts})
+    copies = {}
+    for i, chunk in enumerate(chunks):
+        copies[chunk] = pltpu.make_async_copy(
+            w_ref.at[:, pl.ds(chunk * WIDTH, WIDTH)], w_buf.at[i], sem.at[i]
+        )
+        copies[chunk].start()
+    for i, chunk in enumerate(chunks):
+        copies[chunk].wait()
+        for (which, lo, count), out in zip(parts, outs):
+            if which != chunk:
+                continue
+            rows = rows_ref[pl.ds(lo, count), :]
+            for at in range(0, WIDTH, 256):
+                product = jnp.dot(
+                    rows, w_buf[i, :, pl.ds(at, 256)], preferred_element_type=jnp.float32
+                )
+                out[:, pl.ds(at, 256)] = product.astype(out.dtype)
 
 
 def project_parts(rows, w, parts):
+    chunks = len({chunk for chunk, _, _ in parts})
     return pl.pallas_call(
         functools.partial(project_kernel, parts),
         out_shape=tuple(
             jax.ShapeDtypeStruct((count, WIDTH), jnp.float32 if lo == 0 else jnp.bfloat16)
             for _, lo, count in parts
         ),
-        in_specs=[VMEM, VMEM],
+        in_specs=[VMEM, HBM],
         out_specs=(VMEM,) * len(parts),
-        compiler_params=pltpu.CompilerParams(vmem_limit_bytes=24 * 1024 * 1024),
+        scratch_shapes=[
+            pltpu.VMEM((chunks, w.shape[0], WIDTH), w.dtype),
+            pltpu.SemaphoreType.DMA((chunks,)),
+        ],
+        compiler_params=pltpu.CompilerParams(vmem_limit_bytes=52 * 1024 * 1024),
         cost_estimate=pl.CostEstimate(
-            flops=sum(2 * count * WIDTH * 640 for _, _, count in parts),
+            flops=sum(2 * count * WIDTH * w.shape[0] for _, _, count in parts),
             bytes_accessed=4_000_000,
             transcendentals=0,
         ),

time: 156 us -> 151 us (0.968)
  Pallas kernels: 39.6 us -> 43.2 us
  local copies, waits for them, and re-layouts: 12.6 us -> 9.8 us
  starting transfers between devices: 43.1 us -> 40.4 us
  waiting for transfers between devices: 24.8 us -> 22.4 us
  blocking collectives: 30 us -> 28.3 us
    pallas_call x3, Pallas kernels: 4.24 us -> 10.7 us  [project_parts(): pl.pallas_call(functools.partial(project_kernel, parts), out_shape=tuple(...]
    pallas_call x2, Pallas kernels: 22.9 us -> 17 us  [attend(): pl.pallas_call(functools.partial(stage_kernel, last, pieces), out_shape=o...]
    all_to_all x1, waiting for transfers between devices: 5.56 us -> 2.47 us  [per_device(): q = lax.all_to_all(q.reshape(32, 2, ROWS, HEAD), SPREAD, 0, 0, tiled=True)]
    pallas_call x1, Pallas kernels: 12.4 us -> 15.5 us  [plan(): pl.pallas_call(plan_kernel, out_shape=(jax.ShapeDtypeStruct((4 * UNITS, S...]
    unnamed x19 -> x23, local copies, waits for them, and re-layouts: 6.22 us -> 3.38 us
    ppermute x2, waiting for transfers between devices: 1.71 us -> 3.8 us  [ring_up(): return lax.ppermute(x, 'y', [(i, (i + 1) % 4) for i in range(4)])]
    ppermute x8, starting transfers between devices: 11.6 us -> 9.73 us  [around(): lax.ppermute(x, ('xl', 'xh'), [(index(i), index(i + step)) for i in range...]
    all_to_all x1, blocking collectives: 30 us -> 28.3 us  [per_device(): out = lax.all_to_all(out, ('xh', 'zh', 'zl'), 0, 0, tiled=True)]
  transfers between devices with their start and end apart: 18 -> 18, of which waited for: 7 -> 5; matrix products, arithmetic and copies ran while one was open for 4% -> 5% of each run, Pallas kernels for 18% -> 23%
where the time goes in v6:
time: 151 us; the launch traced here: 150 us
  Pallas kernels  43.2 us (29%)
  starting transfers between devices  40.4 us (27%)
  blocking collectives  28.3 us (19%)
  waiting for transfers between devices  22.4 us (15%)
  local copies, waits for them, and re-layouts  9.8 us (6%)
  other arithmetic  5.67 us (4%)
    all_to_all x1, blocking collectives, per_device(): out = lax.all_to_all(out, ('xh', 'zh', 'zl'), 0, 0, tiled=True)  28.3 us
    pallas_call x2, Pallas kernels, attend(): pl.pallas_call(functools.partial(stage_kernel, last, pieces), out_shape=o...  17 us
    pallas_call x1, Pallas kernels, plan(): pl.pallas_call(plan_kernel, out_shape=(jax.ShapeDtypeStruct((4 * UNITS, S...  15.5 us
    all_to_all x1, waiting for transfers between devices, per_device(): lax.all_to_all(sent, SPREAD, 0, 0, tiled=True)  15.4 us
    ppermute x4, starting transfers between devices, per_device(): lax.ppermute(give, 'c', [(0, 1), (1, 0)])  10.9 us
    pallas_call x3, Pallas kernels, project_parts(): pl.pallas_call(functools.partial(project_kernel, parts), out_shape=tuple(...  10.7 us
    ppermute x8, starting transfers between devices, around(): lax.ppermute(x, ('xl', 'xh'), [(index(i), index(i + step)) for i in range...  9.73 us
    all_to_all x1, starting transfers between devices, per_device(): lax.all_to_all(sent, SPREAD, 0, 0, tiled=True)  9.43 us
  transfers between devices with their start and end apart: 18, of which 5 were waited for; matrix products, arithmetic and copies ran while one was open for 5% of the time, Pallas kernels for 23%

profile of v6, /device:TPU:1, one launch (start us, length us, event | category | flops | bytes accessed | tf_op | source)
XLA Modules:
  0.0 150.5 jit_solution(3310133312358577581)
XLA Ops:
  0.0 1.4 copy.100
  1.4 0.1 copy.103
  1.6 0.3 copy.106
  2.0 0.1 copy.109
  2.1 0.1 copy.104
  2.3 0.1 copy.110
  2.7 0.2 copy.107
  3.0 0.2 copy.101
  3.2 0.0 copy-start.7
  3.3 1.1 pad_maximum_fusion
  4.4 9.4 %all-to-all-start = ((bf16[32,128,128]{2,1,0:T(8,128)(2,1)}), bf16[32,128,128]{2,1,0:T(8,128)(2,1)S(1)}, u32[]{:S(2)}, u32[]{:S(2)}) async-start(bf16[32,128,128]{2,1,0:T(8,128)(2,1)} %pad_maximum_fusion), calls=%async_computation | async-start | bytes 2097152 | tf_op jit(solution)/shard_map/all_to_all | solution.py:361
  13.8 0.3 copy.112
  14.2 0.1 stack_broadcast_in_dim.8
  14.3 0.2 maximum_bitcast_fusion
  14.6 0.6 copy.115
  15.1 15.4 %all-to-all-done = bf16[32,128,128]{2,1,0:T(8,128)(2,1)S(1)} async-done(((bf16[32,128,128]{2,1,0:T(8,128)(2,1)}), bf16[32,128,128]{2,1,0:T(8,128)(2,1)S(1)}, u32[]{:S(2)}, u32[]{:S(2)}) %all-to-all-start) | async-done | bytes 1048608 | tf_op jit(solution)/shard_map/all_to_all | solution.py:361
  30.5 1.5 %broadcast_in_dim.2 = bf16[4,2,4,2,96,128]{5,4,3,2,1,0:T(8,128)(2,1)} broadcast(bf16[4,4,2,96,128]{4,3,2,1,0:T(8,128)(2,1)S(1)} %copy.115), dimensions={0,2,3,4,5} | broadcast | bytes 2359296 | tf_op jit(solution)/shard_map/broadcast_in_dim | solution.py:364
  32.1 4.8 %all-to-all-start.1 = ((bf16[32,2,96,128]{3,2,1,0:T(8,128)(2,1)}), bf16[32,2,96,128]{3,2,1,0:T(8,128)(2,1)}, u32[]{:S(2)}, u32[]{:S(2)}) async-start(bf16[32,2,96,128]{3,2,1,0:T(8,128)(2,1)} %bitcast.30), calls=%async_computation.1 | async-start | bytes 3145728 | tf_op jit(solution)/shard_map/all_to_all | solution.py:365
  36.9 1.4 collective-permute-start
  38.2 1.5 %collective-permute-start.1 = (bf16[8,4,128,128]{3,2,1,0:T(8,128)(2,1)S(1)}, bf16[8,4,128,128]{3,2,1,0:T(8,128)(2,1)S(1)}, u32[]{:S(2)}, u32[]{:S(2)}) collective-permute-start(bf16[8,4,128,128]{3,2,1,0:T(8,128)(2,1)S(1)} %bitcast.69), channel_id=1, source_target_pairs={{0,3},{1,0},{2,1},{3,2},{4,7},{5,4},{6,5},{7,6},{8,11},{9,8},{10,9... | collective-permute-start | bytes 3145736 | tf_op jit(solution)/shard_map/ppermute | solution.py:45
  39.7 1.3 copy.117.table_ref
  41.0 0.7 stack.29.where_ref.refs_0_
  41.7 15.5 %shard_map.64 = (s32[96,16]{1,0:T(8,128)}, s32[2,48]{1,0:T(2,128)}) custom-call(s32[5]{0:T(128)} %stack.29.where_ref.refs_0_, s32[20,96]{1,0:T(8,128)} %count_ref.1, s32[20,96,16]{2,1,0:T(8,128)} %copy.117.table_ref), custom_call_target="tpu_custom_call" | custom-call | flops 8000000000 | bytes 100000 | tf_op jit(solution)/shard_map/pallas_call | solution.py:96
  57.2 2.5 %all-to-all-done.1 = bf16[32,2,96,128]{3,2,1,0:T(8,128)(2,1)} async-done(((bf16[32,2,96,128]{3,2,1,0:T(8,128)(2,1)}), bf16[32,2,96,128]{3,2,1,0:T(8,128)(2,1)}, u32[]{:S(2)}, u32[]{:S(2)}) %all-to-all-start.1) | async-done | bytes 1572896 | tf_op jit(solution)/shard_map/all_to_all | solution.py:365
  59.7 1.6 %copy.116 = bf16[8,4,2,96,128]{4,3,1,0,2:T(8,128)(2,1)S(1)} copy(bf16[8,4,2,96,128]{4,3,2,1,0:T(8,128)(2,1)} %bitcast.31) | data formatting | bytes 3145728 | tf_op jit(solution)/shard_map/reshape | solution.py:366
  61.3 1.3 collective-permute-done.refs_5_
  62.6 0.0 collective-permute-done.1.refs_6_
  62.6 2.6 %collective-permute-start.2 = (bf16[8,4,64,128]{3,2,1,0:T(8,128)(2,1)S(1)}, bf16[8,4,64,128]{3,2,1,0:T(8,128)(2,1)S(1)}, u32[]{:S(2)}, u32[]{:S(2)}) collective-permute-start(bf16[8,4,64,128]{3,2,1,0:T(8,128)(2,1)S(1)} %slice.138), channel_id=1, source_target_pairs={{0,3},{1,0},{2,1},{3,2},{4,7},{5,4},{6,5},{7,6},{8,11},{9,8},{10,9... | collective-permute-start | bytes 1572872 | tf_op jit(solution)/shard_map/ppermute | solution.py:45
  65.3 0.1 collective-permute-start.3
  65.4 10.4 %shard_map.65 = (f32[48,128,128]{2,1,0:T(8,128)S(1)}, f32[48,128,128]{2,1,0:T(8,128)S(1)}, f32[48,128,128]{2,1,0:T(8,128)S(1)}) custom-call(s32[5]{0:T(128)S(1)} %copy-done, s32[96,16]{1,0:T(8,128)S(1)} %copy-done.1, s32[2,48]{1,0:T(2,128)S(1)} %copy-done.2, bf16[48,128,128]{2,1,0:T(8,128)(2,1)S(1)} %bitcast.66, bf16[8,4,128,128]{3,2,1,0:T(8,128)(2,1)S(1)} %bitcast.70, ...), custom_call_target="tpu_custom_call" | custom-call | flops 15000000512 | bytes 6000000 | tf_op jit(solution)/shard_map/pallas_call | solution.py:253
  75.8 2.5 %collective-permute-done.3.refs_8_ = bf16[8,4,64,128]{3,2,1,0:T(8,128)(2,1)S(1)} collective-permute-done((bf16[8,4,64,128]{3,2,1,0:T(8,128)(2,1)S(1)}, bf16[8,4,64,128]{3,2,1,0:T(8,128)(2,1)S(1)}, u32[]{:S(2)}, u32[]{:S(2)}) %collective-permute-start.3) | collective-permute-done | bytes 524320 | tf_op jit(solution)/shard_map/ppermute | solution.py:41
  78.3 6.6 %shard_map.66 = bf16[8,816,128]{2,1,0:T(8,128)(2,1)S(1)} custom-call(s32[5]{0:T(128)S(1)} %copy-done, s32[96,16]{1,0:T(8,128)S(1)} %copy-done.1, s32[2,48]{1,0:T(2,128)S(1)} %copy-done.2, bf16[48,128,128]{2,1,0:T(8,128)(2,1)S(1)} %bitcast.67, f32[48,128,128]{2,1,0:T(8,128)S(1)} %get-tuple-element.34.refs_4_, f32[48,128,128]{2,1,0:T(8,128)S(1)} %get-tuple-element.35.refs_5_, ...), custom_call_target="tpu_custom_call" | custom-call | flops 5000000000 | bytes 2000000 | tf_op jit(solution)/shard_map/pallas_call | solution.py:253
  84.9 28.3 %all_to_all.15 = bf16[8,816,128]{2,1,0:T(8,128)(2,1)S(1)} all-to-all(bf16[8,816,128]{2,1,0:T(8,128)(2,1)S(1)} %shard_map.66), channel_id=1, replica_groups=mesh['xl'=2,'c'=2,'xh'=2,'zh'=2,'zl'=2,'y'=4] {'xh','zh','zl'}, dimensions={0} | all-to-all | bytes 3342336 | tf_op jit(solution)/shard_map/all_to_all | solution.py:377
  113.3 0.1 fusion.12
  113.4 0.1 maximum_select_fusion.4
  113.6 0.5 fusion.1
  114.1 0.5 multiply_reduce_fusion
  114.6 0.3 copy.120
  114.9 0.3 copy.121.rows_ref
  115.1 2.1 %shard_map.68 = (bf16[96,1280]{1,0:T(8,128)(2,1)S(1)}, bf16[96,1280]{1,0:T(8,128)(2,1)S(1)}) custom-call(bf16[384,640]{1,0:T(8,128)(2,1)S(1)} %copy.121.rows_ref, bf16[640,5120]{1,0:T(8,128)(2,1)} %w_ref.5), custom_call_target="tpu_custom_call" | custom-call | flops 314572800 | bytes 4000000 | tf_op jit(solution)/shard_map/pallas_call | solution.py:295
  117.3 1.5 collective-permute-start.4
  118.8 0.6 collective-permute-start.5
  119.4 3.5 %shard_map.69 = (bf16[96,1280]{1,0:T(8,128)(2,1)S(1)}, bf16[96,1280]{1,0:T(8,128)(2,1)S(1)}, bf16[96,1280]{1,0:T(8,128)(2,1)S(1)}, bf16[96,1280]{1,0:T(8,128)(2,...) custom-call(bf16[384,640]{1,0:T(8,128)(2,1)S(1)} %copy.121.rows_ref, bf16[640,5120]{1,0:T(8,128)(2,1)} %w_ref.5), custom_call_target="tpu_custom_call" | custom-call | flops 943718400 | bytes 4000000 | tf_op jit(solution)/shard_map/pallas_call | solution.py:295
  122.9 2.2 %collective-permute-start.7 = (bf16[96,1280]{1,0:T(8,128)(2,1)S(1)}, bf16[96,1280]{1,0:T(8,128)(2,1)S(1)}, u32[]{:S(2)}, u32[]{:S(2)}) collective-permute-start(bf16[96,1280]{1,0:T(8,128)(2,1)S(1)} %get-tuple-element.41), channel_id=1, source_target_pairs={{0,80},{64,0},{16,64},{80,16},{1,81},{65,1},{17,65},{81,17},{2,82}... | collective-permute-start | bytes 737288 | tf_op jit(solution)/shard_map/ppermute | solution.py:268
  125.1 2.7 %collective-permute-start.10 = (bf16[96,1280]{1,0:T(8,128)(2,1)S(1)}, bf16[96,1280]{1,0:T(8,128)(2,1)S(1)}, u32[]{:S(2)}, u32[]{:S(2)}) collective-permute-start(bf16[96,1280]{1,0:T(8,128)(2,1)S(1)} %get-tuple-element.44), channel_id=1, source_target_pairs={{0,80},{64,0},{16,64},{80,16},{1,81},{65,1},{17,65},{81,17},{2,82}... | collective-permute-start | bytes 737288 | tf_op jit(solution)/shard_map/ppermute | solution.py:268
  127.8 5.1 %shard_map.67 = (f32[192,1280]{1,0:T(8,128)S(1)}, f32[192,1280]{1,0:T(8,128)}, f32[192,1280]{1,0:T(8,128)}, f32[192,1280]{1,0:T(8,128)}) custom-call(bf16[384,640]{1,0:T(8,128)(2,1)S(1)} %copy.121.rows_ref, bf16[640,5120]{1,0:T(8,128)(2,1)} %w_ref.5), custom_call_target="tpu_custom_call" | custom-call | flops 1258291200 | bytes 4000000 | tf_op jit(solution)/shard_map/pallas_call | solution.py:295
  132.8 0.1 collective-permute-start.11
  132.9 2.7 %collective-permute-start.13 = (bf16[96,1280]{1,0:T(8,128)(2,1)S(1)}, bf16[96,1280]{1,0:T(8,128)(2,1)S(1)}, u32[]{:S(2)}, u32[]{:S(2)}) collective-permute-start(bf16[96,1280]{1,0:T(8,128)(2,1)S(1)} %get-tuple-element.47), channel_id=1, source_target_pairs={{0,80},{64,0},{16,64},{80,16},{1,81},{65,1},{17,65},{81,17},{2,82}... | collective-permute-start | bytes 737288 | tf_op jit(solution)/shard_map/ppermute | solution.py:268
  135.6 0.1 select_convert_fusion.3
  135.7 0.1 collective-permute-start.14
  135.8 4.7 %collective-permute-start.6 = (bf16[96,1280]{1,0:T(8,128)(2,1)S(1)}, bf16[96,1280]{1,0:T(8,128)(2,1)S(1)}, u32[]{:S(2)}, u32[]{:S(2)}) collective-permute-start(bf16[96,1280]{1,0:T(8,128)(2,1)S(1)} %select_convert_fusion.3), channel_id=1, source_target_pairs={{0,32},{32,0},{1,33},{33,1},{2,34},{34,2},{3,35},{35,3},{4,36},{36... | collective-permute-start | bytes 737288 | tf_op jit(solution)/shard_map/ppermute | solution.py:394
  140.5 1.3 select_convert_fusion.2
  141.8 0.2 collective-permute-start.9
  142.0 0.1 select_convert_fusion.1
  142.1 0.0 copy-start.5
  142.1 3.4 %collective-permute-start.12 = (bf16[96,1280]{1,0:T(8,128)(2,1)S(1)}, bf16[96,1280]{1,0:T(8,128)(2,1)S(1)}, u32[]{:S(2)}, u32[]{:S(2)}) collective-permute-start(bf16[96,1280]{1,0:T(8,128)(2,1)S(1)} %select_convert_fusion.1), channel_id=1, source_target_pairs={{0,32},{32,0},{1,33},{33,1},{2,34},{34,2},{3,35},{35,3},{4,36},{36... | collective-permute-start | bytes 737288 | tf_op jit(solution)/shard_map/ppermute | solution.py:394
  145.6 0.1 select_convert_fusion
  145.7 2.5 %collective-permute-start.15 = (bf16[96,1280]{1,0:T(8,128)(2,1)S(1)}, bf16[96,1280]{1,0:T(8,128)(2,1)S(1)}, u32[]{:S(2)}, u32[]{:S(2)}) collective-permute-start(bf16[96,1280]{1,0:T(8,128)(2,1)S(1)} %select_convert_fusion), channel_id=1, source_target_pairs={{0,32},{32,0},{1,33},{33,1},{2,34},{34,2},{3,35},{35,3},{4,36},{36... | collective-permute-start | bytes 737288 | tf_op jit(solution)/shard_map/ppermute | solution.py:394
  148.2 0.1 add_convert_fusion.3
  148.3 0.1 add_convert_fusion.2
  148.5 0.1 add_convert_fusion.1
  148.6 0.7 collective-permute-done.15
  149.3 0.1 add_convert_fusion
  149.4 1.0 pad_maximum_fusion.1
  (65 shorter events, 0.7 us)
Async XLA Ops:
  0.0 1.6 %copy-start.6 = (bf16[96,2560]{1,0:T(8,128)(2,1)S(1)}, bf16[96,2560]{1,0:T(8,128)(2,1)}, u32[]{:S(2)}) copy-start(bf16[96,2560]{1,0:T(8,128)(2,1)} %param.8) | copy-start | bytes 1474564
  3.2 10.6 %copy-start.7 = (bf16[96,2560]{1,0:T(8,128)(2,1)S(1)}, bf16[96,2560]{1,0:T(8,128)(2,1)}, u32[]{:S(2)}) copy-start(bf16[96,2560]{1,0:T(8,128)(2,1)} %param.6) | copy-start | bytes 1474564
  4.4 26.2 %all-to-all-start = ((bf16[32,128,128]{2,1,0:T(8,128)(2,1)}), bf16[32,128,128]{2,1,0:T(8,128)(2,1)S(1)}, u32[]{:S(2)}, u32[]{:S(2)}) async-start(bf16[32,128,128]{2,1,0:T(8,128)(2,1)} %pad_maximum_fusion), calls=%async_computation | async-start | bytes 2097152 | tf_op jit(solution)/shard_map/all_to_all | solution.py:361
  32.1 7.7 %copy-start.8 = (s32[20,96,16]{1,2,0:T(8,128)S(1)}, s32[20,96,16]{1,2,0:T(8,128)}, u32[]{:S(2)}) copy-start(s32[20,96,16]{1,2,0:T(8,128)} %param.9) | copy-start | bytes 368644
  32.1 27.6 %all-to-all-start.1 = ((bf16[32,2,96,128]{3,2,1,0:T(8,128)(2,1)}), bf16[32,2,96,128]{3,2,1,0:T(8,128)(2,1)}, u32[]{:S(2)}, u32[]{:S(2)}) async-start(bf16[32,2,96,128]{3,2,1,0:T(8,128)(2,1)} %bitcast.30), calls=%async_computation.1 | async-start | bytes 3145728 | tf_op jit(solution)/shard_map/all_to_all | solution.py:365
  36.9 25.7 %collective-permute-start = (bf16[8,4,128,128]{3,2,1,0:T(8,128)(2,1)S(1)}, bf16[8,4,128,128]{3,2,1,0:T(8,128)(2,1)S(1)}, u32[]{:S(2)}, u32[]{:S(2)}) collective-permute-start(bf16[8,4,128,128]{3,2,1,0:T(8,128)(2,1)S(1)} %bitcast.68), channel_id=1, source_target_pairs={{0,1},{1,2},{2,3},{3,0},{4,5},{5,6},{6,7},{7,4},{8,9},{9,10},{10,1... | collective-permute-start | bytes 3145736 | tf_op jit(solution)/shard_map/ppermute | solution.py:41
  38.2 24.4 %collective-permute-start.1 = (bf16[8,4,128,128]{3,2,1,0:T(8,128)(2,1)S(1)}, bf16[8,4,128,128]{3,2,1,0:T(8,128)(2,1)S(1)}, u32[]{:S(2)}, u32[]{:S(2)}) collective-permute-start(bf16[8,4,128,128]{3,2,1,0:T(8,128)(2,1)S(1)} %bitcast.69), channel_id=1, source_target_pairs={{0,3},{1,0},{2,1},{3,2},{4,7},{5,4},{6,5},{7,6},{8,11},{9,8},{10,9... | collective-permute-start | bytes 3145736 | tf_op jit(solution)/shard_map/ppermute | solution.py:45
  59.7 5.7 %copy-start = (s32[5]{0:T(128)S(1)}, s32[5]{0:T(128)}, u32[]{:S(2)}) copy-start(s32[5]{0:T(128)} %stack.29.where_ref.refs_0_) | copy-start | bytes 64
  59.7 5.7 %copy-start.1 = (s32[96,16]{1,0:T(8,128)S(1)}, s32[96,16]{1,0:T(8,128)}, u32[]{:S(2)}) copy-start(s32[96,16]{1,0:T(8,128)} %get-tuple-element.29.refs_1_) | copy-start | bytes 18436
  59.7 5.7 %copy-start.2 = (s32[2,48]{1,0:T(2,128)S(1)}, s32[2,48]{1,0:T(2,128)}, u32[]{:S(2)}) copy-start(s32[2,48]{1,0:T(2,128)} %get-tuple-element.30.refs_2_) | copy-start | bytes 1156
  62.6 13.2 %collective-permute-start.2 = (bf16[8,4,64,128]{3,2,1,0:T(8,128)(2,1)S(1)}, bf16[8,4,64,128]{3,2,1,0:T(8,128)(2,1)S(1)}, u32[]{:S(2)}, u32[]{:S(2)}) collective-permute-start(bf16[8,4,64,128]{3,2,1,0:T(8,128)(2,1)S(1)} %slice.138), channel_id=1, source_target_pairs={{0,3},{1,0},{2,1},{3,2},{4,7},{5,4},{6,5},{7,6},{8,11},{9,8},{10,9... | collective-permute-start | bytes 1572872 | tf_op jit(solution)/shard_map/ppermute | solution.py:45
  65.3 13.0 %collective-permute-start.3 = (bf16[8,4,64,128]{3,2,1,0:T(8,128)(2,1)S(1)}, bf16[8,4,64,128]{3,2,1,0:T(8,128)(2,1)S(1)}, u32[]{:S(2)}, u32[]{:S(2)}) collective-permute-start(bf16[8,4,64,128]{3,2,1,0:T(8,128)(2,1)S(1)} %slice.139), channel_id=1, source_target_pairs={{0,1},{1,2},{2,3},{3,0},{4,5},{5,6},{6,7},{7,4},{8,9},{9,10},{10,1... | collective-permute-start | bytes 1572872 | tf_op jit(solution)/shard_map/ppermute | solution.py:41
  117.3 15.6 %collective-permute-start.4 = (bf16[96,1280]{1,0:T(8,128)(2,1)S(1)}, bf16[96,1280]{1,0:T(8,128)(2,1)S(1)}, u32[]{:S(2)}, u32[]{:S(2)}) collective-permute-start(bf16[96,1280]{1,0:T(8,128)(2,1)S(1)} %get-tuple-element.38), channel_id=1, source_target_pairs={{0,80},{64,0},{16,64},{80,16},{1,81},{65,1},{17,65},{81,17},{2,82}... | collective-permute-start | bytes 737288 | tf_op jit(solution)/shard_map/ppermute | solution.py:268
  118.8 14.1 %collective-permute-start.5 = (bf16[96,1280]{1,0:T(8,128)(2,1)S(1)}, bf16[96,1280]{1,0:T(8,128)(2,1)S(1)}, u32[]{:S(2)}, u32[]{:S(2)}) collective-permute-start(bf16[96,1280]{1,0:T(8,128)(2,1)S(1)} %get-tuple-element.39), channel_id=1, source_target_pairs={{0,64},{64,16},{16,80},{80,0},{1,65},{65,17},{17,81},{81,1},{2,66}... | collective-permute-start | bytes 737288 | tf_op jit(solution)/shard_map/ppermute | solution.py:268
  122.9 12.8 %collective-permute-start.7 = (bf16[96,1280]{1,0:T(8,128)(2,1)S(1)}, bf16[96,1280]{1,0:T(8,128)(2,1)S(1)}, u32[]{:S(2)}, u32[]{:S(2)}) collective-permute-start(bf16[96,1280]{1,0:T(8,128)(2,1)S(1)} %get-tuple-element.41), channel_id=1, source_target_pairs={{0,80},{64,0},{16,64},{80,16},{1,81},{65,1},{17,65},{81,17},{2,82}... | collective-permute-start | bytes 737288 | tf_op jit(solution)/shard_map/ppermute | solution.py:268
  125.1 10.7 %collective-permute-start.8 = (bf16[96,1280]{1,0:T(8,128)(2,1)S(1)}, bf16[96,1280]{1,0:T(8,128)(2,1)S(1)}, u32[]{:S(2)}, u32[]{:S(2)}) collective-permute-start(bf16[96,1280]{1,0:T(8,128)(2,1)S(1)} %get-tuple-element.42), channel_id=1, source_target_pairs={{0,64},{64,16},{16,80},{80,0},{1,65},{65,17},{17,81},{81,1},{2,66}... | collective-permute-start | bytes 737288 | tf_op jit(solution)/shard_map/ppermute | solution.py:268
  125.1 16.7 %collective-permute-start.10 = (bf16[96,1280]{1,0:T(8,128)(2,1)S(1)}, bf16[96,1280]{1,0:T(8,128)(2,1)S(1)}, u32[]{:S(2)}, u32[]{:S(2)}) collective-permute-start(bf16[96,1280]{1,0:T(8,128)(2,1)S(1)} %get-tuple-element.44), channel_id=1, source_target_pairs={{0,80},{64,0},{16,64},{80,16},{1,81},{65,1},{17,65},{81,17},{2,82}... | collective-permute-start | bytes 737288 | tf_op jit(solution)/shard_map/ppermute | solution.py:268
  132.8 9.2 %copy-start.4 = (f32[192,1280]{1,0:T(8,128)S(1)}, f32[192,1280]{1,0:T(8,128)}, u32[]{:S(2)}) copy-start(f32[192,1280]{1,0:T(8,128)} %get-tuple-element.43) | copy-start | bytes 2949124
  132.8 9.2 %collective-permute-start.11 = (bf16[96,1280]{1,0:T(8,128)(2,1)S(1)}, bf16[96,1280]{1,0:T(8,128)(2,1)S(1)}, u32[]{:S(2)}, u32[]{:S(2)}) collective-permute-start(bf16[96,1280]{1,0:T(8,128)(2,1)S(1)} %get-tuple-element.45), channel_id=1, source_target_pairs={{0,64},{64,16},{16,80},{80,0},{1,65},{65,17},{17,81},{81,1},{2,66}... | collective-permute-start | bytes 737288 | tf_op jit(solution)/shard_map/ppermute | solution.py:268
  132.9 12.6 %collective-permute-start.13 = (bf16[96,1280]{1,0:T(8,128)(2,1)S(1)}, bf16[96,1280]{1,0:T(8,128)(2,1)S(1)}, u32[]{:S(2)}, u32[]{:S(2)}) collective-permute-start(bf16[96,1280]{1,0:T(8,128)(2,1)S(1)} %get-tuple-element.47), channel_id=1, source_target_pairs={{0,80},{64,0},{16,64},{80,16},{1,81},{65,1},{17,65},{81,17},{2,82}... | collective-permute-start | bytes 737288 | tf_op jit(solution)/shard_map/ppermute | solution.py:268
  135.7 9.9 %copy-start.3 = (f32[192,1280]{1,0:T(8,128)S(1)}, f32[192,1280]{1,0:T(8,128)}, u32[]{:S(2)}) copy-start(f32[192,1280]{1,0:T(8,128)} %get-tuple-element.46) | copy-start | bytes 2949124
  135.7 9.8 %collective-permute-start.14 = (bf16[96,1280]{1,0:T(8,128)(2,1)S(1)}, bf16[96,1280]{1,0:T(8,128)(2,1)S(1)}, u32[]{:S(2)}, u32[]{:S(2)}) collective-permute-start(bf16[96,1280]{1,0:T(8,128)(2,1)S(1)} %get-tuple-element.48), channel_id=1, source_target_pairs={{0,64},{64,16},{16,80},{80,0},{1,65},{65,17},{17,81},{81,1},{2,66}... | collective-permute-start | bytes 737288 | tf_op jit(solution)/shard_map/ppermute | solution.py:268
  135.8 12.4 %collective-permute-start.6 = (bf16[96,1280]{1,0:T(8,128)(2,1)S(1)}, bf16[96,1280]{1,0:T(8,128)(2,1)S(1)}, u32[]{:S(2)}, u32[]{:S(2)}) collective-permute-start(bf16[96,1280]{1,0:T(8,128)(2,1)S(1)} %select_convert_fusion.3), channel_id=1, source_target_pairs={{0,32},{32,0},{1,33},{33,1},{2,34},{34,2},{3,35},{35,3},{4,36},{36... | collective-permute-start | bytes 737288 | tf_op jit(solution)/shard_map/ppermute | solution.py:394
  141.8 6.5 %collective-permute-start.9 = (bf16[96,1280]{1,0:T(8,128)(2,1)S(1)}, bf16[96,1280]{1,0:T(8,128)(2,1)S(1)}, u32[]{:S(2)}, u32[]{:S(2)}) collective-permute-start(bf16[96,1280]{1,0:T(8,128)(2,1)S(1)} %select_convert_fusion.2), channel_id=1, source_target_pairs={{0,32},{32,0},{1,33},{33,1},{2,34},{34,2},{3,35},{35,3},{4,36},{36... | collective-permute-start | bytes 737288 | tf_op jit(solution)/shard_map/ppermute | solution.py:394
  142.1 6.2 %copy-start.5 = (f32[192,1280]{1,0:T(8,128)S(1)}, f32[192,1280]{1,0:T(8,128)}, u32[]{:S(2)}) copy-start(f32[192,1280]{1,0:T(8,128)} %get-tuple-element.40) | copy-start | bytes 2949124
  142.1 6.3 %collective-permute-start.12 = (bf16[96,1280]{1,0:T(8,128)(2,1)S(1)}, bf16[96,1280]{1,0:T(8,128)(2,1)S(1)}, u32[]{:S(2)}, u32[]{:S(2)}) collective-permute-start(bf16[96,1280]{1,0:T(8,128)(2,1)S(1)} %select_convert_fusion.1), channel_id=1, source_target_pairs={{0,32},{32,0},{1,33},{33,1},{2,34},{34,2},{3,35},{35,3},{4,36},{36... | collective-permute-start | bytes 737288 | tf_op jit(solution)/shard_map/ppermute | solution.py:394
  145.7 3.6 %collective-permute-start.15 = (bf16[96,1280]{1,0:T(8,128)(2,1)S(1)}, bf16[96,1280]{1,0:T(8,128)(2,1)S(1)}, u32[]{:S(2)}, u32[]{:S(2)}) collective-permute-start(bf16[96,1280]{1,0:T(8,128)(2,1)S(1)} %select_convert_fusion), channel_id=1, source_target_pairs={{0,32},{32,0},{1,33},{33,1},{2,34},{34,2},{3,35},{35,3},{4,36},{36... | collective-permute-start | bytes 737288 | tf_op jit(solution)/shard_map/ppermute | solution.py:394

commit v7 on v6

--- a/solution.py
+++ b/solution.py
@@ -31,7 +31,8 @@
 EXT_GROUP = 8
 BATCH = 12
 STATS = 16
-WIDTH = 1280
+BANDS = 4
+WIDTHS = (1280, 1280, 1280, 1280)
 SMEM = pl.BlockSpec(memory_space=pltpu.SMEM)
 VMEM = pl.BlockSpec(memory_space=pltpu.VMEM)
 HBM = pl.BlockSpec(memory_space=pl.ANY)
@@ -45,7 +46,7 @@
     return lax.ppermute(x, "y", [(i, (i - 1) % 4) for i in range(4)])
 
 
-def plan_kernel(where_ref, count_ref, table_ref, start_ref, n_ref, lists, sem):
+def plan_kernel(where_ref, counts_ref, table_ref, start_ref, n_ref, lists, sem):
     y, head, shared, share = [where_ref[i] for i in range(4)]
     copies = [
         pltpu.make_async_copy(table_ref.at[h], lists.at[i], sem.at[i])
@@ -55,61 +56,53 @@
         copy.start()
     for copy in copies:
         copy.wait()
-
+    slots = lax.broadcasted_iota(jnp.int32, (SLOTS, lists.shape[2]), 0)
     for which, h in enumerate((head, shared)):
-
-        def unit_step(local, carry):
-            unit = which * UNITS + local
-            column = (local * 171) >> 9
-            row = (column * 4 + y) * 3 + (local - 3 * column)
-            start_ref[unit, 0] = 0
-            start_ref[2 * UNITS + unit, 0] = 0
-
-            def slot_step(slot, found):
-                block = lists[which, row, slot]
-                sb = (block * 171) >> 9
-                r = block - 3 * sb
-                dy = ((sb & 3) + 4 - y) & 3
-                late = dy == 2
-                place = jnp.where(late, 0, (4 - dy) & 3) - jnp.where(dy == 1, 1, 0)
-                place = place * COLS + (sb >> 2)
-                if which == 0:
-                    start = place * (CHUNKS * MAIN) + r * (BLOCK // 2)
-                else:
-                    chunk = ((r * 8 + share) * 43) >> 8
-                    start = (place * CHUNKS + chunk) * EXT
-                early_n, late_n = found
-                start_ref[jnp.where(late, 2 * UNITS, 0) + unit, jnp.where(late, late_n, early_n)] = start
-                step = late.astype(jnp.int32)
-                return early_n + 1 - step, late_n + step
-
-            zero = jnp.int32(0)
-            early_n, late_n = lax.fori_loop(0, count_ref[h, row], slot_step, (zero, zero))
-            n_ref[0, unit] = early_n
-            n_ref[1, unit] = late_n
-            return carry
-
-        lax.fori_loop(0, UNITS, unit_step, 0)
+        block = lists[which]
+        sb = (block * 171) >> 9
+        r = block - 3 * sb
+        dy = ((sb & 3) + 4 - y) & 3
+        late = dy == 2
+        place = jnp.where(late, 0, (4 - dy) & 3) - jnp.where(dy == 1, 1, 0)
+        place = place * COLS + (sb >> 2)
+        if which == 0:
+            start = place * (CHUNKS * MAIN) + r * (BLOCK // 2)
+        else:
+            chunk = ((r * 8 + share) * 43) >> 8
+            start = (place * CHUNKS + chunk) * EXT
+        live = slots < counts_ref[pl.ds(h, 1), :]
+        for stage in range(2):
+            mine = jnp.where(live & (late == (stage == 1)), 1, 0)
+            found = jnp.zeros((1, block.shape[1]), jnp.int32)
+            sorted_ = jnp.zeros_like(block)
+            for i in range(SLOTS):
+                here = mine[i : i + 1]
+                at = jnp.where(here == 1, found, SLOTS)
+                sorted_ = jnp.where(slots == at, start[i : i + 1], sorted_)
+                found = found + here
+            start_ref[pl.ds((2 * which + stage) * SLOTS, SLOTS), :] = sorted_
+            n_ref[pl.ds(2 * which + stage, 1), :] = found
 
 
 def plan(where, counts, table):
+    rows = counts.shape[1]
     return pl.pallas_call(
         plan_kernel,
         out_shape=(
-            jax.ShapeDtypeStruct((4 * UNITS, SLOTS), jnp.int32),
-            jax.ShapeDtypeStruct((2, 2 * UNITS), jnp.int32),
+            jax.ShapeDtypeStruct((4 * SLOTS, rows), jnp.int32),
+            jax.ShapeDtypeStruct((4, rows), jnp.int32),
         ),
-        in_specs=[SMEM, SMEM, HBM],
-        out_specs=(SMEM, SMEM),
-        scratch_shapes=[pltpu.SMEM((2, 96, SLOTS), jnp.int32), pltpu.SemaphoreType.DMA((2,))],
-        cost_estimate=pl.CostEstimate(flops=8_000_000_000, bytes_accessed=100_000, transcendentals=0),
-    )(where, counts, table)
+        in_specs=[SMEM, VMEM, HBM],
+        out_specs=(VMEM, VMEM),
+        scratch_shapes=[pltpu.VMEM((2, SLOTS, rows), jnp.int32), pltpu.SemaphoreType.DMA((2,))],
+        cost_estimate=pl.CostEstimate(flops=1_000_000, bytes_accessed=100_000, transcendentals=0),
+    )(where, counts, table.transpose(0, 2, 1))
 
 
 def stage_kernel(last, pieces, *refs):
     where_ref, start_ref, n_ref, q_ref = refs[:4]
     refs = refs[4:]
-    xl = where_ref[4]
+    y, xl = where_ref[0], where_ref[4]
     if last:
         before, (last_k, last_v, out_ref), refs = refs[:3], refs[3:6], refs[6:]
         k_main, v_main, k_ext, v_ext, sem, top_ref, tot_ref, acc_ref = refs
@@ -146,17 +139,19 @@
         return lax.dot_general(a, b, (((1,), (1,)), ((), ())), preferred_element_type=jnp.float32)
 
     def run(units, group, key_flat, value_flat, width):
-        ns = [n_ref[stage, unit] for unit in units]
+        lists = [2 * (unit // UNITS) + stage for unit in units]
+        rows = [3 * y + 12 * (unit % UNITS // 3) + unit % 3 for unit in units]
+        ns = [n_ref[i, row] for i, row in zip(lists, rows)]
         most = functools.reduce(jnp.maximum, ns)
 
         def step(t, carry, start=False):
             col = lax.broadcasted_iota(jnp.int32, (1, group * width), 1)
             values, scores = [], []
-            for unit, n in zip(units, ns):
+            for unit, n, which, row in zip(units, ns, lists, rows):
                 starts = []
                 for i in range(group):
                     slot = jnp.maximum(jnp.minimum(group * t + i, n - 1), 0)
-                    at = start_ref[stage * 2 * UNITS + unit, slot]
+                    at = start_ref[which * SLOTS + slot, row]
                     starts.append(pl.multiple_of(at, width))
                 keys = jnp.concatenate([key_flat[pl.ds(r, width), :] for r in starts], axis=0)
                 values.append(
@@ -269,44 +264,48 @@
 
 
 def project_kernel(parts, rows_ref, w_ref, *refs):
-    outs, (w_buf, sem) = refs[:-2], refs[-2:]
     chunks = sorted({chunk for chunk, _, _ in parts})
-    copies = {}
-    for i, chunk in enumerate(chunks):
-        copies[chunk] = pltpu.make_async_copy(
-            w_ref.at[:, pl.ds(chunk * WIDTH, WIDTH)], w_buf.at[i], sem.at[i]
-        )
-        copies[chunk].start()
-    for i, chunk in enumerate(chunks):
-        copies[chunk].wait()
+    outs, bufs, sem = refs[: len(parts)], refs[len(parts) : -1], refs[-1]
+    copies = []
+    for i, (chunk, buf) in enumerate(zip(chunks, bufs)):
+        columns = pl.ds(sum(WIDTHS[:chunk]), WIDTHS[chunk])
+        band = buf.shape[0] // BANDS
+        copies.append([])
+        for j in range(BANDS):
+            rows = pl.ds(j * band, band)
+            copy = pltpu.make_async_copy(w_ref.at[rows, columns], buf.at[rows], sem.at[i, j])
+            copy.start()
+            copies[-1].append(copy)
+    for chunk, buf, bands in zip(chunks, bufs, copies):
+        for copy in bands:
+            copy.wait()
         for (which, lo, count), out in zip(parts, outs):
             if which != chunk:
                 continue
             rows = rows_ref[pl.ds(lo, count), :]
-            for at in range(0, WIDTH, 256):
-                product = jnp.dot(
-                    rows, w_buf[i, :, pl.ds(at, 256)], preferred_element_type=jnp.float32
-                )
-                out[:, pl.ds(at, 256)] = product.astype(out.dtype)
+            for at in range(0, WIDTHS[chunk], 256):
+                columns = pl.ds(at, min(256, WIDTHS[chunk] - at))
+                product = jnp.dot(rows, buf[:, columns], preferred_element_type=jnp.float32)
+                out[:, columns] = product.astype(out.dtype)
 
 
 def project_parts(rows, w, parts):
-    chunks = len({chunk for chunk, _, _ in parts})
+    chunks = sorted({chunk for chunk, _, _ in parts})
     return pl.pallas_call(
         functools.partial(project_kernel, parts),
         out_shape=tuple(
-            jax.ShapeDtypeStruct((count, WIDTH), jnp.float32 if lo == 0 else jnp.bfloat16)
-            for _, lo, count in parts
+            jax.ShapeDtypeStruct((count, WIDTHS[chunk]), jnp.float32 if lo == 0 else jnp.bfloat16)
+            for chunk, lo, count in parts
         ),
         in_specs=[VMEM, HBM],
         out_specs=(VMEM,) * len(parts),
         scratch_shapes=[
-            pltpu.VMEM((chunks, w.shape[0], WIDTH), w.dtype),
-            pltpu.SemaphoreType.DMA((chunks,)),
+            *[pltpu.VMEM((w.shape[0], WIDTHS[chunk]), w.dtype) for chunk in chunks],
+            pltpu.SemaphoreType.DMA((len(chunks), BANDS)),
         ],
         compiler_params=pltpu.CompilerParams(vmem_limit_bytes=52 * 1024 * 1024),
         cost_estimate=pl.CostEstimate(
-            flops=sum(2 * count * WIDTH * w.shape[0] for _, _, count in parts),
+            flops=sum(2 * count * WIDTHS[chunk] * w.shape[0] for chunk, _, count in parts),
             bytes_accessed=4_000_000,
             transcendentals=0,
         ),
@@ -314,26 +313,57 @@
 
 
 def project(rows, w):
-    chunks = w.shape[1] // WIDTH
+    chunks = len(WIDTHS)
     sides = lambda k: [(k, 2 * ROWS, ROWS), (k, 3 * ROWS, ROWS)]
     own = lambda k: [(k, 0, 2 * ROWS)]
-    first = project_parts(rows, w, sides(0))
+    low, high, head = project_parts(rows, w, sides(0) + own(0))
     rest = project_parts(rows, w, sum([sides(k) for k in range(1, chunks)], []))
-    owns = project_parts(rows, w, sum([own(k) for k in range(chunks)], []))
-    sent = first + rest
-    return sent[0::2], sent[1::2], owns
-
-
-def main_keys(rows):
-    runs = rows.reshape(3, 2, RUN, 4, 4, HEAD).transpose(4, 1, 3, 0, 2, 5)
-    return runs.reshape(32, MAIN, HEAD)
-
-
-def shared_keys(rows, xl, c):
-    runs = jnp.pad(rows, ((0, 32), (0, 0), (0, 0))).reshape(8, RUN, 4, HEAD)
-    runs = jnp.where(xl == 0, runs, jnp.roll(runs, -4, axis=0))
-    runs = jnp.where(c == 0, runs, jnp.roll(runs, -2, axis=0))
-    return runs.transpose(0, 2, 1, 3).reshape(32, EXT, HEAD)
+    owns = project_parts(rows, w, sum([own(k) for k in range(1, chunks)], []))
+    return (low,) + rest[0::2], (high,) + rest[1::2], (head,) + owns
+
+
+def pack_kv_kernel(chunk_ref, k_ref, v_ref, out_ref):
+    for j in range(4):
+        for e in range(2):
+            run = (2 * j + e + 2 * chunk_ref[0]) & 7
+            row = pl.multiple_of(jnp.minimum(run, 5) * RUN, RUN)
+            for u in range(4):
+                group = (2 * j + e) * 4 + u
+                for lo, ref in ((0, k_ref), (PART, v_ref)):
+                    head = pl.ds((5 * u + j) * HEAD, HEAD)
+                    for i in range(3):
+                        out_ref[group, pl.ds(lo + i * RUN, RUN), :] = ref[pl.ds((2 * i + e) * RUN, RUN), head]
+                    shared = ref[pl.ds(row, RUN), pl.ds((5 * u + 4) * HEAD, HEAD)]
+                    out_ref[group, pl.ds(lo + MAIN, EXT), :] = shared
+
+
+def pack_kv(chunk, k, v):
+    return pl.pallas_call(
+        pack_kv_kernel,
+        out_shape=jax.ShapeDtypeStruct((32, KV, HEAD), k.dtype),
+        in_specs=[SMEM, VMEM, VMEM],
+        out_specs=VMEM,
+        cost_estimate=pl.CostEstimate(flops=1_000_000, bytes_accessed=2_000_000, transcendentals=0),
+    )(chunk.reshape(1), k, v)
+
+
+def pack_q_kernel(q_ref, out_ref):
+    for u in range(4):
+        for j in range(4):
+            for which, head in enumerate((5 * u + j, 5 * u + 4)):
+                rows = q_ref[:, pl.ds(head * HEAD, HEAD)]
+                for e in range(2):
+                    out_ref[(2 * j + e) * 4 + u, which] = rows
+
+
+def pack_q(q):
+    return pl.pallas_call(
+        pack_q_kernel,
+        out_shape=jax.ShapeDtypeStruct((32, 2, ROWS, HEAD), q.dtype),
+        in_specs=[VMEM],
+        out_specs=VMEM,
+        cost_estimate=pl.CostEstimate(flops=1_000_000, bytes_accessed=2_000_000, transcendentals=0),
+    )(q)
 
 
 def merge(shares, levels):
@@ -346,23 +376,9 @@
     xh, zh, zl, y, xl, c = [lax.axis_index(name) for name in NAMES]
     u = 2 * xl + c
     j = 2 * xh + zh
-    k5 = key_rows.reshape(ROWS, 4, 5, HEAD)
-    v5 = value_rows.reshape(ROWS, 4, 5, HEAD)
-    q5 = queries.reshape(ROWS, 4, 5, HEAD)
-    sent = jnp.concatenate(
-        [
-            main_keys(k5[:, :, :4]),
-            shared_keys(k5[:, :, 4], xl, c),
-            main_keys(v5[:, :, :4]),
-            shared_keys(v5[:, :, 4], xl, c),
-        ],
-        axis=1,
-    )
+    sent = pack_kv((2 * xl + c).astype(jnp.int32), key_rows, value_rows)
     kv = lax.all_to_all(sent, SPREAD, 0, 0, tiled=True).reshape(COLS, CHUNKS, KV, HEAD)
-
-    q = jnp.stack([q5[:, :, :4], jnp.broadcast_to(q5[:, :, 4:], (ROWS, 4, 4, HEAD))])
-    q = jnp.broadcast_to(q.transpose(3, 2, 0, 1, 4)[:, None], (4, 2, 4, 2, ROWS, HEAD))
-    q = lax.all_to_all(q.reshape(32, 2, ROWS, HEAD), SPREAD, 0, 0, tiled=True)
+    q = lax.all_to_all(pack_q(queries), SPREAD, 0, 0, tiled=True)
     q = q.reshape(COLS, CHUNKS, 2, ROWS, HEAD).transpose(2, 0, 1, 3, 4).reshape(2 * UNITS, BLOCK, HEAD)
 
     where = jnp.stack([y, 5 * u + j, 5 * u + 4, 2 * j + zl, xl]).astype(jnp.int32)
@@ -375,6 +391,7 @@
     state = attend(False, where, plans, q, (), (kv, below, above))
     out = attend(True, where, plans, q, state, (last_k, last_v))
     out = lax.all_to_all(out, ("xh", "zh", "zl"), 0, 0, tiled=True)
+    out, w_out, xl, c = lax.optimization_barrier((out, w_out, xl, c))
 
     levels = out[:, 2 * SUPER :].reshape(COLS, 3, STATS, BLOCK)[:, :, :6].astype(jnp.float32)
     levels = jnp.sum(levels.reshape(COLS, 3, 2, 3, BLOCK), axis=3).transpose(2, 0, 1, 3)

time: 151 us -> 146 us (0.967)
  waiting for transfers between devices: 22.4 us -> 40 us
  Pallas kernels: 43.2 us -> 29.3 us
  local copies, waits for them, and re-layouts: 9.8 us -> 2.93 us
  other arithmetic: 5.67 us -> 3.08 us
    all_to_all x1, waiting for transfers between devices: 2.47 us -> 17.1 us  [per_device(): q = lax.all_to_all(pack_q(queries), SPREAD, 0, 0, tiled=True)]
    pallas_call x1 -> x3, Pallas kernels: 15.5 us -> 6.89 us  [the longest x1 2.39 us: pack_q(): pl.pallas_call(pack_q_kernel, out_shape=jax.ShapeDtypeStruct((32, 2, ROWS...]
    pallas_call x2, Pallas kernels: 17 us -> 12 us  [attend(): pl.pallas_call(functools.partial(stage_kernel, last, pieces), out_shape=o...]
    unnamed x23 -> x11, local copies, waits for them, and re-layouts: 3.38 us -> 0.03 us
    ppermute x2, waiting for transfers between devices: 0.01 us -> 3.24 us  [ring_down(): return lax.ppermute(x, 'y', [(i, (i - 1) % 4) for i in range(4)])]
  transfers between devices with their start and end apart: 18 -> 18, of which waited for: 5 -> 6; matrix products, arithmetic and copies ran while one was open for 5% -> 2% of each run, Pallas kernels for 23% -> 13%
where the time goes in v7:
time: 146 us; the launch traced here: 145 us
  starting transfers between devices  40.1 us (27%)
  waiting for transfers between devices  40 us (27%)
  Pallas kernels  29.3 us (20%)
  blocking collectives  29.2 us (20%)
  other arithmetic  3.08 us (2%)
  local copies, waits for them, and re-layouts  2.93 us (2%)
    all_to_all x1, blocking collectives, per_device(): out = lax.all_to_all(out, ('xh', 'zh', 'zl'), 0, 0, tiled=True)  29.2 us
    all_to_all x1, waiting for transfers between devices, per_device(): q = lax.all_to_all(pack_q(queries), SPREAD, 0, 0, tiled=True)  17.1 us
    all_to_all x1, waiting for transfers between devices, per_device(): lax.all_to_all(sent, SPREAD, 0, 0, tiled=True)  14.4 us
    ppermute x4, starting transfers between devices, per_device(): lax.ppermute(give, 'c', [(0, 1), (1, 0)])  12.1 us
    pallas_call x2, Pallas kernels, attend(): pl.pallas_call(functools.partial(stage_kernel, last, pieces), out_shape=o...  12 us
    pallas_call x3, Pallas kernels, project_parts(): pl.pallas_call(functools.partial(project_kernel, parts), out_shape=tuple(...  10.4 us
    all_to_all x1, starting transfers between devices, per_device(): lax.all_to_all(sent, SPREAD, 0, 0, tiled=True)  9.43 us
    ppermute x8, starting transfers between devices, around(): lax.ppermute(x, ('xl', 'xh'), [(index(i), index(i + step)) for i in range...  8.37 us
  transfers between devices with their start and end apart: 18, of which 6 were waited for; matrix products, arithmetic and copies ran while one was open for 2% of the time, Pallas kernels for 13%

profile of v7, /device:TPU:1, one launch (start us, length us, event | category | flops | bytes accessed | tf_op | source)
XLA Modules:
  0.0 145.0 jit_solution(18070102782373900772)
XLA Ops:
  0.0 2.3 %shard_map.64 = bf16[32,128,128]{2,1,0:T(8,128)(2,1)} custom-call(s32[1]{0:T(128)} %bitcast.5.chunk_ref, bf16[96,2560]{1,0:T(8,128)(2,1)} %k_ref.1, bf16[96,2560]{1,0:T(8,128)(2,1)} %v_ref.1), custom_call_target="tpu_custom_call" | custom-call | flops 1000000 | bytes 2000000 | tf_op jit(solution)/shard_map/pallas_call | solution.py:341
  2.3 9.4 %all-to-all-start = ((bf16[32,128,128]{2,1,0:T(8,128)(2,1)}), bf16[32,128,128]{2,1,0:T(8,128)(2,1)S(1)}, u32[]{:S(2)}, u32[]{:S(2)}) async-start(bf16[32,128,128]{2,1,0:T(8,128)(2,1)} %shard_map.64), calls=%async_computation | async-start | bytes 2097152 | tf_op jit(solution)/shard_map/all_to_all | solution.py:380
  11.8 2.4 %shard_map.65 = bf16[32,2,96,128]{3,2,1,0:T(8,128)(2,1)} custom-call(bf16[96,2560]{1,0:T(8,128)(2,1)} %q_ref.1), custom_call_target="tpu_custom_call" | custom-call | flops 1000000 | bytes 2000000 | tf_op jit(solution)/shard_map/pallas_call | solution.py:360
  14.2 14.4 %all-to-all-done = bf16[32,128,128]{2,1,0:T(8,128)(2,1)S(1)} async-done(((bf16[32,128,128]{2,1,0:T(8,128)(2,1)}), bf16[32,128,128]{2,1,0:T(8,128)(2,1)S(1)}, u32[]{:S(2)}, u32[]{:S(2)}) %all-to-all-start) | async-done | bytes 1048608 | tf_op jit(solution)/shard_map/all_to_all | solution.py:380
  28.5 4.7 %all-to-all-start.1 = ((bf16[32,2,96,128]{3,2,1,0:T(8,128)(2,1)}), bf16[32,2,96,128]{3,2,1,0:T(8,128)(2,1)}, u32[]{:S(2)}, u32[]{:S(2)}) async-start(bf16[32,2,96,128]{3,2,1,0:T(8,128)(2,1)} %shard_map.65), calls=%async_computation.1 | async-start | bytes 3145728 | tf_op jit(solution)/shard_map/all_to_all | solution.py:381
  33.2 1.4 collective-permute-start
  34.6 1.5 %collective-permute-start.1 = (bf16[8,4,128,128]{3,2,1,0:T(8,128)(2,1)S(1)}, bf16[8,4,128,128]{3,2,1,0:T(8,128)(2,1)S(1)}, u32[]{:S(2)}, u32[]{:S(2)}) collective-permute-start(bf16[8,4,128,128]{3,2,1,0:T(8,128)(2,1)S(1)} %bitcast.39), channel_id=1, source_target_pairs={{0,3},{1,0},{2,1},{3,2},{4,7},{5,4},{6,5},{7,6},{8,11},{9,8},{10,9... | collective-permute-start | bytes 3145736 | tf_op jit(solution)/shard_map/ppermute | solution.py:46
  36.1 0.6 stack.23.where_ref.refs_0_
  36.7 2.2 %shard_map.66 = (s32[64,96]{1,0:T(8,128)}, s32[4,96]{1,0:T(4,128)}) custom-call(s32[5]{0:T(128)} %stack.23.where_ref.refs_0_, s32[20,96]{1,0:T(8,128)} %counts_ref.1, s32[20,16,96]{2,1,0:T(8,128)} %bitcast.44), custom_call_target="tpu_custom_call" | custom-call | flops 1000000 | bytes 100000 | tf_op jit(solution)/shard_map/pallas_call | solution.py:89
  38.9 17.1 %all-to-all-done.1 = bf16[32,2,96,128]{3,2,1,0:T(8,128)(2,1)} async-done(((bf16[32,2,96,128]{3,2,1,0:T(8,128)(2,1)}), bf16[32,2,96,128]{3,2,1,0:T(8,128)(2,1)}, u32[]{:S(2)}, u32[]{:S(2)}) %all-to-all-start.1) | async-done | bytes 1572896 | tf_op jit(solution)/shard_map/all_to_all | solution.py:381
  56.0 1.6 %copy.20 = bf16[8,4,2,96,128]{4,3,1,0,2:T(8,128)(2,1)S(1)} copy(bf16[8,4,2,96,128]{4,3,2,1,0:T(8,128)(2,1)} %bitcast.7) | data formatting | bytes 3145728 | tf_op jit(solution)/shard_map/reshape | solution.py:382
  57.6 0.0 copy-start.1
  57.6 0.0 copy-start.2
  57.6 1.3 collective-permute-done.refs_5_
  58.9 0.0 collective-permute-done.1.refs_6_
  59.0 2.6 %collective-permute-start.2 = (bf16[8,4,64,128]{3,2,1,0:T(8,128)(2,1)S(1)}, bf16[8,4,64,128]{3,2,1,0:T(8,128)(2,1)S(1)}, u32[]{:S(2)}, u32[]{:S(2)}) collective-permute-start(bf16[8,4,64,128]{3,2,1,0:T(8,128)(2,1)S(1)} %slice.56), channel_id=1, source_target_pairs={{0,3},{1,0},{2,1},{3,2},{4,7},{5,4},{6,5},{7,6},{8,11},{9,8},{10,9... | collective-permute-start | bytes 1572872 | tf_op jit(solution)/shard_map/ppermute | solution.py:46
  61.6 0.1 collective-permute-start.3
  61.7 6.4 %shard_map.67 = (f32[48,128,128]{2,1,0:T(8,128)S(1)}, f32[48,128,128]{2,1,0:T(8,128)S(1)}, f32[48,128,128]{2,1,0:T(8,128)S(1)}) custom-call(s32[5]{0:T(128)S(1)} %copy-done, s32[64,96]{1,0:T(8,128)S(1)} %copy-done.1, s32[4,96]{1,0:T(4,128)S(1)} %copy-done.2, bf16[48,128,128]{2,1,0:T(8,128)(2,1)S(1)} %bitcast.36, bf16[8,4,128,128]{3,2,1,0:T(8,128)(2,1)S(1)} %bitcast.40, ...), custom_call_target="tpu_custom_call" | custom-call | flops 15000000512 | bytes 6000000 | tf_op jit(solution)/shard_map/pallas_call | solution.py:248
  68.1 3.2 %collective-permute-done.2.refs_7_ = bf16[8,4,64,128]{3,2,1,0:T(8,128)(2,1)S(1)} collective-permute-done((bf16[8,4,64,128]{3,2,1,0:T(8,128)(2,1)S(1)}, bf16[8,4,64,128]{3,2,1,0:T(8,128)(2,1)S(1)}, u32[]{:S(2)}, u32[]{:S(2)}) %collective-permute-start.2) | collective-permute-done | bytes 524320 | tf_op jit(solution)/shard_map/ppermute | solution.py:46
  71.4 3.2 %collective-permute-done.3.refs_8_ = bf16[8,4,64,128]{3,2,1,0:T(8,128)(2,1)S(1)} collective-permute-done((bf16[8,4,64,128]{3,2,1,0:T(8,128)(2,1)S(1)}, bf16[8,4,64,128]{3,2,1,0:T(8,128)(2,1)S(1)}, u32[]{:S(2)}, u32[]{:S(2)}) %collective-permute-start.3) | collective-permute-done | bytes 524320 | tf_op jit(solution)/shard_map/ppermute | solution.py:42
  74.6 5.6 %shard_map.68 = bf16[8,816,128]{2,1,0:T(8,128)(2,1)S(1)} custom-call(s32[5]{0:T(128)S(1)} %copy-done, s32[64,96]{1,0:T(8,128)S(1)} %copy-done.1, s32[4,96]{1,0:T(4,128)S(1)} %copy-done.2, bf16[48,128,128]{2,1,0:T(8,128)(2,1)S(1)} %bitcast.37, f32[48,128,128]{2,1,0:T(8,128)S(1)} %get-tuple-element.38.refs_4_, f32[48,128,128]{2,1,0:T(8,128)S(1)} %get-tuple-element.39.refs_5_, ...), custom_call_target="tpu_custom_call" | custom-call | flops 5000000000 | bytes 2000000 | tf_op jit(solution)/shard_map/pallas_call | solution.py:248
  80.3 29.2 %all_to_all.15 = bf16[8,816,128]{2,1,0:T(8,128)(2,1)S(1)} all-to-all(bf16[8,816,128]{2,1,0:T(8,128)(2,1)S(1)} %shard_map.68), channel_id=1, replica_groups=mesh['xl'=2,'c'=2,'xh'=2,'zh'=2,'zl'=2,'y'=4] {'xh','zh','zl'}, dimensions={0} | all-to-all | bytes 3342336 | tf_op jit(solution)/shard_map/all_to_all | solution.py:393
  109.5 0.1 fusion.10
  109.6 0.1 maximum_select_fusion
  109.8 0.5 fusion.1
  110.3 0.5 multiply_reduce_fusion
  110.8 0.3 copy.23
  111.1 0.3 copy.24.rows_ref
  111.4 2.4 %shard_map.69 = (bf16[96,1280]{1,0:T(8,128)(2,1)S(1)}, bf16[96,1280]{1,0:T(8,128)(2,1)S(1)}, f32[192,1280]{1,0:T(8,128)S(1)}) custom-call(bf16[384,640]{1,0:T(8,128)(2,1)S(1)} %copy.24.rows_ref, bf16[640,5120]{1,0:T(8,128)(2,1)} %w_ref.2), custom_call_target="tpu_custom_call" | custom-call | flops 629145600 | bytes 4000000 | tf_op jit(solution)/shard_map/pallas_call | solution.py:294
  113.8 0.1 collective-permute-start.4
  113.9 1.5 %collective-permute-start.5 = (bf16[96,1280]{1,0:T(8,128)(2,1)S(1)}, bf16[96,1280]{1,0:T(8,128)(2,1)S(1)}, u32[]{:S(2)}, u32[]{:S(2)}) collective-permute-start(bf16[96,1280]{1,0:T(8,128)(2,1)S(1)} %get-tuple-element.47), channel_id=1, source_target_pairs={{0,64},{64,16},{16,80},{80,0},{1,65},{65,17},{17,81},{81,1},{2,66}... | collective-permute-start | bytes 737288 | tf_op jit(solution)/shard_map/ppermute | solution.py:263
  115.3 3.6 %shard_map.71 = (bf16[96,1280]{1,0:T(8,128)(2,1)S(1)}, bf16[96,1280]{1,0:T(8,128)(2,1)S(1)}, bf16[96,1280]{1,0:T(8,128)(2,1)S(1)}, bf16[96,1280]{1,0:T(8,128)(2,...) custom-call(bf16[384,640]{1,0:T(8,128)(2,1)S(1)} %copy.24.rows_ref, bf16[640,5120]{1,0:T(8,128)(2,1)} %w_ref.2), custom_call_target="tpu_custom_call" | custom-call | flops 943718400 | bytes 4000000 | tf_op jit(solution)/shard_map/pallas_call | solution.py:294
  118.9 1.4 collective-permute-start.7
  120.3 0.2 collective-permute-start.8
  120.5 2.5 %collective-permute-start.10 = (bf16[96,1280]{1,0:T(8,128)(2,1)S(1)}, bf16[96,1280]{1,0:T(8,128)(2,1)S(1)}, u32[]{:S(2)}, u32[]{:S(2)}) collective-permute-start(bf16[96,1280]{1,0:T(8,128)(2,1)S(1)} %get-tuple-element.52), channel_id=1, source_target_pairs={{0,80},{64,0},{16,64},{80,16},{1,81},{65,1},{17,65},{81,17},{2,82}... | collective-permute-start | bytes 737288 | tf_op jit(solution)/shard_map/ppermute | solution.py:263
  123.0 4.4 %shard_map.70 = (f32[192,1280]{1,0:T(8,128)S(1)}, f32[192,1280]{1,0:T(8,128)}, f32[192,1280]{1,0:T(8,128)}) custom-call(bf16[384,640]{1,0:T(8,128)(2,1)S(1)} %copy.24.rows_ref, bf16[640,5120]{1,0:T(8,128)(2,1)} %w_ref.2), custom_call_target="tpu_custom_call" | custom-call | flops 943718400 | bytes 4000000 | tf_op jit(solution)/shard_map/pallas_call | solution.py:294
  127.3 0.0 collective-permute-done.4
  127.3 0.1 collective-permute-start.11
  127.4 0.0 collective-permute-done.5
  127.4 2.7 %collective-permute-start.13 = (bf16[96,1280]{1,0:T(8,128)(2,1)S(1)}, bf16[96,1280]{1,0:T(8,128)(2,1)S(1)}, u32[]{:S(2)}, u32[]{:S(2)}) collective-permute-start(bf16[96,1280]{1,0:T(8,128)(2,1)S(1)} %get-tuple-element.55), channel_id=1, source_target_pairs={{0,80},{64,0},{16,64},{80,16},{1,81},{65,1},{17,65},{81,17},{2,82}... | collective-permute-start | bytes 737288 | tf_op jit(solution)/shard_map/ppermute | solution.py:263
  130.1 0.1 select_convert_fusion.3
  130.2 0.0 collective-permute-done.7
  130.2 0.1 collective-permute-start.14
  130.3 0.0 collective-permute-done.8
  130.3 4.9 %collective-permute-start.6 = (bf16[96,1280]{1,0:T(8,128)(2,1)S(1)}, bf16[96,1280]{1,0:T(8,128)(2,1)S(1)}, u32[]{:S(2)}, u32[]{:S(2)}) collective-permute-start(bf16[96,1280]{1,0:T(8,128)(2,1)S(1)} %select_convert_fusion.3), channel_id=1, source_target_pairs={{0,32},{32,0},{1,33},{33,1},{2,34},{34,2},{3,35},{35,3},{4,36},{36... | collective-permute-start | bytes 737288 | tf_op jit(solution)/shard_map/ppermute | solution.py:411
  135.2 0.1 select_convert_fusion.2
  135.3 0.0 collective-permute-done.10
  135.3 1.1 collective-permute-start.9
  136.4 0.0 collective-permute-done.11
  136.4 0.1 select_convert_fusion.1
  136.5 3.5 %collective-permute-start.12 = (bf16[96,1280]{1,0:T(8,128)(2,1)S(1)}, bf16[96,1280]{1,0:T(8,128)(2,1)S(1)}, u32[]{:S(2)}, u32[]{:S(2)}) collective-permute-start(bf16[96,1280]{1,0:T(8,128)(2,1)S(1)} %select_convert_fusion.1), channel_id=1, source_target_pairs={{0,32},{32,0},{1,33},{33,1},{2,34},{34,2},{3,35},{35,3},{4,36},{36... | collective-permute-start | bytes 737288 | tf_op jit(solution)/shard_map/ppermute | solution.py:411
  140.0 0.0 collective-permute-done.13
  140.0 0.0 collective-permute-done.14
  140.0 0.1 select_convert_fusion
  140.1 2.6 %collective-permute-start.15 = (bf16[96,1280]{1,0:T(8,128)(2,1)S(1)}, bf16[96,1280]{1,0:T(8,128)(2,1)S(1)}, u32[]{:S(2)}, u32[]{:S(2)}) collective-permute-start(bf16[96,1280]{1,0:T(8,128)(2,1)S(1)} %select_convert_fusion), channel_id=1, source_target_pairs={{0,32},{32,0},{1,33},{33,1},{2,34},{34,2},{3,35},{35,3},{4,36},{36... | collective-permute-start | bytes 737288 | tf_op jit(solution)/shard_map/ppermute | solution.py:411
  142.7 0.0 collective-permute-done.6
  142.7 0.1 add_convert_fusion.3
  142.8 0.0 collective-permute-done.9
  142.8 0.1 add_convert_fusion.2
  143.0 0.0 collective-permute-done.12
  143.0 0.1 add_convert_fusion.1
  143.1 0.7 collective-permute-done.15
  143.8 0.1 add_convert_fusion
  144.0 1.0 pad_maximum_fusion
  (21 shorter events, 0.3 us)
Async XLA Ops:
  2.3 26.2 %all-to-all-start = ((bf16[32,128,128]{2,1,0:T(8,128)(2,1)}), bf16[32,128,128]{2,1,0:T(8,128)(2,1)S(1)}, u32[]{:S(2)}, u32[]{:S(2)}) async-start(bf16[32,128,128]{2,1,0:T(8,128)(2,1)} %shard_map.64), calls=%async_computation | async-start | bytes 2097152 | tf_op jit(solution)/shard_map/all_to_all | solution.py:380
  28.5 27.5 %all-to-all-start.1 = ((bf16[32,2,96,128]{3,2,1,0:T(8,128)(2,1)}), bf16[32,2,96,128]{3,2,1,0:T(8,128)(2,1)}, u32[]{:S(2)}, u32[]{:S(2)}) async-start(bf16[32,2,96,128]{3,2,1,0:T(8,128)(2,1)} %shard_map.65), calls=%async_computation.1 | async-start | bytes 3145728 | tf_op jit(solution)/shard_map/all_to_all | solution.py:381
  33.2 25.7 %collective-permute-start = (bf16[8,4,128,128]{3,2,1,0:T(8,128)(2,1)S(1)}, bf16[8,4,128,128]{3,2,1,0:T(8,128)(2,1)S(1)}, u32[]{:S(2)}, u32[]{:S(2)}) collective-permute-start(bf16[8,4,128,128]{3,2,1,0:T(8,128)(2,1)S(1)} %bitcast.38), channel_id=1, source_target_pairs={{0,1},{1,2},{2,3},{3,0},{4,5},{5,6},{6,7},{7,4},{8,9},{9,10},{10,1... | collective-permute-start | bytes 3145736 | tf_op jit(solution)/shard_map/ppermute | solution.py:42
  34.6 24.4 %collective-permute-start.1 = (bf16[8,4,128,128]{3,2,1,0:T(8,128)(2,1)S(1)}, bf16[8,4,128,128]{3,2,1,0:T(8,128)(2,1)S(1)}, u32[]{:S(2)}, u32[]{:S(2)}) collective-permute-start(bf16[8,4,128,128]{3,2,1,0:T(8,128)(2,1)S(1)} %bitcast.39), channel_id=1, source_target_pairs={{0,3},{1,0},{2,1},{3,2},{4,7},{5,4},{6,5},{7,6},{8,11},{9,8},{10,9... | collective-permute-start | bytes 3145736 | tf_op jit(solution)/shard_map/ppermute | solution.py:46
  57.6 4.1 %copy-start = (s32[5]{0:T(128)S(1)}, s32[5]{0:T(128)}, u32[]{:S(2)}) copy-start(s32[5]{0:T(128)} %stack.23.where_ref.refs_0_) | copy-start | bytes 64
  57.6 4.1 %copy-start.1 = (s32[64,96]{1,0:T(8,128)S(1)}, s32[64,96]{1,0:T(8,128)}, u32[]{:S(2)}) copy-start(s32[64,96]{1,0:T(8,128)} %get-tuple-element.33.refs_1_) | copy-start | bytes 73732
  57.6 4.1 %copy-start.2 = (s32[4,96]{1,0:T(4,128)S(1)}, s32[4,96]{1,0:T(4,128)}, u32[]{:S(2)}) copy-start(s32[4,96]{1,0:T(4,128)} %get-tuple-element.34.refs_2_) | copy-start | bytes 4612
  59.0 12.4 %collective-permute-start.2 = (bf16[8,4,64,128]{3,2,1,0:T(8,128)(2,1)S(1)}, bf16[8,4,64,128]{3,2,1,0:T(8,128)(2,1)S(1)}, u32[]{:S(2)}, u32[]{:S(2)}) collective-permute-start(bf16[8,4,64,128]{3,2,1,0:T(8,128)(2,1)S(1)} %slice.56), channel_id=1, source_target_pairs={{0,3},{1,0},{2,1},{3,2},{4,7},{5,4},{6,5},{7,6},{8,11},{9,8},{10,9... | collective-permute-start | bytes 1572872 | tf_op jit(solution)/shard_map/ppermute | solution.py:46
  61.6 13.0 %collective-permute-start.3 = (bf16[8,4,64,128]{3,2,1,0:T(8,128)(2,1)S(1)}, bf16[8,4,64,128]{3,2,1,0:T(8,128)(2,1)S(1)}, u32[]{:S(2)}, u32[]{:S(2)}) collective-permute-start(bf16[8,4,64,128]{3,2,1,0:T(8,128)(2,1)S(1)} %slice.57), channel_id=1, source_target_pairs={{0,1},{1,2},{2,3},{3,0},{4,5},{5,6},{6,7},{7,4},{8,9},{9,10},{10,1... | collective-permute-start | bytes 1572872 | tf_op jit(solution)/shard_map/ppermute | solution.py:42
  113.8 13.5 %collective-permute-start.4 = (bf16[96,1280]{1,0:T(8,128)(2,1)S(1)}, bf16[96,1280]{1,0:T(8,128)(2,1)S(1)}, u32[]{:S(2)}, u32[]{:S(2)}) collective-permute-start(bf16[96,1280]{1,0:T(8,128)(2,1)S(1)} %get-tuple-element.46), channel_id=1, source_target_pairs={{0,80},{64,0},{16,64},{80,16},{1,81},{65,1},{17,65},{81,17},{2,82}... | collective-permute-start | bytes 737288 | tf_op jit(solution)/shard_map/ppermute | solution.py:263
  113.9 13.5 %collective-permute-start.5 = (bf16[96,1280]{1,0:T(8,128)(2,1)S(1)}, bf16[96,1280]{1,0:T(8,128)(2,1)S(1)}, u32[]{:S(2)}, u32[]{:S(2)}) collective-permute-start(bf16[96,1280]{1,0:T(8,128)(2,1)S(1)} %get-tuple-element.47), channel_id=1, source_target_pairs={{0,64},{64,16},{16,80},{80,0},{1,65},{65,17},{17,81},{81,1},{2,66}... | collective-permute-start | bytes 737288 | tf_op jit(solution)/shard_map/ppermute | solution.py:263
  118.9 11.3 %collective-permute-start.7 = (bf16[96,1280]{1,0:T(8,128)(2,1)S(1)}, bf16[96,1280]{1,0:T(8,128)(2,1)S(1)}, u32[]{:S(2)}, u32[]{:S(2)}) collective-permute-start(bf16[96,1280]{1,0:T(8,128)(2,1)S(1)} %get-tuple-element.49), channel_id=1, source_target_pairs={{0,80},{64,0},{16,64},{80,16},{1,81},{65,1},{17,65},{81,17},{2,82}... | collective-permute-start | bytes 737288 | tf_op jit(solution)/shard_map/ppermute | solution.py:263
  120.3 10.0 %collective-permute-start.8 = (bf16[96,1280]{1,0:T(8,128)(2,1)S(1)}, bf16[96,1280]{1,0:T(8,128)(2,1)S(1)}, u32[]{:S(2)}, u32[]{:S(2)}) collective-permute-start(bf16[96,1280]{1,0:T(8,128)(2,1)S(1)} %get-tuple-element.50), channel_id=1, source_target_pairs={{0,64},{64,16},{16,80},{80,0},{1,65},{65,17},{17,81},{81,1},{2,66}... | collective-permute-start | bytes 737288 | tf_op jit(solution)/shard_map/ppermute | solution.py:263
  120.5 14.9 %collective-permute-start.10 = (bf16[96,1280]{1,0:T(8,128)(2,1)S(1)}, bf16[96,1280]{1,0:T(8,128)(2,1)S(1)}, u32[]{:S(2)}, u32[]{:S(2)}) collective-permute-start(bf16[96,1280]{1,0:T(8,128)(2,1)S(1)} %get-tuple-element.52), channel_id=1, source_target_pairs={{0,80},{64,0},{16,64},{80,16},{1,81},{65,1},{17,65},{81,17},{2,82}... | collective-permute-start | bytes 737288 | tf_op jit(solution)/shard_map/ppermute | solution.py:263
  127.3 9.1 %collective-permute-start.11 = (bf16[96,1280]{1,0:T(8,128)(2,1)S(1)}, bf16[96,1280]{1,0:T(8,128)(2,1)S(1)}, u32[]{:S(2)}, u32[]{:S(2)}) collective-permute-start(bf16[96,1280]{1,0:T(8,128)(2,1)S(1)} %get-tuple-element.53), channel_id=1, source_target_pairs={{0,64},{64,16},{16,80},{80,0},{1,65},{65,17},{17,81},{81,1},{2,66}... | collective-permute-start | bytes 737288 | tf_op jit(solution)/shard_map/ppermute | solution.py:263
  127.4 12.6 %collective-permute-start.13 = (bf16[96,1280]{1,0:T(8,128)(2,1)S(1)}, bf16[96,1280]{1,0:T(8,128)(2,1)S(1)}, u32[]{:S(2)}, u32[]{:S(2)}) collective-permute-start(bf16[96,1280]{1,0:T(8,128)(2,1)S(1)} %get-tuple-element.55), channel_id=1, source_target_pairs={{0,80},{64,0},{16,64},{80,16},{1,81},{65,1},{17,65},{81,17},{2,82}... | collective-permute-start | bytes 737288 | tf_op jit(solution)/shard_map/ppermute | solution.py:263
  130.1 6.3 %copy-start.4 = (f32[192,1280]{1,0:T(8,128)S(1)}, f32[192,1280]{1,0:T(8,128)}, u32[]{:S(2)}) copy-start(f32[192,1280]{1,0:T(8,128)} %get-tuple-element.51) | copy-start | bytes 2949124
  130.2 9.8 %collective-permute-start.14 = (bf16[96,1280]{1,0:T(8,128)(2,1)S(1)}, bf16[96,1280]{1,0:T(8,128)(2,1)S(1)}, u32[]{:S(2)}, u32[]{:S(2)}) collective-permute-start(bf16[96,1280]{1,0:T(8,128)(2,1)S(1)} %get-tuple-element.56), channel_id=1, source_target_pairs={{0,64},{64,16},{16,80},{80,0},{1,65},{65,17},{17,81},{81,1},{2,66}... | collective-permute-start | bytes 737288 | tf_op jit(solution)/shard_map/ppermute | solution.py:263
  130.3 12.4 %collective-permute-start.6 = (bf16[96,1280]{1,0:T(8,128)(2,1)S(1)}, bf16[96,1280]{1,0:T(8,128)(2,1)S(1)}, u32[]{:S(2)}, u32[]{:S(2)}) collective-permute-start(bf16[96,1280]{1,0:T(8,128)(2,1)S(1)} %select_convert_fusion.3), channel_id=1, source_target_pairs={{0,32},{32,0},{1,33},{33,1},{2,34},{34,2},{3,35},{35,3},{4,36},{36... | collective-permute-start | bytes 737288 | tf_op jit(solution)/shard_map/ppermute | solution.py:411
  135.2 4.8 %copy-start.3 = (f32[192,1280]{1,0:T(8,128)S(1)}, f32[192,1280]{1,0:T(8,128)}, u32[]{:S(2)}) copy-start(f32[192,1280]{1,0:T(8,128)} %get-tuple-element.54) | copy-start | bytes 2949124
  135.3 7.5 %collective-permute-start.9 = (bf16[96,1280]{1,0:T(8,128)(2,1)S(1)}, bf16[96,1280]{1,0:T(8,128)(2,1)S(1)}, u32[]{:S(2)}, u32[]{:S(2)}) collective-permute-start(bf16[96,1280]{1,0:T(8,128)(2,1)S(1)} %select_convert_fusion.2), channel_id=1, source_target_pairs={{0,32},{32,0},{1,33},{33,1},{2,34},{34,2},{3,35},{35,3},{4,36},{36... | collective-permute-start | bytes 737288 | tf_op jit(solution)/shard_map/ppermute | solution.py:411
  136.5 6.5 %collective-permute-start.12 = (bf16[96,1280]{1,0:T(8,128)(2,1)S(1)}, bf16[96,1280]{1,0:T(8,128)(2,1)S(1)}, u32[]{:S(2)}, u32[]{:S(2)}) collective-permute-start(bf16[96,1280]{1,0:T(8,128)(2,1)S(1)} %select_convert_fusion.1), channel_id=1, source_target_pairs={{0,32},{32,0},{1,33},{33,1},{2,34},{34,2},{3,35},{35,3},{4,36},{36... | collective-permute-start | bytes 737288 | tf_op jit(solution)/shard_map/ppermute | solution.py:411
  140.1 3.7 %collective-permute-start.15 = (bf16[96,1280]{1,0:T(8,128)(2,1)S(1)}, bf16[96,1280]{1,0:T(8,128)(2,1)S(1)}, u32[]{:S(2)}, u32[]{:S(2)}) collective-permute-start(bf16[96,1280]{1,0:T(8,128)(2,1)S(1)} %select_convert_fusion), channel_id=1, source_target_pairs={{0,32},{32,0},{1,33},{33,1},{2,34},{34,2},{3,35},{35,3},{4,36},{36... | collective-permute-start | bytes 737288 | tf_op jit(solution)/shard_map/ppermute | solution.py:411

commit v8 on v7

--- a/solution.py
+++ b/solution.py
@@ -263,7 +263,7 @@
     return lax.ppermute(x, ("xl", "xh"), [(index(i), index(i + step)) for i in range(4)])
 
 
-def project_kernel(parts, rows_ref, w_ref, *refs):
+def project_kernel(parts, heads_ref, shared_ref, w_ref, *refs):
     chunks = sorted({chunk for chunk, _, _ in parts})
     outs, bufs, sem = refs[: len(parts)], refs[len(parts) : -1], refs[-1]
     copies = []
@@ -282,7 +282,8 @@
         for (which, lo, count), out in zip(parts, outs):
             if which != chunk:
                 continue
-            rows = rows_ref[pl.ds(lo, count), :]
+            rows = [heads_ref[j, pl.ds(lo, count), :] for j in range(4)]
+            rows = jnp.concatenate(rows + [shared_ref[0, pl.ds(lo, count), :]], axis=1)
             for at in range(0, WIDTHS[chunk], 256):
                 columns = pl.ds(at, min(256, WIDTHS[chunk] - at))
                 product = jnp.dot(rows, buf[:, columns], preferred_element_type=jnp.float32)
@@ -297,7 +298,7 @@
             jax.ShapeDtypeStruct((count, WIDTHS[chunk]), jnp.float32 if lo == 0 else jnp.bfloat16)
             for chunk, lo, count in parts
         ),
-        in_specs=[VMEM, HBM],
+        in_specs=[VMEM, VMEM, HBM],
         out_specs=(VMEM,) * len(parts),
         scratch_shapes=[
             *[pltpu.VMEM((w.shape[0], WIDTHS[chunk]), w.dtype) for chunk in chunks],
@@ -309,7 +310,7 @@
             bytes_accessed=4_000_000,
             transcendentals=0,
         ),
-    )(rows, w)
+    )(*rows, w)
 
 
 def project(rows, w):
@@ -399,9 +400,8 @@
     levels = jnp.where(xl == 0, levels, jnp.roll(levels, 2 * ROWS, axis=2))
     heads = merge(out[:, :SUPER].reshape(4, 2, SUPER, HEAD), levels[0].reshape(4, 2, SUPER))
     shared = merge(out[None, :, SUPER : 2 * SUPER], levels[1][None])
-    attended = jnp.concatenate([heads, shared], axis=0).transpose(1, 0, 2).reshape(SUPER, 5 * HEAD)
-
-    lows, highs, owns = project(attended, w_out)
+
+    lows, highs, owns = project((heads, shared), w_out)
     total = []
     for low, high, own in zip(lows, highs, owns):
         first = own[:ROWS] + around(low, -1).astype(jnp.float32)

time: 146 us -> 146 us (level)
  waiting for transfers between devices: 40 us -> 38.3 us
  Pallas kernels: 29.3 us -> 31 us
    ppermute x2, waiting for transfers between devices: 3.24 us -> 1.54 us  [ring_down(): return lax.ppermute(x, 'y', [(i, (i - 1) % 4) for i in range(4)])]
    pallas_call x2, Pallas kernels: 12 us -> 13.7 us  [attend(): pl.pallas_call(functools.partial(stage_kernel, last, pieces), out_shape=o...]
  transfers between devices with their start and end apart: 18 -> 18, of which waited for: 6 -> 6; matrix products, arithmetic and copies ran while one was open for 2% -> 2% of each run, Pallas kernels for 13% -> 14%
where the time goes in v8:
time: 146 us
  starting transfers between devices  41.5 us (28%)
  waiting for transfers between devices  38.3 us (26%)
  Pallas kernels  31 us (21%)
  blocking collectives  29.2 us (20%)
  other arithmetic  3.03 us (2%)
  local copies, waits for them, and re-layouts  2.4 us (2%)
    all_to_all x1, blocking collectives, per_device(): out = lax.all_to_all(out, ('xh', 'zh', 'zl'), 0, 0, tiled=True)  29.2 us
    all_to_all x1, waiting for transfers between devices, per_device(): q = lax.all_to_all(pack_q(queries), SPREAD, 0, 0, tiled=True)  17.1 us
    all_to_all x1, waiting for transfers between devices, per_device(): lax.all_to_all(sent, SPREAD, 0, 0, tiled=True)  14.4 us
    pallas_call x2, Pallas kernels, attend(): pl.pallas_call(functools.partial(stage_kernel, last, pieces), out_shape=o...  13.7 us
    ppermute x4, starting transfers between devices, per_device(): lax.ppermute(give, 'c', [(0, 1), (1, 0)])  12 us
    pallas_call x3, Pallas kernels, project_parts(): pl.pallas_call(functools.partial(project_kernel, parts), out_shape=tuple(...  10.4 us
    ppermute x8, starting transfers between devices, around(): lax.ppermute(x, ('xl', 'xh'), [(index(i), index(i + step)) for i in range...  9.77 us
    all_to_all x1, starting transfers between devices, per_device(): lax.all_to_all(sent, SPREAD, 0, 0, tiled=True)  9.43 us
  transfers between devices with their start and end apart: 18, of which 6 were waited for; matrix products, arithmetic and copies ran while one was open for 2% of the time, Pallas kernels for 14%

profile of v8, /device:TPU:1, one launch (start us, length us, event | category | flops | bytes accessed | tf_op | source)
XLA Modules:
  0.0 145.8 jit_solution(10779422596613005494)
XLA Ops:
  0.0 2.3 %shard_map.64 = bf16[32,128,128]{2,1,0:T(8,128)(2,1)} custom-call(s32[1]{0:T(128)} %bitcast.5.chunk_ref, bf16[96,2560]{1,0:T(8,128)(2,1)} %k_ref.1, bf16[96,2560]{1,0:T(8,128)(2,1)} %v_ref.1), custom_call_target="tpu_custom_call" | custom-call | flops 1000000 | bytes 2000000 | tf_op jit(solution)/shard_map/pallas_call | solution.py:342
  2.3 9.4 %all-to-all-start = ((bf16[32,128,128]{2,1,0:T(8,128)(2,1)}), bf16[32,128,128]{2,1,0:T(8,128)(2,1)S(1)}, u32[]{:S(2)}, u32[]{:S(2)}) async-start(bf16[32,128,128]{2,1,0:T(8,128)(2,1)} %shard_map.64), calls=%async_computation | async-start | bytes 2097152 | tf_op jit(solution)/shard_map/all_to_all | solution.py:381
  11.8 2.4 %shard_map.65 = bf16[32,2,96,128]{3,2,1,0:T(8,128)(2,1)} custom-call(bf16[96,2560]{1,0:T(8,128)(2,1)} %q_ref.1), custom_call_target="tpu_custom_call" | custom-call | flops 1000000 | bytes 2000000 | tf_op jit(solution)/shard_map/pallas_call | solution.py:361
  14.2 14.4 %all-to-all-done = bf16[32,128,128]{2,1,0:T(8,128)(2,1)S(1)} async-done(((bf16[32,128,128]{2,1,0:T(8,128)(2,1)}), bf16[32,128,128]{2,1,0:T(8,128)(2,1)S(1)}, u32[]{:S(2)}, u32[]{:S(2)}) %all-to-all-start) | async-done | bytes 1048608 | tf_op jit(solution)/shard_map/all_to_all | solution.py:381
  28.5 4.7 %all-to-all-start.1 = ((bf16[32,2,96,128]{3,2,1,0:T(8,128)(2,1)}), bf16[32,2,96,128]{3,2,1,0:T(8,128)(2,1)}, u32[]{:S(2)}, u32[]{:S(2)}) async-start(bf16[32,2,96,128]{3,2,1,0:T(8,128)(2,1)} %shard_map.65), calls=%async_computation.1 | async-start | bytes 3145728 | tf_op jit(solution)/shard_map/all_to_all | solution.py:382
  33.2 1.4 collective-permute-start
  34.6 1.5 %collective-permute-start.1 = (bf16[8,4,128,128]{3,2,1,0:T(8,128)(2,1)S(1)}, bf16[8,4,128,128]{3,2,1,0:T(8,128)(2,1)S(1)}, u32[]{:S(2)}, u32[]{:S(2)}) collective-permute-start(bf16[8,4,128,128]{3,2,1,0:T(8,128)(2,1)S(1)} %bitcast.39), channel_id=1, source_target_pairs={{0,3},{1,0},{2,1},{3,2},{4,7},{5,4},{6,5},{7,6},{8,11},{9,8},{10,9... | collective-permute-start | bytes 3145736 | tf_op jit(solution)/shard_map/ppermute | solution.py:46
  36.1 0.6 stack.23.where_ref.refs_0_
  36.7 2.2 %shard_map.66 = (s32[64,96]{1,0:T(8,128)}, s32[4,96]{1,0:T(4,128)}) custom-call(s32[5]{0:T(128)} %stack.23.where_ref.refs_0_, s32[20,96]{1,0:T(8,128)} %counts_ref.1, s32[20,16,96]{2,1,0:T(8,128)} %bitcast.42), custom_call_target="tpu_custom_call" | custom-call | flops 1000000 | bytes 100000 | tf_op jit(solution)/shard_map/pallas_call | solution.py:89
  38.9 17.1 %all-to-all-done.1 = bf16[32,2,96,128]{3,2,1,0:T(8,128)(2,1)} async-done(((bf16[32,2,96,128]{3,2,1,0:T(8,128)(2,1)}), bf16[32,2,96,128]{3,2,1,0:T(8,128)(2,1)}, u32[]{:S(2)}, u32[]{:S(2)}) %all-to-all-start.1) | async-done | bytes 1572896 | tf_op jit(solution)/shard_map/all_to_all | solution.py:382
  56.0 1.6 %copy.12 = bf16[8,4,2,96,128]{4,3,1,0,2:T(8,128)(2,1)S(1)} copy(bf16[8,4,2,96,128]{4,3,2,1,0:T(8,128)(2,1)} %bitcast.7) | data formatting | bytes 3145728 | tf_op jit(solution)/shard_map/reshape | solution.py:383
  57.6 0.0 copy-start
  57.6 0.0 copy-start.1
  57.6 0.0 copy-start.2
  57.6 1.3 collective-permute-done.refs_5_
  58.9 0.0 collective-permute-done.1.refs_6_
  59.0 2.6 %collective-permute-start.2 = (bf16[8,4,64,128]{3,2,1,0:T(8,128)(2,1)S(1)}, bf16[8,4,64,128]{3,2,1,0:T(8,128)(2,1)S(1)}, u32[]{:S(2)}, u32[]{:S(2)}) collective-permute-start(bf16[8,4,64,128]{3,2,1,0:T(8,128)(2,1)S(1)} %slice.56), channel_id=1, source_target_pairs={{0,3},{1,0},{2,1},{3,2},{4,7},{5,4},{6,5},{7,6},{8,11},{9,8},{10,9... | collective-permute-start | bytes 1572872 | tf_op jit(solution)/shard_map/ppermute | solution.py:46
  61.6 0.1 collective-permute-start.3
  61.7 8.1 %shard_map.67 = (f32[48,128,128]{2,1,0:T(8,128)S(1)}, f32[48,128,128]{2,1,0:T(8,128)S(1)}, f32[48,128,128]{2,1,0:T(8,128)S(1)}) custom-call(s32[5]{0:T(128)S(1)} %copy-done, s32[64,96]{1,0:T(8,128)S(1)} %copy-done.1, s32[4,96]{1,0:T(4,128)S(1)} %copy-done.2, bf16[48,128,128]{2,1,0:T(8,128)(2,1)S(1)} %bitcast.36, bf16[8,4,128,128]{3,2,1,0:T(8,128)(2,1)S(1)} %bitcast.40, ...), custom_call_target="tpu_custom_call" | custom-call | flops 15000000512 | bytes 6000000 | tf_op jit(solution)/shard_map/pallas_call | solution.py:248
  69.8 1.5 %collective-permute-done.2.refs_7_ = bf16[8,4,64,128]{3,2,1,0:T(8,128)(2,1)S(1)} collective-permute-done((bf16[8,4,64,128]{3,2,1,0:T(8,128)(2,1)S(1)}, bf16[8,4,64,128]{3,2,1,0:T(8,128)(2,1)S(1)}, u32[]{:S(2)}, u32[]{:S(2)}) %collective-permute-start.2) | collective-permute-done | bytes 524320 | tf_op jit(solution)/shard_map/ppermute | solution.py:46
  71.4 3.2 %collective-permute-done.3.refs_8_ = bf16[8,4,64,128]{3,2,1,0:T(8,128)(2,1)S(1)} collective-permute-done((bf16[8,4,64,128]{3,2,1,0:T(8,128)(2,1)S(1)}, bf16[8,4,64,128]{3,2,1,0:T(8,128)(2,1)S(1)}, u32[]{:S(2)}, u32[]{:S(2)}) %collective-permute-start.3) | collective-permute-done | bytes 524320 | tf_op jit(solution)/shard_map/ppermute | solution.py:42
  74.6 5.6 %shard_map.68 = bf16[8,816,128]{2,1,0:T(8,128)(2,1)S(1)} custom-call(s32[5]{0:T(128)S(1)} %copy-done, s32[64,96]{1,0:T(8,128)S(1)} %copy-done.1, s32[4,96]{1,0:T(4,128)S(1)} %copy-done.2, bf16[48,128,128]{2,1,0:T(8,128)(2,1)S(1)} %bitcast.37, f32[48,128,128]{2,1,0:T(8,128)S(1)} %get-tuple-element.38.refs_4_, f32[48,128,128]{2,1,0:T(8,128)S(1)} %get-tuple-element.39.refs_5_, ...), custom_call_target="tpu_custom_call" | custom-call | flops 5000000000 | bytes 2000000 | tf_op jit(solution)/shard_map/pallas_call | solution.py:248
  80.3 29.2 %all_to_all.15 = bf16[8,816,128]{2,1,0:T(8,128)(2,1)S(1)} all-to-all(bf16[8,816,128]{2,1,0:T(8,128)(2,1)S(1)} %shard_map.68), channel_id=1, replica_groups=mesh['xl'=2,'c'=2,'xh'=2,'zh'=2,'zl'=2,'y'=4] {'xh','zh','zl'}, dimensions={0} | all-to-all | bytes 3342336 | tf_op jit(solution)/shard_map/all_to_all | solution.py:394
  109.5 0.1 fusion.9
  109.6 0.1 maximum_select_fusion
  109.8 0.5 multiply_reduce_fusion
  110.3 0.5 fusion.1.heads_ref
  110.8 2.4 %shard_map.69 = (bf16[96,1280]{1,0:T(8,128)(2,1)S(1)}, bf16[96,1280]{1,0:T(8,128)(2,1)S(1)}, f32[192,1280]{1,0:T(8,128)S(1)}) custom-call(bf16[4,384,128]{2,1,0:T(8,128)(2,1)S(1)} %fusion.1.heads_ref, bf16[1,384,128]{2,1,0:T(8,128)(2,1)S(1)} %bitcast.33, bf16[640,5120]{1,0:T(8,128)(2,1)} %w_ref.2), custom_call_target="tpu_custom_call" | custom-call | flops 629145600 | bytes 4000000 | tf_op jit(solution)/shard_map/pallas_call | solution.py:295
  113.2 1.5 %collective-permute-start.4 = (bf16[96,1280]{1,0:T(8,128)(2,1)S(1)}, bf16[96,1280]{1,0:T(8,128)(2,1)S(1)}, u32[]{:S(2)}, u32[]{:S(2)}) collective-permute-start(bf16[96,1280]{1,0:T(8,128)(2,1)S(1)} %get-tuple-element.46), channel_id=1, source_target_pairs={{0,80},{64,0},{16,64},{80,16},{1,81},{65,1},{17,65},{81,17},{2,82}... | collective-permute-start | bytes 737288 | tf_op jit(solution)/shard_map/ppermute | solution.py:263
  114.8 0.5 collective-permute-start.5
  115.3 3.6 %shard_map.71 = (bf16[96,1280]{1,0:T(8,128)(2,1)S(1)}, bf16[96,1280]{1,0:T(8,128)(2,1)S(1)}, bf16[96,1280]{1,0:T(8,128)(2,1)S(1)}, bf16[96,1280]{1,0:T(8,128)(2,...) custom-call(bf16[4,384,128]{2,1,0:T(8,128)(2,1)S(1)} %fusion.1.heads_ref, ...), custom_call_target="tpu_custom_call" | custom-call | flops 943718400 | bytes 4000000 | tf_op jit(solution)/shard_map/pallas_call | solution.py:295
  118.9 2.2 %collective-permute-start.7 = (bf16[96,1280]{1,0:T(8,128)(2,1)S(1)}, bf16[96,1280]{1,0:T(8,128)(2,1)S(1)}, u32[]{:S(2)}, u32[]{:S(2)}) collective-permute-start(bf16[96,1280]{1,0:T(8,128)(2,1)S(1)} %get-tuple-element.49), channel_id=1, source_target_pairs={{0,80},{64,0},{16,64},{80,16},{1,81},{65,1},{17,65},{81,17},{2,82}... | collective-permute-start | bytes 737288 | tf_op jit(solution)/shard_map/ppermute | solution.py:263
  121.1 0.0 collective-permute-start.8
  121.1 2.7 %collective-permute-start.10 = (bf16[96,1280]{1,0:T(8,128)(2,1)S(1)}, bf16[96,1280]{1,0:T(8,128)(2,1)S(1)}, u32[]{:S(2)}, u32[]{:S(2)}) collective-permute-start(bf16[96,1280]{1,0:T(8,128)(2,1)S(1)} %get-tuple-element.52), channel_id=1, source_target_pairs={{0,80},{64,0},{16,64},{80,16},{1,81},{65,1},{17,65},{81,17},{2,82}... | collective-permute-start | bytes 737288 | tf_op jit(solution)/shard_map/ppermute | solution.py:263
  123.8 4.4 %shard_map.70 = (f32[192,1280]{1,0:T(8,128)S(1)}, f32[192,1280]{1,0:T(8,128)}, f32[192,1280]{1,0:T(8,128)}) custom-call(bf16[4,384,128]{2,1,0:T(8,128)(2,1)S(1)} %fusion.1.heads_ref, bf16[1,384,128]{2,1,0:T(8,128)(2,1)S(1)} %bitcast.35, bf16[640,5120]{1,0:T(8,128)(2,1)} %w_ref.2), custom_call_target="tpu_custom_call" | custom-call | flops 943718400 | bytes 4000000 | tf_op jit(solution)/shard_map/pallas_call | solution.py:295
  128.2 0.0 collective-permute-done.4
  128.2 0.1 collective-permute-start.11
  128.3 0.0 collective-permute-done.5
  128.3 2.7 %collective-permute-start.13 = (bf16[96,1280]{1,0:T(8,128)(2,1)S(1)}, bf16[96,1280]{1,0:T(8,128)(2,1)S(1)}, u32[]{:S(2)}, u32[]{:S(2)}) collective-permute-start(bf16[96,1280]{1,0:T(8,128)(2,1)S(1)} %get-tuple-element.55), channel_id=1, source_target_pairs={{0,80},{64,0},{16,64},{80,16},{1,81},{65,1},{17,65},{81,17},{2,82}... | collective-permute-start | bytes 737288 | tf_op jit(solution)/shard_map/ppermute | solution.py:263
  130.9 0.1 select_convert_fusion.3
  131.0 0.0 collective-permute-done.7
  131.0 0.1 collective-permute-start.14
  131.1 0.0 collective-permute-done.8
  131.1 4.7 %collective-permute-start.6 = (bf16[96,1280]{1,0:T(8,128)(2,1)S(1)}, bf16[96,1280]{1,0:T(8,128)(2,1)S(1)}, u32[]{:S(2)}, u32[]{:S(2)}) collective-permute-start(bf16[96,1280]{1,0:T(8,128)(2,1)S(1)} %select_convert_fusion.3), channel_id=1, source_target_pairs={{0,32},{32,0},{1,33},{33,1},{2,34},{34,2},{3,35},{35,3},{4,36},{36... | collective-permute-start | bytes 737288 | tf_op jit(solution)/shard_map/ppermute | solution.py:411
  135.8 0.1 select_convert_fusion.2
  135.9 0.0 collective-permute-done.10
  135.9 0.1 collective-permute-start.9
  136.0 0.0 collective-permute-done.11
  136.0 0.1 select_convert_fusion.1
  136.1 4.7 %collective-permute-start.12 = (bf16[96,1280]{1,0:T(8,128)(2,1)S(1)}, bf16[96,1280]{1,0:T(8,128)(2,1)S(1)}, u32[]{:S(2)}, u32[]{:S(2)}) collective-permute-start(bf16[96,1280]{1,0:T(8,128)(2,1)S(1)} %select_convert_fusion.1), channel_id=1, source_target_pairs={{0,32},{32,0},{1,33},{33,1},{2,34},{34,2},{3,35},{35,3},{4,36},{36... | collective-permute-start | bytes 737288 | tf_op jit(solution)/shard_map/ppermute | solution.py:411
  140.9 0.0 collective-permute-done.13
  140.9 0.0 collective-permute-done.14
  140.9 0.0 copy-done.3
  140.9 0.1 select_convert_fusion
  141.0 2.5 %collective-permute-start.15 = (bf16[96,1280]{1,0:T(8,128)(2,1)S(1)}, bf16[96,1280]{1,0:T(8,128)(2,1)S(1)}, u32[]{:S(2)}, u32[]{:S(2)}) collective-permute-start(bf16[96,1280]{1,0:T(8,128)(2,1)S(1)} %select_convert_fusion), channel_id=1, source_target_pairs={{0,32},{32,0},{1,33},{33,1},{2,34},{34,2},{3,35},{35,3},{4,36},{36... | collective-permute-start | bytes 737288 | tf_op jit(solution)/shard_map/ppermute | solution.py:411
  143.5 0.0 collective-permute-done.6
  143.5 0.1 add_convert_fusion.3
  143.6 0.0 collective-permute-done.9
  143.6 0.1 add_convert_fusion.2
  143.8 0.0 collective-permute-done.12
  143.8 0.1 add_convert_fusion.1
  143.9 0.7 collective-permute-done.15
  144.6 0.1 add_convert_fusion
  144.8 1.0 pad_maximum_fusion
  (18 shorter events, 0.2 us)
Async XLA Ops:
  2.3 26.2 %all-to-all-start = ((bf16[32,128,128]{2,1,0:T(8,128)(2,1)}), bf16[32,128,128]{2,1,0:T(8,128)(2,1)S(1)}, u32[]{:S(2)}, u32[]{:S(2)}) async-start(bf16[32,128,128]{2,1,0:T(8,128)(2,1)} %shard_map.64), calls=%async_computation | async-start | bytes 2097152 | tf_op jit(solution)/shard_map/all_to_all | solution.py:381
  28.5 27.5 %all-to-all-start.1 = ((bf16[32,2,96,128]{3,2,1,0:T(8,128)(2,1)}), bf16[32,2,96,128]{3,2,1,0:T(8,128)(2,1)}, u32[]{:S(2)}, u32[]{:S(2)}) async-start(bf16[32,2,96,128]{3,2,1,0:T(8,128)(2,1)} %shard_map.65), calls=%async_computation.1 | async-start | bytes 3145728 | tf_op jit(solution)/shard_map/all_to_all | solution.py:382
  33.2 25.7 %collective-permute-start = (bf16[8,4,128,128]{3,2,1,0:T(8,128)(2,1)S(1)}, bf16[8,4,128,128]{3,2,1,0:T(8,128)(2,1)S(1)}, u32[]{:S(2)}, u32[]{:S(2)}) collective-permute-start(bf16[8,4,128,128]{3,2,1,0:T(8,128)(2,1)S(1)} %bitcast.38), channel_id=1, source_target_pairs={{0,1},{1,2},{2,3},{3,0},{4,5},{5,6},{6,7},{7,4},{8,9},{9,10},{10,1... | collective-permute-start | bytes 3145736 | tf_op jit(solution)/shard_map/ppermute | solution.py:42
  34.6 24.4 %collective-permute-start.1 = (bf16[8,4,128,128]{3,2,1,0:T(8,128)(2,1)S(1)}, bf16[8,4,128,128]{3,2,1,0:T(8,128)(2,1)S(1)}, u32[]{:S(2)}, u32[]{:S(2)}) collective-permute-start(bf16[8,4,128,128]{3,2,1,0:T(8,128)(2,1)S(1)} %bitcast.39), channel_id=1, source_target_pairs={{0,3},{1,0},{2,1},{3,2},{4,7},{5,4},{6,5},{7,6},{8,11},{9,8},{10,9... | collective-permute-start | bytes 3145736 | tf_op jit(solution)/shard_map/ppermute | solution.py:46
  57.6 4.1 %copy-start = (s32[5]{0:T(128)S(1)}, s32[5]{0:T(128)}, u32[]{:S(2)}) copy-start(s32[5]{0:T(128)} %stack.23.where_ref.refs_0_) | copy-start | bytes 64
  57.6 4.1 %copy-start.1 = (s32[64,96]{1,0:T(8,128)S(1)}, s32[64,96]{1,0:T(8,128)}, u32[]{:S(2)}) copy-start(s32[64,96]{1,0:T(8,128)} %get-tuple-element.33.refs_1_) | copy-start | bytes 73732
  57.6 4.1 %copy-start.2 = (s32[4,96]{1,0:T(4,128)S(1)}, s32[4,96]{1,0:T(4,128)}, u32[]{:S(2)}) copy-start(s32[4,96]{1,0:T(4,128)} %get-tuple-element.34.refs_2_) | copy-start | bytes 4612
  59.0 12.4 %collective-permute-start.2 = (bf16[8,4,64,128]{3,2,1,0:T(8,128)(2,1)S(1)}, bf16[8,4,64,128]{3,2,1,0:T(8,128)(2,1)S(1)}, u32[]{:S(2)}, u32[]{:S(2)}) collective-permute-start(bf16[8,4,64,128]{3,2,1,0:T(8,128)(2,1)S(1)} %slice.56), channel_id=1, source_target_pairs={{0,3},{1,0},{2,1},{3,2},{4,7},{5,4},{6,5},{7,6},{8,11},{9,8},{10,9... | collective-permute-start | bytes 1572872 | tf_op jit(solution)/shard_map/ppermute | solution.py:46
  61.6 13.0 %collective-permute-start.3 = (bf16[8,4,64,128]{3,2,1,0:T(8,128)(2,1)S(1)}, bf16[8,4,64,128]{3,2,1,0:T(8,128)(2,1)S(1)}, u32[]{:S(2)}, u32[]{:S(2)}) collective-permute-start(bf16[8,4,64,128]{3,2,1,0:T(8,128)(2,1)S(1)} %slice.57), channel_id=1, source_target_pairs={{0,1},{1,2},{2,3},{3,0},{4,5},{5,6},{6,7},{7,4},{8,9},{9,10},{10,1... | collective-permute-start | bytes 1572872 | tf_op jit(solution)/shard_map/ppermute | solution.py:42
  113.2 14.9 %collective-permute-start.4 = (bf16[96,1280]{1,0:T(8,128)(2,1)S(1)}, bf16[96,1280]{1,0:T(8,128)(2,1)S(1)}, u32[]{:S(2)}, u32[]{:S(2)}) collective-permute-start(bf16[96,1280]{1,0:T(8,128)(2,1)S(1)} %get-tuple-element.46), channel_id=1, source_target_pairs={{0,80},{64,0},{16,64},{80,16},{1,81},{65,1},{17,65},{81,17},{2,82}... | collective-permute-start | bytes 737288 | tf_op jit(solution)/shard_map/ppermute | solution.py:263
  114.8 13.5 %collective-permute-start.5 = (bf16[96,1280]{1,0:T(8,128)(2,1)S(1)}, bf16[96,1280]{1,0:T(8,128)(2,1)S(1)}, u32[]{:S(2)}, u32[]{:S(2)}) collective-permute-start(bf16[96,1280]{1,0:T(8,128)(2,1)S(1)} %get-tuple-element.47), channel_id=1, source_target_pairs={{0,64},{64,16},{16,80},{80,0},{1,65},{65,17},{17,81},{81,1},{2,66}... | collective-permute-start | bytes 737288 | tf_op jit(solution)/shard_map/ppermute | solution.py:263
  118.9 12.2 %collective-permute-start.7 = (bf16[96,1280]{1,0:T(8,128)(2,1)S(1)}, bf16[96,1280]{1,0:T(8,128)(2,1)S(1)}, u32[]{:S(2)}, u32[]{:S(2)}) collective-permute-start(bf16[96,1280]{1,0:T(8,128)(2,1)S(1)} %get-tuple-element.49), channel_id=1, source_target_pairs={{0,80},{64,0},{16,64},{80,16},{1,81},{65,1},{17,65},{81,17},{2,82}... | collective-permute-start | bytes 737288 | tf_op jit(solution)/shard_map/ppermute | solution.py:263
  121.1 10.0 %collective-permute-start.8 = (bf16[96,1280]{1,0:T(8,128)(2,1)S(1)}, bf16[96,1280]{1,0:T(8,128)(2,1)S(1)}, u32[]{:S(2)}, u32[]{:S(2)}) collective-permute-start(bf16[96,1280]{1,0:T(8,128)(2,1)S(1)} %get-tuple-element.50), channel_id=1, source_target_pairs={{0,64},{64,16},{16,80},{80,0},{1,65},{65,17},{17,81},{81,1},{2,66}... | collective-permute-start | bytes 737288 | tf_op jit(solution)/shard_map/ppermute | solution.py:263
  121.1 14.8 %collective-permute-start.10 = (bf16[96,1280]{1,0:T(8,128)(2,1)S(1)}, bf16[96,1280]{1,0:T(8,128)(2,1)S(1)}, u32[]{:S(2)}, u32[]{:S(2)}) collective-permute-start(bf16[96,1280]{1,0:T(8,128)(2,1)S(1)} %get-tuple-element.52), channel_id=1, source_target_pairs={{0,80},{64,0},{16,64},{80,16},{1,81},{65,1},{17,65},{81,17},{2,82}... | collective-permute-start | bytes 737288 | tf_op jit(solution)/shard_map/ppermute | solution.py:263
  128.2 7.9 %collective-permute-start.11 = (bf16[96,1280]{1,0:T(8,128)(2,1)S(1)}, bf16[96,1280]{1,0:T(8,128)(2,1)S(1)}, u32[]{:S(2)}, u32[]{:S(2)}) collective-permute-start(bf16[96,1280]{1,0:T(8,128)(2,1)S(1)} %get-tuple-element.53), channel_id=1, source_target_pairs={{0,64},{64,16},{16,80},{80,0},{1,65},{65,17},{17,81},{81,1},{2,66}... | collective-permute-start | bytes 737288 | tf_op jit(solution)/shard_map/ppermute | solution.py:263
  128.3 12.6 %collective-permute-start.13 = (bf16[96,1280]{1,0:T(8,128)(2,1)S(1)}, bf16[96,1280]{1,0:T(8,128)(2,1)S(1)}, u32[]{:S(2)}, u32[]{:S(2)}) collective-permute-start(bf16[96,1280]{1,0:T(8,128)(2,1)S(1)} %get-tuple-element.55), channel_id=1, source_target_pairs={{0,80},{64,0},{16,64},{80,16},{1,81},{65,1},{17,65},{81,17},{2,82}... | collective-permute-start | bytes 737288 | tf_op jit(solution)/shard_map/ppermute | solution.py:263
  130.9 5.1 %copy-start.4 = (f32[192,1280]{1,0:T(8,128)S(1)}, f32[192,1280]{1,0:T(8,128)}, u32[]{:S(2)}) copy-start(f32[192,1280]{1,0:T(8,128)} %get-tuple-element.51) | copy-start | bytes 2949124
  131.0 9.8 %collective-permute-start.14 = (bf16[96,1280]{1,0:T(8,128)(2,1)S(1)}, bf16[96,1280]{1,0:T(8,128)(2,1)S(1)}, u32[]{:S(2)}, u32[]{:S(2)}) collective-permute-start(bf16[96,1280]{1,0:T(8,128)(2,1)S(1)} %get-tuple-element.56), channel_id=1, source_target_pairs={{0,64},{64,16},{16,80},{80,0},{1,65},{65,17},{17,81},{81,1},{2,66}... | collective-permute-start | bytes 737288 | tf_op jit(solution)/shard_map/ppermute | solution.py:263
  131.1 12.4 %collective-permute-start.6 = (bf16[96,1280]{1,0:T(8,128)(2,1)S(1)}, bf16[96,1280]{1,0:T(8,128)(2,1)S(1)}, u32[]{:S(2)}, u32[]{:S(2)}) collective-permute-start(bf16[96,1280]{1,0:T(8,128)(2,1)S(1)} %select_convert_fusion.3), channel_id=1, source_target_pairs={{0,32},{32,0},{1,33},{33,1},{2,34},{34,2},{3,35},{35,3},{4,36},{36... | collective-permute-start | bytes 737288 | tf_op jit(solution)/shard_map/ppermute | solution.py:411
  135.8 5.1 %copy-start.3 = (f32[192,1280]{1,0:T(8,128)S(1)}, f32[192,1280]{1,0:T(8,128)}, u32[]{:S(2)}) copy-start(f32[192,1280]{1,0:T(8,128)} %get-tuple-element.54) | copy-start | bytes 2949124
  135.9 7.7 %collective-permute-start.9 = (bf16[96,1280]{1,0:T(8,128)(2,1)S(1)}, bf16[96,1280]{1,0:T(8,128)(2,1)S(1)}, u32[]{:S(2)}, u32[]{:S(2)}) collective-permute-start(bf16[96,1280]{1,0:T(8,128)(2,1)S(1)} %select_convert_fusion.2), channel_id=1, source_target_pairs={{0,32},{32,0},{1,33},{33,1},{2,34},{34,2},{3,35},{35,3},{4,36},{36... | collective-permute-start | bytes 737288 | tf_op jit(solution)/shard_map/ppermute | solution.py:411
  136.1 7.6 %collective-permute-start.12 = (bf16[96,1280]{1,0:T(8,128)(2,1)S(1)}, bf16[96,1280]{1,0:T(8,128)(2,1)S(1)}, u32[]{:S(2)}, u32[]{:S(2)}) collective-permute-start(bf16[96,1280]{1,0:T(8,128)(2,1)S(1)} %select_convert_fusion.1), channel_id=1, source_target_pairs={{0,32},{32,0},{1,33},{33,1},{2,34},{34,2},{3,35},{35,3},{4,36},{36... | collective-permute-start | bytes 737288 | tf_op jit(solution)/shard_map/ppermute | solution.py:411
  141.0 3.7 %collective-permute-start.15 = (bf16[96,1280]{1,0:T(8,128)(2,1)S(1)}, bf16[96,1280]{1,0:T(8,128)(2,1)S(1)}, u32[]{:S(2)}, u32[]{:S(2)}) collective-permute-start(bf16[96,1280]{1,0:T(8,128)(2,1)S(1)} %select_convert_fusion), channel_id=1, source_target_pairs={{0,32},{32,0},{1,33},{33,1},{2,34},{34,2},{3,35},{35,3},{4,36},{36... | collective-permute-start | bytes 737288 | tf_op jit(solution)/shard_map/ppermute | solution.py:411
